TPU v7x, 128 devices: a whole 4x4x4 slice. The times are simulated.
128 devices in a mesh: seq: 8 (over z, core), vocab: 16 (over y, x).
Axes of the slice: x: 4, y: 4, z: 4, core: 2. Of those that a mesh axis runs over, the one named last changes fastest.
Arguments:
- hidden: bfloat16 [512, 5376], P('seq', 'vocab'), may hold values from -48 to 48
- head_weight: bfloat16 [131072, 5376], P(('seq', 'vocab')), may hold values from -1 to 1
- teacher_logits: float32 [512, 256], P(('seq', 'vocab')), may hold values from -16 to 300
- teacher_ids: int32 [512, 256], P(('seq', 'vocab')), may hold values from 0 to 131071, as said below
Outputs:
- cross_entropy: float32 [512], P(('seq', 'vocab'))
- entropy: float32 [512], P(('seq', 'vocab'))
- grad_hidden: bfloat16 [512, 5376], P('seq', 'vocab')
- grad_weight: bfloat16 [131072, 5376], P(('seq', 'vocab'))
Inputs may be any that keep to these rules, and one draw needn't show every extreme that they name: `teacher_ids`: each row names 256 different ids, grouped by owner o = id // 1024 in ascending order of o. In every row one owner has exactly 6 ids, every other owner 1 or 2.
All inputs are finite; a program needn't handle non-finite values.
Results may differ from a plain program's by a relative error of at most 0.011.
Values may be sent and summed in bfloat16 or wider, within the bound.
No kernel may reach another device: no remote copies, remote signals or barrier semaphores. Data moves between devices by JAX's collectives and lax.ppermute only.
A program may use at most 128 MiB of HBM per device.

v0:
```python
import jax
import jax.numpy as jnp
from jax import lax
from jax.sharding import PartitionSpec as P

loss_scale = 64.0


def body(hidden, head_weight, teacher_logits, teacher_ids):
    seq_count = lax.axis_size("seq")
    vocab_count = lax.axis_size("vocab")
    owner_count = seq_count * vocab_count
    device_index = lax.axis_index(("seq", "vocab"))
    vocab_rows = head_weight.shape[0]
    tok_rows = hidden.shape[0]
    feat_part = hidden.shape[1]
    features = lax.all_gather(hidden, "vocab", axis=1, tiled=True)
    gathered = lax.all_gather(features, "seq", axis=0, tiled=True)
    token_total = gathered.shape[0]
    logits = lax.dot_general(
        gathered, head_weight, (((1,), (1,)), ((), ())), preferred_element_type=jnp.float32
    )
    teacher_prob = jax.nn.softmax(teacher_logits, axis=1)
    src_rows, teach_width = teacher_ids.shape
    capacity = 2 * (teach_width // owner_count) + 2
    owners_of = teacher_ids // vocab_rows
    owner_iota = jnp.arange(owner_count, dtype=jnp.int32)
    starts = jnp.sum((owners_of[:, None, :] < owner_iota[None, :, None]).astype(jnp.int32), axis=2)
    slot_pos = jnp.arange(teach_width, dtype=jnp.int32)[None, :] - jnp.take_along_axis(
        starts, owners_of, axis=1
    )
    row_ids = jnp.broadcast_to(jnp.arange(src_rows, dtype=jnp.int32)[:, None], teacher_ids.shape)
    send_prob = (
        jnp.zeros((owner_count, src_rows, capacity), jnp.float32)
        .at[owners_of, row_ids, slot_pos]
        .set(teacher_prob)
    )
    pad_ids = jnp.broadcast_to(
        (owner_iota * vocab_rows)[:, None, None], (owner_count, src_rows, capacity)
    )
    send_ids = pad_ids.at[owners_of, row_ids, slot_pos].set(teacher_ids)
    got_prob, got_ids = (
        lax.all_to_all(send_prob, ("seq", "vocab"), split_axis=0, concat_axis=0, tiled=True),
        lax.all_to_all(send_ids, ("seq", "vocab"), split_axis=0, concat_axis=0, tiled=True),
    )
    got_prob = got_prob.reshape(token_total, capacity)
    local_ids = got_ids.reshape(token_total, capacity) - device_index * vocab_rows
    columns = jnp.arange(vocab_rows, dtype=jnp.int32)[None, :]

    def place(slot_index, target_acc):
        wanted = lax.dynamic_slice_in_dim(local_ids, slot_index, 1, 1)
        weight_col = lax.dynamic_slice_in_dim(got_prob, slot_index, 1, 1)
        return target_acc + jnp.where(columns == wanted, weight_col, 0.0)

    target = lax.fori_loop(0, capacity, place, jnp.zeros((token_total, vocab_rows), jnp.float32))
    cross_part = jnp.sum(target * logits, axis=1)
    peak_val = lax.pmax(jnp.max(logits, axis=1), ("seq", "vocab"))
    expo = jnp.exp(logits - peak_val[:, None])
    total_sum, moment, cross_sum = lax.psum(
        (jnp.sum(expo, axis=1), jnp.sum(expo * logits, axis=1), cross_part), ("seq", "vocab")
    )
    student = expo / total_sum[:, None]
    log_total = peak_val + jnp.log(total_sum)
    cross_entropy = lax.dynamic_slice_in_dim(
        log_total - cross_sum, device_index * src_rows, src_rows, 0
    )
    entropy = lax.dynamic_slice_in_dim(
        log_total - moment / total_sum, device_index * src_rows, src_rows, 0
    )
    grad_logits = (loss_scale * (student - target)).astype(jnp.bfloat16)
    grad_weight = lax.dot_general(
        grad_logits, gathered, (((0,), (0,)), ((), ())), preferred_element_type=jnp.float32
    ).astype(jnp.bfloat16)
    full_term = jnp.dot(grad_logits, head_weight, preferred_element_type=jnp.float32)
    block_order = full_term.reshape(seq_count, tok_rows, vocab_count, feat_part)
    block_order = block_order.transpose(0, 2, 1, 3).reshape(owner_count * tok_rows, feat_part)
    grad_share = lax.psum_scatter(block_order, ("seq", "vocab"), scatter_dimension=0, tiled=True)
    return (cross_entropy, entropy, grad_share.astype(jnp.bfloat16), grad_weight)


def solution(mesh):
    placed = (
        P("seq", "vocab"),
        P(("seq", "vocab"), None),
        P(("seq", "vocab"), None),
        P(("seq", "vocab"), None),
    )
    return jax.shard_map(
        body,
        mesh=mesh,
        in_specs=placed,
        out_specs=(
            P(("seq", "vocab")),
            P(("seq", "vocab")),
            P("seq", "vocab"),
            P(("seq", "vocab"), None),
        ),
        check_vma=False,
    )
```

profile of v0, /device:TPU:0, one launch (start us, length us, event | category | flops | bytes accessed | tf_op | source)
XLA Modules:
  0.0 495.4 jit_solution(13134371476669482229)
XLA Ops:
  7.2 24.7 %all-gather = bf16[16,336,64]{1,2,0:T(8,128)(2,1)S(1)} all-gather(bf16[1,336,64]{1,2,0:T(8,128)(2,1)} %bitcast.60), channel_id=1, replica_groups=mesh['seq'=8,'vocab'=16] {'vocab'}, dimensions={0}, use_global_device_ids=true | all-gather | bytes 731136 | tf_op jit(solution)/shard_map/all_gather | solution.py:17
  31.9 0.5 copy.31
  32.4 1.7 reshape.87
  34.4 8.8 %gather_fusion = s32[1024]{0:T(1024)S(1)} fusion(s32[4,128]{1,0:T(4,128)S(1)} %convert_reduce_fusion, s32[1024]{0:T(1024)S(1)} %bitcast.50), kind=kCustom, calls=%fused_computation | custom fusion | bytes 16384 | tf_op jit(solution)/shard_map/jit(take_along_axis)/gather | solution.py:29
  43.5 4.3 scatter_fusion
  47.8 0.8 copy.32
  48.7 9.0 %all-to-all-start = ((s32[128,4,6]{2,1,0:T(4,128)}), s32[128,4,6]{2,1,0:T(4,128)S(1)}, u32[]{:S(2)}, u32[]{:S(2)}) async-start(s32[128,4,6]{2,1,0:T(4,128)} %copy.32), calls=%async_computation | async-start | bytes 524288 | tf_op jit(solution)/shard_map/all_to_all | solution.py:44
  58.1 4.3 scatter_custom_fusion.1
  62.4 0.9 copy.35
  63.2 5.3 %all-to-all-done = s32[128,4,6]{2,1,0:T(4,128)S(1)} async-done(((s32[128,4,6]{2,1,0:T(4,128)}), s32[128,4,6]{2,1,0:T(4,128)S(1)}, u32[]{:S(2)}, u32[]{:S(2)}) %all-to-all-start) | async-done | bytes 12320 | tf_op jit(solution)/shard_map/all_to_all | solution.py:44
  68.5 4.7 all-to-all-start.1
  73.6 0.2 sub.57
  73.8 10.3 %all-to-all-done.1 = f32[128,4,6]{2,1,0:T(4,128)S(1)} async-done(((f32[128,4,6]{2,1,0:T(4,128)}), f32[128,4,6]{2,1,0:T(4,128)S(1)}, u32[]{:S(2)}, u32[]{:S(2)}) %all-to-all-start.1) | async-done | bytes 12320 | tf_op jit(solution)/shard_map/all_to_all | solution.py:43
  84.2 3.4 while.14
  84.2 0.5 select_add_fusion.2
  84.8 0.5 select_add_fusion.2
  85.4 0.5 select_add_fusion.2
  85.9 0.5 select_add_fusion.2
  86.5 0.5 select_add_fusion.2
  87.1 0.5 select_add_fusion.2
  87.6 11.4 %fusion.11 = (f32[512]{0:T(512)S(1)}, f32[512,1024]{1,0:T(8,128)}) fusion(bf16[512,5376]{1,0:T(8,128)(2,1)} %all-gather.3.cloned.1.call-done, bf16[1024,5376]{1,0:T(8,128)(2,1)} %param.7), kind=kOutput, calls=%fused_computation.42 | convolution fusion | flops 5637668352 | bytes 18614272 | tf_op jit(solution)/shard_map/dot_general | solution.py:20
  99.0 62.7 %pmax.7 = f32[512]{0:T(512)S(1)} all-reduce(f32[512]{0:T(512)S(1)} %get-tuple-element.134), channel_id=1, replica_groups=mesh['seq'=8,'vocab'=16] {'seq','vocab'}, use_global_device_ids=true, to_apply=%region_1.0 | all-reduce | flops 512 | bytes 4096 | tf_op jit(solution)/shard_map/pmax | solution.py:57
  161.7 2.4 multiply_reduce_fusion
  164.1 62.7 %all-reduce = (f32[512]{0:T(512)S(1)}, f32[512]{0:T(512)S(1)}, f32[512]{0:T(512)S(1)}) all-reduce(f32[512]{0:T(512)S(1)} %get-tuple-element.118, f32[512]{0:T(512)S(1)} %get-tuple-element.117, f32[512]{0:T(512)S(1)} %get-tuple-element.116), channel_id=1, replica_groups=mesh['seq'=8,'vocab'=16] {'seq','vocab'}, use_global_device_ids=true, to_apply=%region_12.13 | all-reduce | flops 1536 | bytes 12288 | tf_op jit(solution)/shard_map/psum | solution.py:59
  226.8 13.5 %fusion.12 = f32[512,5376]{1,0:T(8,128)} fusion(bf16[1024,5376]{1,0:T(8,128)(2,1)} %param.7, f32[512,1024]{1,0:T(8,128)S(1)} %get-tuple-element.98, f32[512,1024]{1,0:T(8,128)} %get-tuple-element.135, f32[512]{0:T(512)S(1)} %get-tuple-element.128, f32[512]{0:T(512)S(1)} %pmax.7), kind=kOutput, calls=%fused_computation.43 | convolution fusion | flops 5639766016 | bytes 26218496 | tf_op jit(solution)/shard_map/dot_general | solution.py:74
  240.3 14.9 %reshape.58 = f32[8,64,16,336]{3,2,1,0:T(8,128)} reshape(f32[512,5376]{1,0:T(8,128)} %fusion.12) | data formatting | bytes 22020096 | tf_op jit(solution)/shard_map/reshape | solution.py:75
  255.2 12.9 %copy.37 = f32[8,16,64,336]{3,2,1,0:T(8,128)} copy(f32[8,16,64,336]{3,1,2,0:T(8,128)} %bitcast.52) | data formatting | bytes 22020096 | tf_op jit(solution)/shard_map/transpose | solution.py:76
  268.1 0.6 dynamic_slice.20
  268.7 0.6 dynamic_slice.21
  269.3 11.8 %convolution_convert_fusion = bf16[1024,5376]{1,0:T(8,128)(2,1)} fusion(bf16[512,5376]{1,0:T(8,128)(2,1)} %all-gather.3.cloned.1.call-done, f32[512,1024]{1,0:T(8,128)S(1)} %get-tuple-element.98, f32[512,1024]{1,0:T(8,128)} %get-tuple-element.135, f32[512]{0:T(512)S(1)} %get-tuple-element.128, f32[512]{0:T(512)S(1)} %pmax.7), kind=kOutput, calls=%fused_computation.8 | convolution fusion | flops 5645271040 | bytes 20713472 | tf_op jit(solution)/shard_map/dot_general | solution.py:71
  281.1 206.0 %reduce-scatter.2.cloned.1.call-done = f32[64,336]{1,0:T(8,128)} async-done(((f32[8192,336]{1,0:T(8,128)}), f32[64,336]{1,0:T(8,128)}) %reduce-scatter.2.cloned.1.call-update) | async-done | bytes 86032 | tf_op jit(solution)/shard_map/reduce_scatter | solution.py:77
  487.1 1.5 convert_element_type.14
  (49 shorter events, 1.5 us)
Async XLA Ops:
  7.2 80.5 %all-gather.3.cloned.1.call-start = ((), (), s32[]{:S(2)}) async-start(), calls=%async_computation.3 | async-start | bytes 6193152 | tf_op jit(solution)/shard_map/all_gather | solution.py:18
  7.2 26.9 %copy-start.1 = (s32[4,256]{1,0:T(4,128)S(1)}, s32[4,256]{1,0:T(4,128)}, u32[]{:S(2)}) copy-start(s32[4,256]{1,0:T(4,128)} %param.9) | copy-start | bytes 12292
  34.4 8.9 %copy-start.3 = (s32[3]{0:T(128)S(1)}, s32[3]{0:T(128)}, u32[]{:S(2)}) copy-start(s32[3]{0:T(128)} %constant.94) | copy-start | bytes 40
  34.4 8.9 %copy-start.2 = (s32[3]{0:T(128)S(1)}, s32[3]{0:T(128)}, u32[]{:S(2)}) copy-start(s32[3]{0:T(128)} %constant.97) | copy-start | bytes 40
  43.4 14.2 %copy-start = (f32[4,256]{1,0:T(4,128)S(1)}, f32[4,256]{1,0:T(4,128)}, u32[]{:S(2)}) copy-start(f32[4,256]{1,0:T(4,128)} %param.8) | copy-start | bytes 12292
  48.7 19.9 %all-to-all-start = ((s32[128,4,6]{2,1,0:T(4,128)}), s32[128,4,6]{2,1,0:T(4,128)S(1)}, u32[]{:S(2)}, u32[]{:S(2)}) async-start(s32[128,4,6]{2,1,0:T(4,128)} %copy.32), calls=%async_computation | async-start | bytes 524288 | tf_op jit(solution)/shard_map/all_to_all | solution.py:44
  68.5 15.6 %all-to-all-start.1 = ((f32[128,4,6]{2,1,0:T(4,128)}), f32[128,4,6]{2,1,0:T(4,128)S(1)}, u32[]{:S(2)}, u32[]{:S(2)}) async-start(f32[128,4,6]{2,1,0:T(4,128)} %copy.35), calls=%async_computation.1 | async-start | bytes 524288 | tf_op jit(solution)/shard_map/all_to_all | solution.py:43
  73.2 413.9 %reduce-scatter.2.cloned.1.call-start = ((), (), s32[]{:S(2)}) async-start(), calls=%async_computation.4 | async-start | bytes 12681216 | tf_op jit(solution)/shard_map/reduce_scatter | solution.py:77
Sparse Core Ops, SparseCore 0:
  34.3 40.9 all-gather.2
  268.2 218.8 reduce-scatter.1
where the time goes:
time: 496 us; the launch traced here: 495 us
  waiting for transfers between devices  222 us (45%)
  blocking collectives  150 us (30%)
  local copies, waits for them, and re-layouts  51.1 us (10%)
  matrix products  36.7 us (7%)
  between operations  14.3 us (3%)
  starting transfers between devices  13.7 us (3%)
  other arithmetic  7.71 us (2%)
    reduce_scatter x1, waiting for transfers between devices, body(): lax.psum_scatter(block_order, ('seq', 'vocab'), scatter_dimension=0, tile...  206 us
    psum x1, blocking collectives, body(): lax.psum((jnp.sum(expo, axis=1), jnp.sum(expo * logits, axis=1), cross_pa...  62.7 us
    pmax x1, blocking collectives, body(): peak_val = lax.pmax(jnp.max(logits, axis=1), ('seq', 'vocab'))  62.7 us
    all_gather x1, blocking collectives, body(): features = lax.all_gather(hidden, 'vocab', axis=1, tiled=True)  24.7 us
    reshape x1, local copies, waits for them, and re-layouts, body(): block_order = full_term.reshape(seq_count, tok_rows, vocab_count, feat_part)  14.9 us
    dot_general x1, matrix products, body(): jnp.dot(grad_logits, head_weight, preferred_element_type=jnp.float32)  13.5 us
    transpose x1, local copies, waits for them, and re-layouts, body(): block_order.transpose(0, 2, 1, 3).reshape(owner_count * tok_rows, feat_part)  12.9 us
    dot_general x1, matrix products, body(): lax.dot_general(grad_logits, gathered, (((0,), (0,)), ((), ())), preferre...  11.8 us
  transfers between devices with their start and end apart: 4, of which 3 were waited for; matrix products, arithmetic and copies ran while one was open for 7% of the time, Pallas kernels for 0%

commit v1 on v0

v1 whole, which is shorter than its diff:
```python
import functools

import jax
import jax.numpy as jnp
from jax import lax
from jax.experimental import pallas as pl
from jax.experimental.pallas import tpu as pltpu
from jax.sharding import PartitionSpec as P

loss_scale = 64.0
SLOTS = 6
OFFSETS = (0, 3, 1, 2)
LANES = 128
ANY = pl.BlockSpec(memory_space=pl.ANY)
VMEM_LIMIT = 50 * 1024 * 1024
BOTH = ("seq", "vocab")


def params():
    return pltpu.CompilerParams(vmem_limit_bytes=VMEM_LIMIT)


def cost(flops, nbytes):
    return pl.CostEstimate(flops=int(flops), bytes_accessed=int(nbytes), transcendentals=0)


def teacher_kernel(owners, vocab_rows, logits_ref, ids_ref, out_ref):
    rows, width = logits_ref.shape
    scores = logits_ref[...]
    expo = jnp.exp(scores - jnp.max(scores, axis=1, keepdims=True))
    prob = expo / jnp.sum(expo, axis=1, keepdims=True)
    ids = ids_ref[...]
    shift = vocab_rows.bit_length() - 1
    owner_iota = lax.broadcasted_iota(jnp.int32, (owners, width), 0)
    slot_iota = lax.broadcasted_iota(jnp.int32, (owners, width), 1)
    lane = lax.broadcasted_iota(jnp.int32, (owners, rows * 16), 1)
    out = jnp.zeros((owners, rows * 16), jnp.float32)
    for row in range(rows):
        row_ids = jnp.broadcast_to(ids[row : row + 1, :], (owners, width))
        row_prob = jnp.broadcast_to(prob[row : row + 1, :], (owners, width))
        owner = lax.shift_right_logical(row_ids, shift)
        start = jnp.sum((owner < owner_iota).astype(jnp.int32), axis=1, keepdims=True)
        place = jnp.where(owner == owner_iota, slot_iota - start, -1)
        local = (row_ids - owner * vocab_rows + 1).astype(jnp.float32)
        for slot in range(SLOTS):
            hit = place == slot
            value = jnp.sum(jnp.where(hit, row_prob, 0.0), axis=1, keepdims=True)
            index = jnp.sum(jnp.where(hit, local, 0.0), axis=1, keepdims=True) - 1.0
            out = out + jnp.where(lane == row * 16 + slot, value, 0.0)
            out = out + jnp.where(lane == row * 16 + 8 + slot, index, 0.0)
    out_ref[...] = out


def teacher_rows(owners, vocab_rows, teacher_logits, teacher_ids):
    rows = teacher_logits.shape[0]
    return pl.pallas_call(
        functools.partial(teacher_kernel, owners, vocab_rows),
        out_shape=jax.ShapeDtypeStruct((owners, rows * 16), jnp.float32),
        compiler_params=params(),
        cost_estimate=cost(4e6, 40000),
    )(teacher_logits, teacher_ids)


def dot_nt(a, b):
    return lax.dot_general(a, b, (((1,), (1,)), ((), ())), preferred_element_type=jnp.float32)


def local_stats(logits, target):
    peak = jnp.max(logits, axis=0, keepdims=True)
    expo = jnp.exp(logits - peak)
    total = jnp.sum(expo, axis=0, keepdims=True)
    mean = jnp.sum(expo * logits, axis=0, keepdims=True) / total
    cross = jnp.sum(target * logits, axis=0, keepdims=True)
    lse = peak + jnp.log(total)
    row = lax.broadcasted_iota(jnp.int32, (8, LANES), 0)
    return jnp.where(row == 0, lse, jnp.where(row == 1, mean, jnp.where(row == 2, cross, 0.0)))


def load_blocks(pieces, dest, sems):
    copies = [
        pltpu.make_async_copy(src, dest.at[pl.ds(pl.multiple_of(row, 32), src.shape[0])], sems.at[k])
        for k, (src, row) in enumerate(pieces)
    ]
    for copy in copies:
        copy.start()
    return copies


def first_kernel(pos, got, w, own, own2, left, left2, right, right2, out, target, stats, held, keep, teach, sems):
    step = pl.program_id(0)
    z, core = pos[0], pos[1]
    mine, other = core * 64, (1 - core) * 64

    @pl.when(step == 0)
    def _():
        copies = load_blocks(
            [(own, mine), (own2, other), (left, 128 + mine), (left2, 128 + other), (right, 256 + mine), (right2, 256 + other)],
            held, sems,
        )
        flipped = got[...].T
        source = lax.broadcasted_iota(jnp.int32, (LANES, 4 * LANES), 0)
        token = lax.broadcasted_iota(jnp.int32, (LANES, 4 * LANES), 1)
        spread = jnp.zeros((16, 4 * LANES), jnp.float32)
        for row in range(4):
            pick = (token == source * 4 + row).astype(jnp.float32)
            spread = spread + jnp.dot(
                flipped[row * 16 : row * 16 + 16], pick,
                precision=lax.Precision.HIGHEST, preferred_element_type=jnp.float32,
            )
        for block in range(4):
            teach[block] = spread[:, block * LANES : (block + 1) * LANES]
        for copy in copies:
            copy.wait()

    rows = w.shape[0]
    logits = dot_nt(w[...], held[...])
    base = pl.multiple_of(step * rows, rows)
    word = (lax.broadcasted_iota(jnp.int32, (rows, LANES), 0) + step * rows).astype(jnp.float32)
    for slot in range(4):
        info = teach[(z + OFFSETS[slot]) % 4]
        dense = jnp.zeros((rows, LANES), jnp.float32)
        for k in range(SLOTS):
            dense = dense + jnp.where(word == info[8 + k : 9 + k], info[k : k + 1], 0.0)
        target[slot] = dense
        if slot < 3:
            part = logits[:, slot * LANES : (slot + 1) * LANES]
            out[slot] = part
            keep[slot, pl.ds(base, rows)] = part
            keep[3 + slot, pl.ds(base, rows)] = dense

    @pl.when(step == pl.num_programs(0) - 1)
    def _():
        for slot in range(3):
            stats[slot] = local_stats(keep[slot], keep[3 + slot])


def first_logits(pos, got, w, blocks):
    vocab, width = w.shape
    rows = 256
    grid_spec = pltpu.PrefetchScalarGridSpec(
        num_scalar_prefetch=1,
        grid=(vocab // rows,),
        in_specs=[
            pl.BlockSpec(got.shape, lambda i, s: (0, 0)),
            pl.BlockSpec((rows, width), lambda i, s: (i, 0)),
        ] + [ANY] * 6,
        out_specs=[
            pl.BlockSpec((3, rows, LANES), lambda i, s: (0, i, 0)),
            pl.BlockSpec((4, rows, LANES), lambda i, s: (0, i, 0)),
            pl.BlockSpec((3, 8, LANES), lambda i, s: (0, 0, 0)),
        ],
        scratch_shapes=[
            pltpu.VMEM((384, width), jnp.bfloat16),
            pltpu.VMEM((6, vocab, LANES), jnp.float32),
            pltpu.VMEM((4, 16, LANES), jnp.float32),
            pltpu.SemaphoreType.DMA((6,)),
        ],
    )
    return pl.pallas_call(
        first_kernel,
        grid_spec=grid_spec,
        out_shape=[
            jax.ShapeDtypeStruct((3, vocab, LANES), jnp.float32),
            jax.ShapeDtypeStruct((4, vocab, LANES), jnp.float32),
            jax.ShapeDtypeStruct((3, 8, LANES), jnp.float32),
        ],
        compiler_params=params(),
        cost_estimate=cost(2 * vocab * width * 384, vocab * width * 2 + 384 * width * 2),
    )(pos, got, w, *blocks)


def last_kernel(pos, w, target, early, far_a, far_b, far_a2, far_b2, out, send, held, keep, table, sems):
    step = pl.program_id(0)
    z, core = pos[0], pos[1]
    mine, other = core * 64, (1 - core) * 64

    @pl.when(step == 0)
    def _():
        copies = load_blocks(
            [(far_a, mine), (far_b, mine + 32), (far_a2, other), (far_b2, other + 32)], held, sems
        )
        for copy in copies:
            copy.wait()

    rows = w.shape[0]
    logits = dot_nt(w[...], held[...])
    out[...] = logits
    base = pl.multiple_of(step * rows, rows)
    keep[0, pl.ds(base, rows)] = logits
    keep[1, pl.ds(base, rows)] = target[0]

    @pl.when(step == pl.num_programs(0) - 1)
    def _():
        for slot in range(3):
            table[(z + OFFSETS[slot]) % 4] = early[slot]
        table[(z + OFFSETS[3]) % 4] = local_stats(keep[0], keep[1])
        lane = lax.broadcasted_iota(jnp.int32, (32, LANES), 1)
        row = lax.broadcasted_iota(jnp.int32, (32, LANES), 0)
        for block in range(4):
            info = table[block]
            send[:, block * LANES : (block + 1) * LANES] = jnp.broadcast_to(info[0:1], (LANES, LANES))
            extra = jnp.zeros((32, LANES), jnp.float32)
            for kind in range(3):
                for token in range(4):
                    value = jnp.sum(
                        jnp.where(lane == row * 4 + token, info[kind : kind + 1], 0.0), axis=1, keepdims=True
                    )
                    extra = extra + jnp.where(lane == kind * 4 + token, value, 0.0)
            send[block * 32 : (block + 1) * 32, 4 * LANES : 5 * LANES] = extra


def last_logits(pos, w, target, early, blocks):
    vocab, width = w.shape
    rows = 256
    grid_spec = pltpu.PrefetchScalarGridSpec(
        num_scalar_prefetch=1,
        grid=(vocab // rows,),
        in_specs=[
            pl.BlockSpec((rows, width), lambda i, s: (i, 0)),
            pl.BlockSpec((1, rows, LANES), lambda i, s: (3, i, 0)),
            pl.BlockSpec((3, 8, LANES), lambda i, s: (0, 0, 0)),
        ] + [ANY] * 4,
        out_specs=[
            pl.BlockSpec((rows, LANES), lambda i, s: (i, 0)),
            pl.BlockSpec((LANES, 5 * LANES), lambda i, s: (0, 0)),
        ],
        scratch_shapes=[
            pltpu.VMEM((LANES, width), jnp.bfloat16),
            pltpu.VMEM((2, vocab, LANES), jnp.float32),
            pltpu.VMEM((4, 8, LANES), jnp.float32),
            pltpu.SemaphoreType.DMA((4,)),
        ],
    )
    return pl.pallas_call(
        last_kernel,
        grid_spec=grid_spec,
        out_shape=[
            jax.ShapeDtypeStruct((vocab, LANES), jnp.float32),
            jax.ShapeDtypeStruct((LANES, 5 * LANES), jnp.float32),
        ],
        compiler_params=params(),
        cost_estimate=cost(2 * vocab * width * 128, vocab * width * 2),
    )(pos, w, target, early, *blocks)


def grad_of(logits, lse, target):
    return loss_scale * (jnp.exp(logits - lse) - target)


def far_grad_kernel(pos, stats, logits, target, w, mine_out, other_out, grad_out, lse_out, loss_out, left, acc, lse_z):
    step = pl.program_id(0)
    z, core = pos[0], pos[1]

    @pl.when(step == 0)
    def _():
        parts = stats[:, : 4 * LANES]
        peak = jnp.max(parts, axis=0, keepdims=True)
        lse = peak + jnp.log(jnp.sum(jnp.exp(parts - peak), axis=0, keepdims=True))
        for block in range(4):
            lse_z[block] = jnp.broadcast_to(lse[:, block * LANES : (block + 1) * LANES], (8, LANES))
        lse_out[...] = lse_z[...]
        few = stats[:, 4 * LANES :]
        peak = jnp.max(few, axis=0, keepdims=True)
        weight = jnp.exp(few - peak)
        total = jnp.sum(weight, axis=0, keepdims=True)
        mean = jnp.sum(weight * pltpu.roll(few, LANES - 4, 1), axis=0, keepdims=True) / total
        cross = jnp.sum(pltpu.roll(few, LANES - 8, 1), axis=0, keepdims=True)
        lse4 = peak + jnp.log(total)
        row = lax.broadcasted_iota(jnp.int32, (8, LANES), 0)
        loss_out[...] = jnp.where(row == 0, lse4 - cross, lse4 - mean)
        far = lse_z[(z + OFFSETS[3]) % 4]
        grad = grad_of(logits[...], far[0:1], target[0])
        grad_out[...] = grad.astype(jnp.bfloat16)
        left[...] = grad.T.astype(jnp.bfloat16)

    acc[...] = jnp.dot(left[...], w[...], preferred_element_type=jnp.float32)
    mine_out[...] = acc[pl.ds(pl.multiple_of(core * 64, 64), 64)]
    other_out[...] = acc[pl.ds(pl.multiple_of((1 - core) * 64, 64), 64)].astype(jnp.bfloat16)


def far_grad(pos, stats, logits, target, w):
    vocab, width = w.shape
    cols = 768
    grid_spec = pltpu.PrefetchScalarGridSpec(
        num_scalar_prefetch=1,
        grid=(width // cols,),
        in_specs=[
            pl.BlockSpec((LANES, 5 * LANES), lambda i, s: (0, 0)),
            pl.BlockSpec((vocab, LANES), lambda i, s: (0, 0)),
            pl.BlockSpec((1, vocab, LANES), lambda i, s: (3, 0, 0)),
            pl.BlockSpec((vocab, cols), lambda i, s: (0, i)),
        ],
        out_specs=[
            pl.BlockSpec((64, cols), lambda i, s: (0, i)),
            pl.BlockSpec((64, cols), lambda i, s: (0, i)),
            pl.BlockSpec((vocab, LANES), lambda i, s: (0, 0)),
            pl.BlockSpec((4, 8, LANES), lambda i, s: (0, 0, 0)),
            pl.BlockSpec((8, LANES), lambda i, s: (0, 0)),
        ],
        scratch_shapes=[
            pltpu.VMEM((LANES, vocab), jnp.bfloat16),
            pltpu.VMEM((LANES, cols), jnp.float32),
            pltpu.VMEM((4, 8, LANES), jnp.float32),
        ],
    )
    return pl.pallas_call(
        far_grad_kernel,
        grid_spec=grid_spec,
        out_shape=[
            jax.ShapeDtypeStruct((64, width), jnp.float32),
            jax.ShapeDtypeStruct((64, width), jnp.bfloat16),
            jax.ShapeDtypeStruct((vocab, LANES), jnp.bfloat16),
            jax.ShapeDtypeStruct((4, 8, LANES), jnp.float32),
            jax.ShapeDtypeStruct((8, LANES), jnp.float32),
        ],
        compiler_params=params(),
        cost_estimate=cost(2 * vocab * width * 128, vocab * width * 2),
    )(pos, stats, logits, target, w)


def grads_kernel(pos, logits, target, lse, far, wide_out, left_out):
    z = pos[0]
    for slot in range(3):
        row = lse[(z + OFFSETS[slot]) % 4]
        grad = grad_of(logits[slot], row[0:1], target[slot])
        wide_out[:, slot * LANES : (slot + 1) * LANES] = grad.astype(jnp.bfloat16)
        left_out[slot * LANES : (slot + 1) * LANES, :] = grad.T.astype(jnp.bfloat16)
    wide_out[:, 3 * LANES :] = far[...]


def near_grads(pos, logits, target, lse, far):
    vocab = far.shape[0]
    whole = pl.BlockSpec(memory_space=pltpu.VMEM)
    return pl.pallas_call(
        grads_kernel,
        in_specs=[pl.BlockSpec(memory_space=pltpu.SMEM)] + [whole] * 4,
        out_specs=[whole] * 2,
        out_shape=[
            jax.ShapeDtypeStruct((vocab, 4 * LANES), jnp.bfloat16),
            jax.ShapeDtypeStruct((3 * LANES, vocab), jnp.bfloat16),
        ],
        compiler_params=params(),
        cost_estimate=cost(2e6, 5e6),
    )(pos, logits, target, lse, far)


def near_kernel(pos, left, w, mine_out, other_out, own_out, acc):
    core = pos[1]
    acc[...] = jnp.dot(left[...], w[...], preferred_element_type=jnp.float32)
    for slot in range(3):
        mine_out[slot] = acc[pl.ds(pl.multiple_of(slot * 128 + core * 64, 64), 64)]
        part = acc[pl.ds(pl.multiple_of(slot * 128 + (1 - core) * 64, 64), 64)].astype(jnp.bfloat16)
        if slot == 0:
            own_out[...] = part
        else:
            other_out[slot - 1] = part


def near_grad(pos, left, w):
    vocab, width = w.shape
    cols = 768
    grid_spec = pltpu.PrefetchScalarGridSpec(
        num_scalar_prefetch=1,
        grid=(width // cols,),
        in_specs=[
            pl.BlockSpec((3 * LANES, vocab), lambda i, s: (0, 0)),
            pl.BlockSpec((vocab, cols), lambda i, s: (0, i)),
        ],
        out_specs=[
            pl.BlockSpec((3, 64, cols), lambda i, s: (0, 0, i)),
            pl.BlockSpec((2, 64, cols), lambda i, s: (0, 0, i)),
            pl.BlockSpec((64, cols), lambda i, s: (0, i)),
        ],
        scratch_shapes=[pltpu.VMEM((3 * LANES, cols), jnp.float32)],
    )
    return pl.pallas_call(
        near_kernel,
        grid_spec=grid_spec,
        out_shape=[
            jax.ShapeDtypeStruct((3, 64, width), jnp.float32),
            jax.ShapeDtypeStruct((2, 64, width), jnp.bfloat16),
            jax.ShapeDtypeStruct((64, width), jnp.bfloat16),
        ],
        compiler_params=params(),
        cost_estimate=cost(2 * vocab * width * 384, vocab * width * 2),
    )(pos, left, w)


def weight_kernel(pos, grad, own, own2, left, left2, right, right2, far_a, far_b, far_a2, far_b2, out, held, sems):
    core = pos[1]
    mine, other = core * 64, (1 - core) * 64

    @pl.when(pl.program_id(0) == 0)
    def _():
        copies = load_blocks(
            [
                (own, mine), (own2, other), (left, 128 + mine), (left2, 128 + other),
                (right, 256 + mine), (right2, 256 + other),
                (far_a, 384 + mine), (far_b, 384 + mine + 32), (far_a2, 384 + other), (far_b2, 384 + other + 32),
            ],
            held, sems,
        )
        for copy in copies:
            copy.wait()

    width = out.shape[1]
    cols = 768
    for tile in range(width // cols):
        at = slice(tile * cols, (tile + 1) * cols)
        out[:, at] = jnp.dot(grad[...], held[:, at], preferred_element_type=jnp.float32).astype(jnp.bfloat16)


def weight_grad(pos, grad, blocks, width):
    vocab, tokens = grad.shape
    rows = 256
    grid_spec = pltpu.PrefetchScalarGridSpec(
        num_scalar_prefetch=1,
        grid=(vocab // rows,),
        in_specs=[pl.BlockSpec((rows, tokens), lambda i, s: (i, 0))] + [ANY] * 10,
        out_specs=pl.BlockSpec((rows, width), lambda i, s: (i, 0)),
        scratch_shapes=[pltpu.VMEM((tokens, width), jnp.bfloat16), pltpu.SemaphoreType.DMA((10,))],
    )
    return pl.pallas_call(
        weight_kernel,
        grid_spec=grid_spec,
        out_shape=jax.ShapeDtypeStruct((vocab, width), jnp.bfloat16),
        compiler_params=params(),
        cost_estimate=cost(2 * vocab * width * tokens, vocab * width * 2 + tokens * width * 2),
    )(pos, grad, *blocks)


def body(hidden, head_weight, teacher_logits, teacher_ids):
    seq_count = lax.axis_size("seq")
    vocab_count = lax.axis_size("vocab")
    owners = seq_count * vocab_count
    vocab_rows, width = head_weight.shape
    tok_rows, feat_part = hidden.shape
    seq_index = lax.axis_index("seq")
    pos = jnp.stack([seq_index // 2, seq_index % 2]).astype(jnp.int32)
    up = [(i, (i + 2) % seq_count) for i in range(seq_count)]
    down = [(i, (i - 2) % seq_count) for i in range(seq_count)]
    twin = [(i, i ^ 1) for i in range(seq_count)]

    def move(x, perm):
        return lax.ppermute(x, "seq", perm)

    f32 = jnp.float32
    bf16 = jnp.bfloat16
    half = tok_rows // 2

    spread = jnp.broadcast_to(hidden[None], (vocab_count, tok_rows, feat_part))
    spread = lax.all_to_all(spread, "vocab", split_axis=0, concat_axis=0, tiled=True)
    own = spread.transpose(1, 0, 2).reshape(tok_rows, width)
    left = move(own, up)
    right = move(own, down)
    own2 = move(own, twin)
    teach = teacher_rows(owners, vocab_rows, teacher_logits, teacher_ids)
    teach, _ = lax.optimization_barrier((teach, own))
    got = lax.all_to_all(teach, BOTH, split_axis=0, concat_axis=0, tiled=True)
    far_a = move(left[:half], up)
    far_b = move(right[half:], down)
    left2 = move(left, twin)
    right2 = move(right, twin)
    near_blocks = (own, own2, left, left2, right, right2)
    logits, target, early = first_logits(pos, got, head_weight, near_blocks)
    far_blocks = (far_a, far_b, move(far_a, twin), move(far_b, twin))
    far_logits, send = last_logits(pos, head_weight, target, early, far_blocks)
    stats = lax.all_to_all(send, BOTH, split_axis=0, concat_axis=0, tiled=True)

    far_mine, far_other, grad_far, lse, loss = far_grad(pos, stats, far_logits, target, head_weight)
    far_swap = move(far_other, twin)
    wide, left_grad = near_grads(pos, logits, target, lse, grad_far)
    far_sum = (far_mine + far_swap.astype(f32)).astype(bf16)
    go_up = move(far_sum[:half], up)
    go_down = move(far_sum[half:], down)
    mine, other, own_other = near_grad(pos, left_grad, head_weight)
    swap = move(other, twin)
    own_swap = move(own_other, twin)
    to_left = mine[1] + swap[0].astype(f32)
    to_right = mine[2] + swap[1].astype(f32)
    right_b = move(to_right[half:].astype(bf16), up)
    left_b = move(to_left[:half].astype(bf16), down)
    right_a = move((to_right[:half] + go_up.astype(f32)).astype(bf16), up)
    left_a = move((to_left[half:] + go_down.astype(f32)).astype(bf16), down)
    grad_weight = weight_grad(pos, wide, near_blocks + far_blocks, width)
    own_sum = mine[0] + own_swap.astype(f32)
    upper = own_sum[:half] + right_a.astype(f32) + left_b.astype(f32)
    lower = own_sum[half:] + right_b.astype(f32) + left_a.astype(f32)
    total = jnp.concatenate([upper, lower], axis=0).astype(bf16)
    parts = total.reshape(tok_rows, vocab_count, feat_part).transpose(1, 0, 2)
    parts = lax.all_to_all(parts, "vocab", split_axis=0, concat_axis=0, tiled=True)
    grad_hidden = jnp.sum(parts.astype(f32), axis=0).astype(bf16)
    rows = teacher_logits.shape[0]
    return loss[0, :rows], loss[1, :rows], grad_hidden, grad_weight


def solution(mesh):
    placed = (
        P("seq", "vocab"),
        P(("seq", "vocab"), None),
        P(("seq", "vocab"), None),
        P(("seq", "vocab"), None),
    )
    return jax.shard_map(
        body,
        mesh=mesh,
        in_specs=placed,
        out_specs=(
            P(("seq", "vocab")),
            P(("seq", "vocab")),
            P("seq", "vocab"),
            P(("seq", "vocab"), None),
        ),
        check_vma=False,
    )
```

time: 496 us -> 183 us (0.37)
  waiting for transfers between devices: 222 us -> 50.3 us
  blocking collectives: 150 us -> 37.2 us
  Pallas kernels: 0 us -> 57.1 us
  local copies, waits for them, and re-layouts: 51.1 us -> 7.3 us
  matrix products: 36.7 us -> 0 us
  between operations: 14.3 us -> 0.9 us
  starting transfers between devices: 13.7 us -> 24.7 us
    reduce_scatter x1 -> x0, waiting for transfers between devices: 206 us -> none  [body(): lax.psum_scatter(block_order, ('seq', 'vocab'), scatter_dimension=0, tile...]
    psum x1 -> x0, blocking collectives: 62.7 us -> none  [body(): lax.psum((jnp.sum(expo, axis=1), jnp.sum(expo * logits, axis=1), cross_pa...]
    pmax x1 -> x0, blocking collectives: 62.7 us -> none  [body(): peak_val = lax.pmax(jnp.max(logits, axis=1), ('seq', 'vocab'))]
    pallas_call x0 -> x7, Pallas kernels: none -> 57.1 us  [the longest x1 13.8 us: first_logits(): pl.pallas_call(first_kernel, grid_spec=grid_spec, out_shape=[jax.ShapeDty...]
    ppermute x0 -> x18, waiting for transfers between devices: none -> 42.9 us  [move(): return lax.ppermute(x, 'seq', perm)]
    all_to_all x0 -> x2, blocking collectives: none -> 37.2 us  [the longest x1 21.3 us: body(): lax.all_to_all(spread, 'vocab', split_axis=0, concat_axis=0, tiled=True)]
    dot_general x3 -> x0, matrix products: 36.7 us -> none  [the longest x1 13.5 us: body(): jnp.dot(grad_logits, head_weight, preferred_element_type=jnp.float32)]
    all_gather x1 -> x0, blocking collectives: 24.7 us -> none  [body(): features = lax.all_gather(hidden, 'vocab', axis=1, tiled=True)]
  transfers between devices with their start and end apart: 4 -> 20, of which waited for: 3 -> 12; matrix products, arithmetic and copies ran while one was open for 7% -> 1% of each run, Pallas kernels for 0% -> 22%
where the time goes in v1:
time: 183 us; the launch traced here: 182 us
  Pallas kernels  57.1 us (31%)
  waiting for transfers between devices  50.3 us (27%)
  blocking collectives  37.2 us (20%)
  starting transfers between devices  24.7 us (13%)
  local copies, waits for them, and re-layouts  7.3 us (4%)
  other arithmetic  4.55 us (2%)
    ppermute x18, waiting for transfers between devices, move(): return lax.ppermute(x, 'seq', perm)  42.9 us
    all_to_all x1, blocking collectives, body(): lax.all_to_all(spread, 'vocab', split_axis=0, concat_axis=0, tiled=True)  21.3 us
    all_to_all x1, blocking collectives, body(): stats = lax.all_to_all(send, BOTH, split_axis=0, concat_axis=0, tiled=True)  15.9 us
    ppermute x18, starting transfers between devices, move(): return lax.ppermute(x, 'seq', perm)  14.9 us
    pallas_call x1, Pallas kernels, first_logits(): pl.pallas_call(first_kernel, grid_spec=grid_spec, out_shape=[jax.ShapeDty...  13.8 us
    pallas_call x1, Pallas kernels, weight_grad(): pl.pallas_call(weight_kernel, grid_spec=grid_spec, out_shape=jax.ShapeDty...  11.7 us
    pallas_call x1, Pallas kernels, near_grad(): pl.pallas_call(near_kernel, grid_spec=grid_spec, out_shape=[jax.ShapeDtyp...  11.1 us
    pallas_call x1, Pallas kernels, far_grad(): pl.pallas_call(far_grad_kernel, grid_spec=grid_spec, out_shape=[jax.Shape...  8.4 us
  transfers between devices with their start and end apart: 20, of which 12 were waited for; matrix products, arithmetic and copies ran while one was open for 1% of the time, Pallas kernels for 22%

profile of v1, /device:TPU:0, one launch (start us, length us, event | category | flops | bytes accessed | tf_op | source)
XLA Modules:
  0.0 182.1 jit_solution(3965788662759362240)
XLA Ops:
  1.5 21.3 %all_to_all.32 = bf16[16,64,336]{2,1,0:T(8,128)(2,1)S(1)} all-to-all(bf16[16,64,336]{2,1,0:T(8,128)(2,1)S(1)} %broadcast_in_dim.2), channel_id=1, replica_groups=mesh['seq'=8,'vocab'=16] {'vocab'}, dimensions={0} | all-to-all | bytes 1376256 | tf_op jit(solution)/shard_map/all_to_all | solution.py:452
  24.2 4.1 %collective-permute-start.3 = (bf16[64,5376]{1,0:T(8,128)(2,1)S(1)}, bf16[64,5376]{1,0:T(8,128)(2,1)S(1)}, u32[]{:S(2)}, u32[]{:S(2)}) collective-permute-start(bf16[64,5376]{1,0:T(8,128)(2,1)S(1)} %reshape.31.own), channel_id=1, source_target_pairs={{0,96},{16,112},{32,0},{48,16},{64,32},{80,48},{96,64},{112,80},{1... | collective-permute-start | bytes 2064392 | tf_op jit(solution)/shard_map/ppermute | solution.py:445
  28.3 13.6 %collective-permute-done.3.right = bf16[64,5376]{1,0:T(8,128)(2,1)S(1)} collective-permute-done((bf16[64,5376]{1,0:T(8,128)(2,1)S(1)}, bf16[64,5376]{1,0:T(8,128)(2,1)S(1)}, u32[]{:S(2)}, u32[]{:S(2)}) %collective-permute-start.3) | collective-permute-done | bytes 688160 | tf_op jit(solution)/shard_map/ppermute | solution.py:445
  41.8 3.4 %collective-permute-done.1.left = bf16[64,5376]{1,0:T(8,128)(2,1)S(1)} collective-permute-done((bf16[64,5376]{1,0:T(8,128)(2,1)S(1)}, bf16[64,5376]{1,0:T(8,128)(2,1)S(1)}, u32[]{:S(2)}, u32[]{:S(2)}) %collective-permute-start.1) | collective-permute-done | bytes 688160 | tf_op jit(solution)/shard_map/ppermute | solution.py:445
  46.8 1.3 collective-permute-start.5
  48.1 1.9 %shard_map.75 = f32[128,64]{1,0:T(8,128)} custom-call(f32[4,256]{1,0:T(4,128)S(1)} %copy-done.2, s32[4,256]{1,0:T(4,128)S(1)} %copy-done.3), custom_call_target="tpu_custom_call" | custom-call | flops 4000000 | bytes 40000 | tf_op jit(solution)/shard_map/pallas_call | solution.py:56
  50.1 5.6 %all-to-all-start.1 = ((f32[128,1,64]{2,1,0:T(1,128)}), f32[128,1,64]{2,1,0:T(1,128)S(1)}, u32[]{:S(2)}, u32[]{:S(2)}) async-start(f32[128,1,64]{2,1,0:T(1,128)} %bitcast.4), calls=%async_computation.1 | async-start | bytes 131072 | tf_op jit(solution)/shard_map/all_to_all | solution.py:459
  55.7 0.9 collective-permute-done.6.far_b
  56.7 1.2 collective-permute-done.5.far_a
  57.9 7.3 %all-to-all-done.1 = f32[128,1,64]{2,1,0:T(1,128)S(1)} async-done(((f32[128,1,64]{2,1,0:T(1,128)}), f32[128,1,64]{2,1,0:T(1,128)S(1)}, u32[]{:S(2)}, u32[]{:S(2)}) %all-to-all-start.1) | async-done | bytes 32800 | tf_op jit(solution)/shard_map/all_to_all | solution.py:459
  65.1 13.8 %shard_map.76 = (f32[3,1024,128]{2,1,0:T(8,128)}, f32[4,1024,128]{2,1,0:T(8,128)}, f32[3,8,128]{2,1,0:T(8,128)S(1)}) custom-call(s32[2]{0:T(128)S(1)} %pad_add_fusion.pos, f32[128,64]{1,0:T(8,128)S(1)} %bitcast.37, bf16[1024,5376]{1,0:T(8,128)(2,1)} %w.7, bf16[64,5376]{1,0:T(8,128)(2,1)S(1)} %reshape.31.own, bf16[64,5376]{1,0:T(8,128)(2,1)} %collective-permute-done.own2, ...), custom_call_target="tpu_custom_call" | custom-call | flops 4227858432 | bytes 15138816 | tf_op jit(solution)/shard_map/pallas_call | solution.py:159
  78.9 8.1 %shard_map.77 = (f32[1024,128]{1,0:T(8,128)S(1)}, f32[128,640]{1,0:T(8,128)S(1)}) custom-call(s32[2]{0:T(128)S(1)} %pad_add_fusion.pos, bf16[1024,5376]{1,0:T(8,128)(2,1)} %w.7, f32[4,1024,128]{2,1,0:T(8,128)} %get-tuple-element.21.target, f32[3,8,128]{2,1,0:T(8,128)S(1)} %get-tuple-element.22.early, bf16[32,5376]{1,0:T(8,128)(2,1)S(1)} %collective-permute-done.5.far_a, ...), custom_call_target="tpu_custom_call" | custom-call | flops 1409286144 | bytes 11010048 | tf_op jit(solution)/shard_map/pallas_call | solution.py:234
  87.4 15.9 %all_to_all.33 = f32[128,1,640]{2,1,0:T(1,128)S(1)} all-to-all(f32[128,1,640]{2,1,0:T(1,128)S(1)} %copy.10), channel_id=1, replica_groups=mesh['seq'=8,'vocab'=16] {'seq','vocab'}, dimensions={0} | all-to-all | bytes 655360 | tf_op jit(solution)/shard_map/all_to_all | solution.py:468
  103.4 8.4 %shard_map.78 = (f32[64,5376]{1,0:T(8,128)S(1)}, bf16[64,5376]{1,0:T(8,128)(2,1)S(1)}, bf16[1024,128]{1,0:T(8,128)(2,1)S(1)}, f32[4,8,128]{2,1,0:T(8,128)S(1)}, f32[8,128]{1,0:T(8,128)S(1)}) custom-call(s32[2]{0:T(128)S(1)} %pad_add_fusion.pos, f32[128,640]{1,0:T(8,128)S(1)} %bitcast.35, f32[1024,128]{1,0:T(8,128)S(1)} %get-tuple-element.24.logits, ...), custom_call_target="tpu_custom_call" | custom-call | flops 1409286144 | bytes 11010048 | tf_op jit(solution)/shard_map/pallas_call | solution.py:306
  111.9 2.1 %shard_map.79 = (bf16[1024,512]{1,0:T(8,128)(2,1)S(1)}, bf16[384,1024]{1,0:T(8,128)(2,1)S(1)}) custom-call(s32[2]{0:T(128)S(1)} %pad_add_fusion.pos, f32[3,1024,128]{2,1,0:T(8,128)S(1)} %copy-done, f32[4,1024,128]{2,1,0:T(8,128)} %get-tuple-element.21.target, f32[4,8,128]{2,1,0:T(8,128)S(1)} %get-tuple-element.27.lse, ...), custom_call_target="tpu_custom_call" | custom-call | flops 2000000 | bytes 5000000 | tf_op jit(solution)/shard_map/pallas_call | solution.py:334
  114.0 1.0 copy-done.4
  114.9 11.1 %shard_map.80 = (f32[3,64,5376]{2,1,0:T(8,128)}, bf16[2,64,5376]{2,1,0:T(8,128)(2,1)S(1)}, bf16[64,5376]{1,0:T(8,128)(2,1)S(1)}) custom-call(s32[2]{0:T(128)S(1)} %pad_add_fusion.pos, bf16[384,1024]{1,0:T(8,128)(2,1)S(1)} %get-tuple-element.29.left, bf16[1024,5376]{1,0:T(8,128)(2,1)} %w.7), custom_call_target="tpu_custom_call" | custom-call | flops 4227858432 | bytes 11010048 | tf_op jit(solution)/shard_map/pallas_call | solution.py:376
  126.8 0.9 collective-permute-start.12
  127.7 2.4 %collective-permute-start.16 = (bf16[32,5376]{1,0:T(8,128)(2,1)S(1)}, bf16[32,5376]{1,0:T(8,128)(2,1)S(1)}, u32[]{:S(2)}, u32[]{:S(2)}) collective-permute-start(bf16[32,5376]{1,0:T(8,128)(2,1)S(1)} %get-tuple-element.41), channel_id=1, source_target_pairs={{0,96},{16,112},{32,0},{48,16},{64,32},{80,48},{96,64},{112,80},{1... | collective-permute-start | bytes 1032200 | tf_op jit(solution)/shard_map/ppermute | solution.py:445
  130.6 1.0 collective-permute-start.14
  131.6 7.0 %collective-permute-done.16 = bf16[32,5376]{1,0:T(8,128)(2,1)S(1)} collective-permute-done((bf16[32,5376]{1,0:T(8,128)(2,1)S(1)}, bf16[32,5376]{1,0:T(8,128)(2,1)S(1)}, u32[]{:S(2)}, u32[]{:S(2)}) %collective-permute-start.16) | collective-permute-done | bytes 344096 | tf_op jit(solution)/shard_map/ppermute | solution.py:445
  138.7 3.7 %collective-permute-start.17 = (bf16[32,5376]{1,0:T(8,128)(2,1)S(1)}, bf16[32,5376]{1,0:T(8,128)(2,1)S(1)}, u32[]{:S(2)}, u32[]{:S(2)}) collective-permute-start(bf16[32,5376]{1,0:T(8,128)(2,1)S(1)} %fusion.1), channel_id=1, source_target_pairs={{0,96},{16,112},{32,0},{48,16},{64,32},{80,48},{96,64},{112,80},{1... | collective-permute-start | bytes 1032200 | tf_op jit(solution)/shard_map/ppermute | solution.py:445
  142.7 3.3 %collective-permute-done.14 = bf16[32,5376]{1,0:T(8,128)(2,1)S(1)} collective-permute-done((bf16[32,5376]{1,0:T(8,128)(2,1)S(1)}, bf16[32,5376]{1,0:T(8,128)(2,1)S(1)}, u32[]{:S(2)}, u32[]{:S(2)}) %collective-permute-start.14) | collective-permute-done | bytes 344096 | tf_op jit(solution)/shard_map/ppermute | solution.py:445
  146.0 6.6 %collective-permute-done.17 = bf16[32,5376]{1,0:T(8,128)(2,1)S(1)} collective-permute-done((bf16[32,5376]{1,0:T(8,128)(2,1)S(1)}, bf16[32,5376]{1,0:T(8,128)(2,1)S(1)}, u32[]{:S(2)}, u32[]{:S(2)}) %collective-permute-start.17) | collective-permute-done | bytes 344096 | tf_op jit(solution)/shard_map/ppermute | solution.py:445
  152.6 1.9 %collective-permute-done.15 = bf16[32,5376]{1,0:T(8,128)(2,1)S(1)} collective-permute-done((bf16[32,5376]{1,0:T(8,128)(2,1)S(1)}, bf16[32,5376]{1,0:T(8,128)(2,1)S(1)}, u32[]{:S(2)}, u32[]{:S(2)}) %collective-permute-start.15) | collective-permute-done | bytes 344096 | tf_op jit(solution)/shard_map/ppermute | solution.py:445
  154.6 4.7 %collective-permute-done.13 = bf16[32,5376]{1,0:T(8,128)(2,1)S(1)} collective-permute-done((bf16[32,5376]{1,0:T(8,128)(2,1)S(1)}, bf16[32,5376]{1,0:T(8,128)(2,1)S(1)}, u32[]{:S(2)}, u32[]{:S(2)}) %collective-permute-start.13) | collective-permute-done | bytes 344096 | tf_op jit(solution)/shard_map/ppermute | solution.py:445
  159.3 0.9 fusion.7
  160.9 1.6 concatenate.10
  162.5 1.0 maximum_bitcast_fusion
  163.6 4.3 %all-to-all-start.3 = ((bf16[16,64,336]{2,1,0:T(8,128)(2,1)}), bf16[16,64,336]{2,1,0:T(8,128)(2,1)}, u32[]{:S(2)}, u32[]{:S(2)}) async-start(bf16[16,64,336]{2,1,0:T(8,128)(2,1)} %maximum_bitcast_fusion), calls=%async_computation.3 | async-start | bytes 1572864 | tf_op jit(solution)/shard_map/all_to_all | solution.py:491
  168.4 11.7 %shard_map.81 = bf16[1024,5376]{1,0:T(8,128)(2,1)} custom-call(s32[2]{0:T(128)S(1)} %pad_add_fusion.pos, bf16[1024,512]{1,0:T(8,128)(2,1)} %copy-done.4, bf16[64,5376]{1,0:T(8,128)(2,1)S(1)} %reshape.31.own, bf16[64,5376]{1,0:T(8,128)(2,1)} %collective-permute-done.own2, bf16[64,5376]{1,0:T(8,128)(2,1)S(1)} %collective-permute-done.1.left, ...), custom_call_target="tpu_custom_call" | custom-call | flops 5637144576 | bytes 16515072 | tf_op jit(solution)/shard_map/pallas_call | solution.py:423
  180.2 1.9 %reduce_sum.12 = bf16[64,336]{1,0:T(8,128)(2,1)} reduce(bf16[16,64,336]{2,1,0:T(8,128)(2,1)} %all-to-all-done.3, bf16[]{:T(256)} %constant.32.clone.1), dimensions={0}, to_apply=%region_0.1 | reduce | flops 322560 | bytes 731138 | tf_op jit(solution)/shard_map/reduce_sum | solution.py:492
  (53 shorter events, 7.3 us)
Async XLA Ops:
  23.3 24.9 %copy-start.2 = (f32[4,256]{1,0:T(4,128)S(1)}, f32[4,256]{1,0:T(4,128)}, u32[]{:S(2)}) copy-start(f32[4,256]{1,0:T(4,128)} %logits_ref.1) | copy-start | bytes 12292
  23.3 24.9 %copy-start.3 = (s32[4,256]{1,0:T(4,128)S(1)}, s32[4,256]{1,0:T(4,128)}, u32[]{:S(2)}) copy-start(s32[4,256]{1,0:T(4,128)} %ids_ref.1) | copy-start | bytes 12292
  24.2 17.7 %collective-permute-start.3 = (bf16[64,5376]{1,0:T(8,128)(2,1)S(1)}, bf16[64,5376]{1,0:T(8,128)(2,1)S(1)}, u32[]{:S(2)}, u32[]{:S(2)}) collective-permute-start(bf16[64,5376]{1,0:T(8,128)(2,1)S(1)} %reshape.31.own), channel_id=1, source_target_pairs={{0,96},{16,112},{32,0},{48,16},{64,32},{80,48},{96,64},{112,80},{1... | collective-permute-start | bytes 2064392 | tf_op jit(solution)/shard_map/ppermute | solution.py:445
  28.3 17.0 %collective-permute-start.1 = (bf16[64,5376]{1,0:T(8,128)(2,1)S(1)}, bf16[64,5376]{1,0:T(8,128)(2,1)S(1)}, u32[]{:S(2)}, u32[]{:S(2)}) collective-permute-start(bf16[64,5376]{1,0:T(8,128)(2,1)S(1)} %reshape.31.own), channel_id=1, source_target_pairs={{0,32},{16,48},{32,64},{48,80},{64,96},{80,112},{96,0},{112,16},{1... | collective-permute-start | bytes 2064392 | tf_op jit(solution)/shard_map/ppermute | solution.py:445
  28.3 36.9 %collective-permute-start = (bf16[64,5376]{1,0:T(8,128)(2,1)S(1)}, bf16[64,5376]{1,0:T(8,128)(2,1)}, u32[]{:S(2)}, u32[]{:S(2)}) collective-permute-start(bf16[64,5376]{1,0:T(8,128)(2,1)S(1)} %reshape.31.own), channel_id=1, source_target_pairs={{0,16},{16,0},{32,48},{48,32},{64,80},{80,64},{96,112},{112,96},{1... | collective-permute-start | bytes 2064392 | tf_op jit(solution)/shard_map/ppermute | solution.py:445
  41.8 37.1 %copy-start.1 = (bf16[64,5376]{1,0:T(8,128)(2,1)}, bf16[64,5376]{1,0:T(8,128)(2,1)S(1)}, u32[]{:S(2)}) copy-start(bf16[64,5376]{1,0:T(8,128)(2,1)S(1)} %collective-permute-done.3.right) | copy-start | bytes 2064388
  41.8 23.3 %collective-permute-start.4 = (bf16[64,5376]{1,0:T(8,128)(2,1)S(1)}, bf16[64,5376]{1,0:T(8,128)(2,1)}, u32[]{:S(2)}, u32[]{:S(2)}) collective-permute-start(bf16[64,5376]{1,0:T(8,128)(2,1)S(1)} %collective-permute-done.3.right), channel_id=1, source_target_pairs={{0,16},{16,0},{32,48},{48,32},{64,80},{80,64},{96,112},{112,96},{1... | collective-permute-start | bytes 2064392 | tf_op jit(solution)/shard_map/ppermute | solution.py:445
  45.2 19.9 %collective-permute-start.2 = (bf16[64,5376]{1,0:T(8,128)(2,1)S(1)}, bf16[64,5376]{1,0:T(8,128)(2,1)}, u32[]{:S(2)}, u32[]{:S(2)}) collective-permute-start(bf16[64,5376]{1,0:T(8,128)(2,1)S(1)} %collective-permute-done.1.left), channel_id=1, source_target_pairs={{0,16},{16,0},{32,48},{48,32},{64,80},{80,64},{96,112},{112,96},{1... | collective-permute-start | bytes 2064392 | tf_op jit(solution)/shard_map/ppermute | solution.py:445
  46.0 10.7 %collective-permute-start.6 = (bf16[32,5376]{1,0:T(8,128)(2,1)}, bf16[32,5376]{1,0:T(8,128)(2,1)S(1)}, u32[]{:S(2)}, u32[]{:S(2)}) collective-permute-start(bf16[32,5376]{1,0:T(8,128)(2,1)} %slice.81), channel_id=1, source_target_pairs={{0,96},{16,112},{32,0},{48,16},{64,32},{80,48},{96,64},{112,80},{1... | collective-permute-start | bytes 1032200 | tf_op jit(solution)/shard_map/ppermute | solution.py:445
  46.8 11.1 %collective-permute-start.5 = (bf16[32,5376]{1,0:T(8,128)(2,1)S(1)}, bf16[32,5376]{1,0:T(8,128)(2,1)S(1)}, u32[]{:S(2)}, u32[]{:S(2)}) collective-permute-start(bf16[32,5376]{1,0:T(8,128)(2,1)S(1)} %slice.80), channel_id=1, source_target_pairs={{0,32},{16,48},{32,64},{48,80},{64,96},{80,112},{96,0},{112,16},{1... | collective-permute-start | bytes 1032200 | tf_op jit(solution)/shard_map/ppermute | solution.py:445
  50.1 15.1 %all-to-all-start.1 = ((f32[128,1,64]{2,1,0:T(1,128)}), f32[128,1,64]{2,1,0:T(1,128)S(1)}, u32[]{:S(2)}, u32[]{:S(2)}) async-start(f32[128,1,64]{2,1,0:T(1,128)} %bitcast.4), calls=%async_computation.1 | async-start | bytes 131072 | tf_op jit(solution)/shard_map/all_to_all | solution.py:459
  56.7 22.2 %collective-permute-start.8 = (bf16[32,5376]{1,0:T(8,128)(2,1)S(1)}, bf16[32,5376]{1,0:T(8,128)(2,1)S(1)}, u32[]{:S(2)}, u32[]{:S(2)}) collective-permute-start(bf16[32,5376]{1,0:T(8,128)(2,1)S(1)} %collective-permute-done.6.far_b), channel_id=1, source_target_pairs={{0,16},{16,0},{32,48},{48,32},{64,80},{80,64},{96,112},{112,96},{1... | collective-permute-start | bytes 1032200 | tf_op jit(solution)/shard_map/ppermute | solution.py:445
  57.9 21.1 %collective-permute-start.7 = (bf16[32,5376]{1,0:T(8,128)(2,1)S(1)}, bf16[32,5376]{1,0:T(8,128)(2,1)S(1)}, u32[]{:S(2)}, u32[]{:S(2)}) collective-permute-start(bf16[32,5376]{1,0:T(8,128)(2,1)S(1)} %collective-permute-done.5.far_a), channel_id=1, source_target_pairs={{0,16},{16,0},{32,48},{48,32},{64,80},{80,64},{96,112},{112,96},{1... | collective-permute-start | bytes 1032200 | tf_op jit(solution)/shard_map/ppermute | solution.py:445
  103.4 8.5 %copy-start = (f32[3,1024,128]{2,1,0:T(8,128)S(1)}, f32[3,1024,128]{2,1,0:T(8,128)}, u32[]{:S(2)}) copy-start(f32[3,1024,128]{2,1,0:T(8,128)} %get-tuple-element.26.logits) | copy-start | bytes 4718596
  111.8 14.8 %collective-permute-start.11 = (bf16[64,5376]{1,0:T(8,128)(2,1)S(1)}, bf16[64,5376]{1,0:T(8,128)(2,1)S(1)}, u32[]{:S(2)}, u32[]{:S(2)}) collective-permute-start(bf16[64,5376]{1,0:T(8,128)(2,1)S(1)} %get-tuple-element.34), channel_id=1, source_target_pairs={{0,16},{16,0},{32,48},{48,32},{64,80},{80,64},{96,112},{112,96},{1... | collective-permute-start | bytes 2064392 | tf_op jit(solution)/shard_map/ppermute | solution.py:445
  114.0 1.0 copy-start.4
  126.1 16.4 %collective-permute-start.9 = (bf16[64,5376]{1,0:T(8,128)(2,1)S(1)}, bf16[64,5376]{1,0:T(8,128)(2,1)S(1)}, u32[]{:S(2)}, u32[]{:S(2)}) collective-permute-start(bf16[64,5376]{1,0:T(8,128)(2,1)S(1)} %get-tuple-element.31), channel_id=1, source_target_pairs={{0,16},{16,0},{32,48},{48,32},{64,80},{80,64},{96,112},{112,96},{1... | collective-permute-start | bytes 2064392 | tf_op jit(solution)/shard_map/ppermute | solution.py:445
  126.6 3.7 %collective-permute-start.10 = (bf16[2,64,5376]{2,1,0:T(8,128)(2,1)S(1)}, bf16[2,64,5376]{2,1,0:T(8,128)(2,1)S(1)}, u32[]{:S(2)}, u32[]{:S(2)}) collective-permute-start(bf16[2,64,5376]{2,1,0:T(8,128)(2,1)S(1)} %get-tuple-element.32), channel_id=1, source_target_pairs={{0,16},{16,0},{32,48},{48,32},{64,80},{80,64},{96,112},{112,96},{1... | collective-permute-start | bytes 4128776 | tf_op jit(solution)/shard_map/ppermute | solution.py:445
  126.6 3.7 %copy-start.5 = (f32[3,64,5376]{2,1,0:T(8,128)S(1)}, f32[3,64,5376]{2,1,0:T(8,128)}, u32[]{:S(2)}) copy-start(f32[3,64,5376]{2,1,0:T(8,128)} %get-tuple-element.30) | copy-start | bytes 12386308
  126.8 15.6 %collective-permute-start.12 = (bf16[32,5376]{1,0:T(8,128)(2,1)S(1)}, bf16[32,5376]{1,0:T(8,128)(2,1)S(1)}, u32[]{:S(2)}, u32[]{:S(2)}) collective-permute-start(bf16[32,5376]{1,0:T(8,128)(2,1)S(1)} %get-tuple-element.40), channel_id=1, source_target_pairs={{0,32},{16,48},{32,64},{48,80},{64,96},{80,112},{96,0},{112,16},{1... | collective-permute-start | bytes 1032200 | tf_op jit(solution)/shard_map/ppermute | solution.py:445
  127.7 10.9 %collective-permute-start.16 = (bf16[32,5376]{1,0:T(8,128)(2,1)S(1)}, bf16[32,5376]{1,0:T(8,128)(2,1)S(1)}, u32[]{:S(2)}, u32[]{:S(2)}) collective-permute-start(bf16[32,5376]{1,0:T(8,128)(2,1)S(1)} %get-tuple-element.41), channel_id=1, source_target_pairs={{0,96},{16,112},{32,0},{48,16},{64,32},{80,48},{96,64},{112,80},{1... | collective-permute-start | bytes 1032200 | tf_op jit(solution)/shard_map/ppermute | solution.py:445
  130.6 15.4 %collective-permute-start.14 = (bf16[32,5376]{1,0:T(8,128)(2,1)S(1)}, bf16[32,5376]{1,0:T(8,128)(2,1)S(1)}, u32[]{:S(2)}, u32[]{:S(2)}) collective-permute-start(bf16[32,5376]{1,0:T(8,128)(2,1)S(1)} %fusion.8), channel_id=1, source_target_pairs={{0,96},{16,112},{32,0},{48,16},{64,32},{80,48},{96,64},{112,80},{1... | collective-permute-start | bytes 1032200 | tf_op jit(solution)/shard_map/ppermute | solution.py:445
  138.7 14.0 %collective-permute-start.17 = (bf16[32,5376]{1,0:T(8,128)(2,1)S(1)}, bf16[32,5376]{1,0:T(8,128)(2,1)S(1)}, u32[]{:S(2)}, u32[]{:S(2)}) collective-permute-start(bf16[32,5376]{1,0:T(8,128)(2,1)S(1)} %fusion.1), channel_id=1, source_target_pairs={{0,96},{16,112},{32,0},{48,16},{64,32},{80,48},{96,64},{112,80},{1... | collective-permute-start | bytes 1032200 | tf_op jit(solution)/shard_map/ppermute | solution.py:445
  142.4 12.2 %collective-permute-start.15 = (bf16[32,5376]{1,0:T(8,128)(2,1)S(1)}, bf16[32,5376]{1,0:T(8,128)(2,1)S(1)}, u32[]{:S(2)}, u32[]{:S(2)}) collective-permute-start(bf16[32,5376]{1,0:T(8,128)(2,1)S(1)} %fusion.9), channel_id=1, source_target_pairs={{0,32},{16,48},{32,64},{48,80},{64,96},{80,112},{96,0},{112,16},{1... | collective-permute-start | bytes 1032200 | tf_op jit(solution)/shard_map/ppermute | solution.py:445
  142.4 16.9 %collective-permute-start.13 = (bf16[32,5376]{1,0:T(8,128)(2,1)S(1)}, bf16[32,5376]{1,0:T(8,128)(2,1)S(1)}, u32[]{:S(2)}, u32[]{:S(2)}) collective-permute-start(bf16[32,5376]{1,0:T(8,128)(2,1)S(1)} %fusion.5), channel_id=1, source_target_pairs={{0,32},{16,48},{32,64},{48,80},{64,96},{80,112},{96,0},{112,16},{1... | collective-permute-start | bytes 1032200 | tf_op jit(solution)/shard_map/ppermute | solution.py:445
  163.6 16.6 %all-to-all-start.3 = ((bf16[16,64,336]{2,1,0:T(8,128)(2,1)}), bf16[16,64,336]{2,1,0:T(8,128)(2,1)}, u32[]{:S(2)}, u32[]{:S(2)}) async-start(bf16[16,64,336]{2,1,0:T(8,128)(2,1)} %maximum_bitcast_fusion), calls=%async_computation.3 | async-start | bytes 1572864 | tf_op jit(solution)/shard_map/all_to_all | solution.py:491

commit v2 on v0

v2 whole, which is shorter than its diff:
```python
import functools

import jax
import jax.numpy as jnp
from jax import lax
from jax.experimental import pallas as pl
from jax.experimental.pallas import tpu as pltpu
from jax.sharding import PartitionSpec as P

loss_scale = 64.0
SLOTS = 6
OFFSETS = (0, 3, 1, 2)
LANES = 128
COLS = 768
ANY = pl.BlockSpec(memory_space=pl.ANY)
WHOLE = pl.BlockSpec(memory_space=pltpu.VMEM)
FAR = pl.BlockSpec(memory_space=pltpu.HBM)
SCALARS = pl.BlockSpec(memory_space=pltpu.SMEM)
VMEM_LIMIT = 16 * 1024 * 1024
BOTH = ("seq", "vocab")


def params():
    return pltpu.CompilerParams(vmem_limit_bytes=VMEM_LIMIT)


def cost(flops, nbytes):
    return pl.CostEstimate(flops=int(flops), bytes_accessed=int(nbytes), transcendentals=0)


def teacher_kernel(owners, vocab_rows, logits_ref, ids_ref, out_ref):
    rows, width = logits_ref.shape
    scores = logits_ref[...]
    expo = jnp.exp(scores - jnp.max(scores, axis=1, keepdims=True))
    prob = expo / jnp.sum(expo, axis=1, keepdims=True)
    ids = ids_ref[...]
    shift = vocab_rows.bit_length() - 1
    owner_iota = lax.broadcasted_iota(jnp.int32, (owners, width), 0)
    slot_iota = lax.broadcasted_iota(jnp.int32, (owners, width), 1)
    lane = lax.broadcasted_iota(jnp.int32, (owners, rows * 16), 1)
    out = jnp.zeros((owners, rows * 16), jnp.float32)
    for row in range(rows):
        row_ids = jnp.broadcast_to(ids[row : row + 1, :], (owners, width))
        row_prob = jnp.broadcast_to(prob[row : row + 1, :], (owners, width))
        owner = lax.shift_right_logical(row_ids, shift)
        start = jnp.sum((owner < owner_iota).astype(jnp.int32), axis=1, keepdims=True)
        place = jnp.where(owner == owner_iota, slot_iota - start, -1)
        local = (row_ids - owner * vocab_rows + 1).astype(jnp.float32)
        for slot in range(SLOTS):
            hit = place == slot
            value = jnp.sum(jnp.where(hit, row_prob, 0.0), axis=1, keepdims=True)
            index = jnp.sum(jnp.where(hit, local, 0.0), axis=1, keepdims=True) - 1.0
            out = out + jnp.where(lane == row * 16 + slot, value, 0.0)
            out = out + jnp.where(lane == row * 16 + 8 + slot, index, 0.0)
    out_ref[...] = out


def teacher_rows(owners, vocab_rows, teacher_logits, teacher_ids):
    rows = teacher_logits.shape[0]
    return pl.pallas_call(
        functools.partial(teacher_kernel, owners, vocab_rows),
        out_shape=jax.ShapeDtypeStruct((owners, rows * 16), jnp.float32),
        compiler_params=params(),
        cost_estimate=cost(4e6, 40000),
    )(teacher_logits, teacher_ids)


def dot_nt(a, b):
    return lax.dot_general(a, b, (((1,), (1,)), ((), ())), preferred_element_type=jnp.float32)


def local_stats(logits, target):
    peak = jnp.max(logits, axis=0, keepdims=True)
    expo = jnp.exp(logits - peak)
    total = jnp.sum(expo, axis=0, keepdims=True)
    mean = jnp.sum(expo * logits, axis=0, keepdims=True) / total
    cross = jnp.sum(target * logits, axis=0, keepdims=True)
    lse = peak + jnp.log(total)
    row = lax.broadcasted_iota(jnp.int32, (8, LANES), 0)
    return jnp.where(row == 0, lse, jnp.where(row == 1, mean, jnp.where(row == 2, cross, 0.0)))


def load_blocks(pieces, dest, sems):
    copies = [
        pltpu.make_async_copy(src, dest.at[pl.ds(pl.multiple_of(row, 32), src.shape[0])], sems.at[k])
        for k, (src, row) in enumerate(pieces)
    ]
    for copy in copies:
        copy.start()
    return copies


def first_kernel(pos, got, source, own, own2, left, left2, right, right2, w, out, target, stats, held, teach, sems):
    z, core = pos[0], pos[1]
    count = sems.shape[0]
    chunk = source.shape[0] // count
    copies = [
        pltpu.make_async_copy(source.at[pl.ds(k * chunk, chunk)], w.at[pl.ds(k * chunk, chunk)], sems.at[k])
        for k in range(count)
    ]
    for copy in copies:
        copy.start()
    for slot, mine, other in ((0, own, own2), (1, left, left2), (2, right, right2)):
        held[pl.ds(pl.multiple_of(slot * 128 + core * 64, 64), 64)] = mine[...]
        held[pl.ds(pl.multiple_of(slot * 128 + (1 - core) * 64, 64), 64)] = other[...]
    flipped = got[...].T
    source_row = lax.broadcasted_iota(jnp.int32, (LANES, 4 * LANES), 0)
    token = lax.broadcasted_iota(jnp.int32, (LANES, 4 * LANES), 1)
    spread = jnp.zeros((16, 4 * LANES), jnp.float32)
    for row in range(4):
        pick = (token == source_row * 4 + row).astype(jnp.float32)
        spread = spread + jnp.dot(
            flipped[row * 16 : row * 16 + 16], pick,
            precision=lax.Precision.HIGHEST, preferred_element_type=jnp.float32,
        )
    for block in range(4):
        teach[block] = spread[:, block * LANES : (block + 1) * LANES]
    rows = 64

    @pl.loop(0, w.shape[0] // rows)
    def _(step):
        base = pl.multiple_of(step * rows, rows)
        word = (lax.broadcasted_iota(jnp.int32, (rows, LANES), 0) + step * rows).astype(jnp.float32)
        for slot in range(4):
            info = teach[(z + OFFSETS[slot]) % 4]
            dense = jnp.zeros((rows, LANES), jnp.float32)
            for k in range(SLOTS):
                dense = dense + jnp.where(word == info[8 + k : 9 + k], info[k : k + 1], 0.0)
            target[slot, pl.ds(base, rows)] = dense

    for k in range(count):
        copies[k].wait()
        at = slice(k * chunk, (k + 1) * chunk)
        logits = dot_nt(w[at], held[...])
        for slot in range(3):
            out[slot, at] = logits[:, slot * LANES : (slot + 1) * LANES]
    for slot in range(3):
        stats[slot] = local_stats(out[slot], target[slot])


def first_logits(pos, got, source, blocks):
    vocab, width = source.shape
    return pl.pallas_call(
        first_kernel,
        in_specs=[SCALARS, WHOLE, FAR] + [WHOLE] * 6,
        out_specs=[WHOLE] * 5,
        out_shape=[
            pltpu.VMEM((vocab, width), jnp.bfloat16),
            jax.ShapeDtypeStruct((3, vocab, LANES), jnp.float32),
            jax.ShapeDtypeStruct((4, vocab, LANES), jnp.float32),
            jax.ShapeDtypeStruct((3, 8, LANES), jnp.float32),
            jax.ShapeDtypeStruct((3 * LANES, width), jnp.bfloat16),
        ],
        scratch_shapes=[pltpu.VMEM((4, 16, LANES), jnp.float32), pltpu.SemaphoreType.DMA((2,))],
        compiler_params=params(),
        cost_estimate=cost(1000, 1000),
    )(pos, got, pltpu.with_memory_space_constraint(source, pltpu.HBM), *blocks)


def last_kernel(pos, w, target, early, far_a, far_b, far_a2, far_b2, out, send, held, table, sems):
    z, core = pos[0], pos[1]
    mine, other = core * 64, (1 - core) * 64
    copies = load_blocks(
        [(far_a, mine), (far_b, mine + 32), (far_a2, other), (far_b2, other + 32)], held, sems
    )
    for copy in copies:
        copy.wait()
    out[...] = dot_nt(w[...], held[...])
    for slot in range(3):
        table[(z + OFFSETS[slot]) % 4] = early[slot]
    table[(z + OFFSETS[3]) % 4] = local_stats(out[...], target[3])
    lane = lax.broadcasted_iota(jnp.int32, (32, LANES), 1)
    row = lax.broadcasted_iota(jnp.int32, (32, LANES), 0)
    for block in range(4):
        info = table[block]
        send[:, block * LANES : (block + 1) * LANES] = jnp.broadcast_to(info[0:1], (LANES, LANES))
        extra = jnp.zeros((32, LANES), jnp.float32)
        for kind in range(3):
            for token in range(4):
                value = jnp.sum(
                    jnp.where(lane == row * 4 + token, info[kind : kind + 1], 0.0), axis=1, keepdims=True
                )
                extra = extra + jnp.where(lane == kind * 4 + token, value, 0.0)
        send[block * 32 : (block + 1) * 32, 4 * LANES : 5 * LANES] = extra


def last_logits(pos, w, target, early, blocks):
    vocab, width = w.shape
    return pl.pallas_call(
        last_kernel,
        in_specs=[SCALARS] + [WHOLE] * 3 + [ANY] * 4,
        out_specs=[WHOLE] * 3,
        out_shape=[
            jax.ShapeDtypeStruct((vocab, LANES), jnp.float32),
            jax.ShapeDtypeStruct((LANES, 5 * LANES), jnp.float32),
            jax.ShapeDtypeStruct((LANES, width), jnp.bfloat16),
        ],
        scratch_shapes=[pltpu.VMEM((4, 8, LANES), jnp.float32), pltpu.SemaphoreType.DMA((4,))],
        compiler_params=params(),
        cost_estimate=cost(2 * vocab * width * 128, vocab * width * 2),
    )(pos, w, target, early, *blocks)


def grad_of(logits, lse, target):
    return loss_scale * (jnp.exp(logits - lse) - target)


def split_rows(pos, acc, at, base, mine_out, other_out):
    core = pos[1]
    mine_out[:, at] = acc[pl.ds(pl.multiple_of(base + core * 64, 64), 64)]
    other_out[:, at] = acc[pl.ds(pl.multiple_of(base + (1 - core) * 64, 64), 64)].astype(jnp.bfloat16)


def far_grad_kernel(pos, stats, logits, target, w, mine_out, other_out, grad_out, lse_out, loss_out, acc):
    z = pos[0]
    parts = stats[:, : 4 * LANES]
    peak = jnp.max(parts, axis=0, keepdims=True)
    lse = peak + jnp.log(jnp.sum(jnp.exp(parts - peak), axis=0, keepdims=True))
    for block in range(4):
        lse_out[block] = jnp.broadcast_to(lse[:, block * LANES : (block + 1) * LANES], (8, LANES))
    few = stats[:, 4 * LANES :]
    peak = jnp.max(few, axis=0, keepdims=True)
    weight = jnp.exp(few - peak)
    total = jnp.sum(weight, axis=0, keepdims=True)
    mean = jnp.sum(weight * pltpu.roll(few, LANES - 4, 1), axis=0, keepdims=True) / total
    cross = jnp.sum(pltpu.roll(few, LANES - 8, 1), axis=0, keepdims=True)
    lse4 = peak + jnp.log(total)
    row = lax.broadcasted_iota(jnp.int32, (8, LANES), 0)
    loss_out[...] = jnp.where(row == 0, lse4 - cross, lse4 - mean)
    far = lse_out[(z + OFFSETS[3]) % 4]
    grad = grad_of(logits[...], far[0:1], target[3])
    grad_out[...] = grad.astype(jnp.bfloat16)
    left = grad.T.astype(jnp.bfloat16)
    for tile in range(w.shape[1] // COLS):
        at = slice(tile * COLS, (tile + 1) * COLS)
        acc[...] = jnp.dot(left, w[:, at], preferred_element_type=jnp.float32)
        split_rows(pos, acc, at, 0, mine_out, other_out)


def far_grad(pos, stats, logits, target, w):
    vocab, width = w.shape
    return pl.pallas_call(
        far_grad_kernel,
        in_specs=[SCALARS] + [WHOLE] * 4,
        out_specs=[WHOLE] * 5,
        out_shape=[
            jax.ShapeDtypeStruct((64, width), jnp.float32),
            jax.ShapeDtypeStruct((64, width), jnp.bfloat16),
            jax.ShapeDtypeStruct((vocab, LANES), jnp.bfloat16),
            jax.ShapeDtypeStruct((4, 8, LANES), jnp.float32),
            jax.ShapeDtypeStruct((8, LANES), jnp.float32),
        ],
        scratch_shapes=[pltpu.VMEM((LANES, COLS), jnp.float32)],
        compiler_params=params(),
        cost_estimate=cost(2 * vocab * width * 128, vocab * width * 2),
    )(pos, stats, logits, target, w)


def grads_kernel(pos, logits, target, lse, far, wide_out, left_out):
    z = pos[0]
    for slot in range(3):
        row = lse[(z + OFFSETS[slot]) % 4]
        grad = grad_of(logits[slot], row[0:1], target[slot])
        wide_out[:, slot * LANES : (slot + 1) * LANES] = grad.astype(jnp.bfloat16)
        left_out[slot * LANES : (slot + 1) * LANES, :] = grad.T.astype(jnp.bfloat16)
    wide_out[:, 3 * LANES :] = far[...]


def near_grads(pos, logits, target, lse, far):
    vocab = far.shape[0]
    return pl.pallas_call(
        grads_kernel,
        in_specs=[SCALARS] + [WHOLE] * 4,
        out_specs=[WHOLE] * 2,
        out_shape=[
            jax.ShapeDtypeStruct((vocab, 4 * LANES), jnp.bfloat16),
            jax.ShapeDtypeStruct((3 * LANES, vocab), jnp.bfloat16),
        ],
        compiler_params=params(),
        cost_estimate=cost(2e6, 5e6),
    )(pos, logits, target, lse, far)


def near_kernel(pos, left, w, mine_out, other_out, acc):
    core = pos[1]
    for tile in range(w.shape[1] // COLS):
        at = slice(tile * COLS, (tile + 1) * COLS)
        acc[...] = jnp.dot(left[...], w[:, at], preferred_element_type=jnp.float32)
        for slot in range(3):
            to = slice(slot * 64, (slot + 1) * 64)
            mine_out[to, at] = acc[pl.ds(pl.multiple_of(slot * 128 + core * 64, 64), 64)]
            part = acc[pl.ds(pl.multiple_of(slot * 128 + (1 - core) * 64, 64), 64)]
            other_out[to, at] = part.astype(jnp.bfloat16)


def near_grad(pos, left, w):
    vocab, width = w.shape
    tokens = left.shape[0]
    return pl.pallas_call(
        near_kernel,
        in_specs=[SCALARS] + [WHOLE] * 2,
        out_specs=[WHOLE] * 2,
        out_shape=[
            jax.ShapeDtypeStruct((tokens // 2, width), jnp.float32),
            jax.ShapeDtypeStruct((tokens // 2, width), jnp.bfloat16),
        ],
        scratch_shapes=[pltpu.VMEM((tokens, COLS), jnp.float32)],
        compiler_params=params(),
        cost_estimate=cost(2 * vocab * width * tokens, vocab * width * 2),
    )(pos, left, w)


def weight_kernel(grad, near, far, out):
    for tile in range(out.shape[1] // COLS):
        at = slice(tile * COLS, (tile + 1) * COLS)
        held = jnp.concatenate([near[:, at], far[:, at]], axis=0)
        out[:, at] = jnp.dot(grad[...], held, preferred_element_type=jnp.float32).astype(jnp.bfloat16)


def weight_grad(grad, near, far):
    vocab, tokens = grad.shape
    width = near.shape[1]
    rows = 256
    return pl.pallas_call(
        weight_kernel,
        grid=(vocab // rows,),
        in_specs=[pl.BlockSpec((rows, tokens), lambda i: (i, 0)), WHOLE, WHOLE],
        out_specs=pl.BlockSpec((rows, width), lambda i: (i, 0)),
        out_shape=jax.ShapeDtypeStruct((vocab, width), jnp.bfloat16),
        compiler_params=params(),
        cost_estimate=cost(2 * vocab * width * tokens, vocab * width * 2 + tokens * width * 2),
    )(grad, near, far)


def widen_kernel(upper, lower, out):
    out[0] = upper[...].astype(jnp.float32)
    out[1] = lower[...].astype(jnp.float32)


def widen(upper, lower):
    return pl.pallas_call(
        widen_kernel,
        in_specs=[WHOLE] * 2,
        out_specs=WHOLE,
        out_shape=jax.ShapeDtypeStruct((2, *upper.shape), jnp.float32),
        compiler_params=params(),
        cost_estimate=cost(1e11, 1e9),
    )(upper, lower)


def fold_kernel(near, from_left, from_right, out, total):
    rows = from_left.shape[0]
    total[...] = near[:rows] + from_left[...].astype(jnp.float32) + from_right[...].astype(jnp.float32)
    part = out.shape[2]
    for index in range(out.shape[0]):
        out[index] = total[:, index * part : (index + 1) * part].astype(jnp.bfloat16)


def fold(count, pieces):
    rows, width = pieces[1].shape
    return pl.pallas_call(
        fold_kernel,
        in_specs=[WHOLE] * 3,
        out_specs=WHOLE,
        out_shape=jax.ShapeDtypeStruct((count, rows, width // count), jnp.bfloat16),
        scratch_shapes=[pltpu.VMEM((rows, width), jnp.float32)],
        compiler_params=params(),
        cost_estimate=cost(2e6, 4e6),
    )(*pieces)


def sum_kernel(parts, out):
    total = parts[0].astype(jnp.float32)
    for index in range(1, parts.shape[0]):
        total = total + parts[index].astype(jnp.float32)
    out[...] = total.astype(jnp.bfloat16)


def sum_parts(parts):
    return pl.pallas_call(
        sum_kernel,
        in_specs=[WHOLE],
        out_specs=WHOLE,
        out_shape=jax.ShapeDtypeStruct(parts.shape[1:], jnp.bfloat16),
        compiler_params=params(),
        cost_estimate=cost(4e5, 8e5),
    )(parts)


def body(hidden, head_weight, teacher_logits, teacher_ids):
    seq_count = lax.axis_size("seq")
    vocab_count = lax.axis_size("vocab")
    owners = seq_count * vocab_count
    vocab_rows, width = head_weight.shape
    tok_rows, feat_part = hidden.shape
    seq_index = lax.axis_index("seq")
    pos = jnp.stack([seq_index // 2, seq_index % 2]).astype(jnp.int32)
    up = [(i, (i + 2) % seq_count) for i in range(seq_count)]
    down = [(i, (i - 2) % seq_count) for i in range(seq_count)]
    twin = [(i, i ^ 1) for i in range(seq_count)]

    def move(x, perm):
        return lax.ppermute(x, "seq", perm)

    def after(x, *before):
        return lax.optimization_barrier((x, before))[0]

    f32 = jnp.float32
    bf16 = jnp.bfloat16
    half = tok_rows // 2

    spread = jnp.broadcast_to(hidden[None], (vocab_count, tok_rows, feat_part))
    spread = lax.all_to_all(spread, "vocab", split_axis=0, concat_axis=0, tiled=True)
    teach = teacher_rows(owners, vocab_rows, teacher_logits, teacher_ids)
    spread, (teach, pos) = lax.optimization_barrier((spread, (teach, pos)))
    own = spread.transpose(1, 0, 2).reshape(tok_rows, width)
    left = move(own, up)
    right = move(own, down)
    own2 = move(own, twin)
    teach = after(teach, own)
    got = lax.all_to_all(teach, BOTH, split_axis=0, concat_axis=0, tiled=True)
    left, right = after((left, right), got)
    far_a = move(left[:half], up)
    far_b = move(right[half:], down)
    near_blocks = (own, own2, left, move(left, twin), right, move(right, twin))
    weight, logits, target, early, near_rows = first_logits(pos, got, head_weight, near_blocks)
    far_a, far_b = after((far_a, far_b), early)
    far_blocks = (far_a, far_b, move(far_a, twin), move(far_b, twin))
    far_logits, send, far_rows = last_logits(pos, weight, target, early, far_blocks)
    stats = lax.all_to_all(send, BOTH, split_axis=0, concat_axis=0, tiled=True)

    far_mine, far_other, grad_far, lse, loss = far_grad(pos, stats, far_logits, target, weight)
    far_swap = move(far_other, twin)
    wide, near_left = near_grads(pos, logits, target, lse, grad_far)
    far_sum = (far_mine + far_swap.astype(f32)).astype(bf16)
    go_up = move(far_sum[:half], up)
    go_down = move(far_sum[half:], down)
    near_left = after(near_left, far_sum)
    mine, other = near_grad(pos, near_left, weight)
    swap = move(other, twin)
    passed = widen(go_up, go_down)
    swap = after(swap, passed)
    near_sum = mine + swap.astype(f32)
    to_right = near_sum[2 * tok_rows :]
    to_right = jnp.concatenate([to_right[:half] + passed[0], to_right[half:]]).astype(bf16)
    to_left = near_sum[tok_rows : 2 * tok_rows]
    to_left = jnp.concatenate([to_left[:half], to_left[half:] + passed[1]]).astype(bf16)
    from_left = move(to_right, up)
    from_right = move(to_left, down)
    grad_weight = weight_grad(wide, near_rows, far_rows)
    parts = fold(vocab_count, (near_sum, from_left, from_right))
    parts = lax.all_to_all(parts, "vocab", split_axis=0, concat_axis=0, tiled=True)
    grad_hidden = sum_parts(parts)
    rows = teacher_logits.shape[0]
    return loss[0, :rows], loss[1, :rows], grad_hidden, grad_weight


def solution(mesh):
    placed = (
        P("seq", "vocab"),
        P(("seq", "vocab"), None),
        P(("seq", "vocab"), None),
        P(("seq", "vocab"), None),
    )
    return jax.shard_map(
        body,
        mesh=mesh,
        in_specs=placed,
        out_specs=(
            P(("seq", "vocab")),
            P(("seq", "vocab")),
            P("seq", "vocab"),
            P(("seq", "vocab"), None),
        ),
        check_vma=False,
    )
```

time: 496 us -> 141 us (0.28)
  waiting for transfers between devices: 222 us -> 49 us
  blocking collectives: 150 us -> 16.5 us
  local copies, waits for them, and re-layouts: 51.1 us -> 8.31 us
  matrix products: 36.7 us -> 0 us
  Pallas kernels: 0 us -> 34.9 us
  starting transfers between devices: 13.7 us -> 29.7 us
  between operations: 14.3 us -> 0.9 us
  other arithmetic: 7.71 us -> 0.82 us
    reduce_scatter x1 -> x0, waiting for transfers between devices: 206 us -> none  [body(): lax.psum_scatter(block_order, ('seq', 'vocab'), scatter_dimension=0, tile...]
    psum x1 -> x0, blocking collectives: 62.7 us -> none  [body(): lax.psum((jnp.sum(expo, axis=1), jnp.sum(expo * logits, axis=1), cross_pa...]
    pmax x1 -> x0, blocking collectives: 62.7 us -> none  [body(): peak_val = lax.pmax(jnp.max(logits, axis=1), ('seq', 'vocab'))]
    dot_general x3 -> x0, matrix products: 36.7 us -> none  [the longest x1 13.5 us: body(): jnp.dot(grad_logits, head_weight, preferred_element_type=jnp.float32)]
    pallas_call x0 -> x10, Pallas kernels: none -> 34.9 us  [the longest x1 9.59 us: first_logits(): pl.pallas_call(first_kernel, in_specs=[SCALARS, WHOLE, FAR] + [WHOLE] * 6...]
    all_gather x1 -> x0, blocking collectives: 24.7 us -> none  [body(): features = lax.all_gather(hidden, 'vocab', axis=1, tiled=True)]
    ppermute x0 -> x15, waiting for transfers between devices: none -> 22.5 us  [move(): return lax.ppermute(x, 'seq', perm)]
    all_to_all x0 -> x1, blocking collectives: none -> 16.5 us  [body(): stats = lax.all_to_all(send, BOTH, split_axis=0, concat_axis=0, tiled=True)]
  transfers between devices with their start and end apart: 4 -> 18, of which waited for: 3 -> 10; matrix products, arithmetic and copies ran while one was open for 7% -> 0% of each run, Pallas kernels for 0% -> 19%
where the time goes in v2:
time: 141 us; the launch traced here: 140 us
  waiting for transfers between devices  49 us (35%)
  Pallas kernels  34.9 us (25%)
  starting transfers between devices  29.7 us (21%)
  blocking collectives  16.5 us (12%)
  local copies, waits for them, and re-layouts  8.31 us (6%)
    ppermute x15, waiting for transfers between devices, move(): return lax.ppermute(x, 'seq', perm)  22.5 us
    all_to_all x1, blocking collectives, body(): stats = lax.all_to_all(send, BOTH, split_axis=0, concat_axis=0, tiled=True)  16.5 us
    ppermute x15, starting transfers between devices, move(): return lax.ppermute(x, 'seq', perm)  13 us
    all_to_all x1, waiting for transfers between devices, body(): lax.all_to_all(spread, 'vocab', split_axis=0, concat_axis=0, tiled=True)  12.4 us
    all_to_all x1, waiting for transfers between devices, body(): got = lax.all_to_all(teach, BOTH, split_axis=0, concat_axis=0, tiled=True)  11.1 us
    pallas_call x1, Pallas kernels, first_logits(): pl.pallas_call(first_kernel, in_specs=[SCALARS, WHOLE, FAR] + [WHOLE] * 6...  9.59 us
    pallas_call x1, Pallas kernels, weight_grad(): pl.pallas_call(weight_kernel, grid=(vocab // rows,), in_specs=[pl.BlockSp...  7.98 us
    all_to_all x1, starting transfers between devices, body(): lax.all_to_all(spread, 'vocab', split_axis=0, concat_axis=0, tiled=True)  7.12 us
  transfers between devices with their start and end apart: 18, of which 10 were waited for; matrix products, arithmetic and copies ran while one was open for 0% of the time, Pallas kernels for 19%

profile of v2, /device:TPU:0, one launch (start us, length us, event | category | flops | bytes accessed | tf_op | source)
XLA Modules:
  0.0 140.2 jit_solution(13334709039961814533)
XLA Ops:
  0.7 1.8 %broadcast_in_dim.2 = bf16[16,64,336]{2,1,0:T(8,128)(2,1)} broadcast(bf16[64,336]{1,0:T(8,128)(2,1)} %param.4), dimensions={1,2} | broadcast | bytes 731136 | tf_op jit(solution)/shard_map/broadcast_in_dim | solution.py:412
  2.4 7.1 %all-to-all-start = ((bf16[16,64,336]{2,1,0:T(8,128)(2,1)}), bf16[16,64,336]{2,1,0:T(8,128)(2,1)S(1)}, u32[]{:S(2)}, u32[]{:S(2)}) async-start(bf16[16,64,336]{2,1,0:T(8,128)(2,1)} %broadcast_in_dim.2), calls=%async_computation | async-start | bytes 1572864 | tf_op jit(solution)/shard_map/all_to_all | solution.py:413
  9.6 1.9 %shard_map.75 = f32[128,64]{1,0:T(8,128)} custom-call(f32[4,256]{1,0:T(4,128)S(1)} %copy-done, s32[4,256]{1,0:T(4,128)S(1)} %copy-done.1), custom_call_target="tpu_custom_call" | custom-call | flops 4000000 | bytes 40000 | tf_op jit(solution)/shard_map/pallas_call | solution.py:60
  11.6 12.4 %all-to-all-done = bf16[16,64,336]{2,1,0:T(8,128)(2,1)S(1)} async-done(((bf16[16,64,336]{2,1,0:T(8,128)(2,1)}), bf16[16,64,336]{2,1,0:T(8,128)(2,1)S(1)}, u32[]{:S(2)}, u32[]{:S(2)}) %all-to-all-start) | async-done | bytes 688160 | tf_op jit(solution)/shard_map/all_to_all | solution.py:413
  24.5 0.9 reshape.16.own
  25.4 4.1 %collective-permute-start.2 = (bf16[64,5376]{1,0:T(8,128)(2,1)S(1)}, bf16[64,5376]{1,0:T(8,128)(2,1)S(1)}, u32[]{:S(2)}, u32[]{:S(2)}) collective-permute-start(bf16[64,5376]{1,0:T(8,128)(2,1)S(1)} %reshape.16.own), channel_id=1, source_target_pairs={{0,96},{16,112},{32,0},{48,16},{64,32},{80,48},{96,64},{112,80},{1... | collective-permute-start | bytes 2064392 | tf_op jit(solution)/shard_map/ppermute | solution.py:403
  29.5 6.0 %all-to-all-start.1 = ((f32[128,1,64]{2,1,0:T(1,128)}), f32[128,1,64]{2,1,0:T(1,128)S(1)}, u32[]{:S(2)}, u32[]{:S(2)}) async-start(f32[128,1,64]{2,1,0:T(1,128)} %bitcast.4), calls=%async_computation.1 | async-start | bytes 131072 | tf_op jit(solution)/shard_map/all_to_all | solution.py:421
  35.7 11.1 %all-to-all-done.1 = f32[128,1,64]{2,1,0:T(1,128)S(1)} async-done(((f32[128,1,64]{2,1,0:T(1,128)}), f32[128,1,64]{2,1,0:T(1,128)S(1)}, u32[]{:S(2)}, u32[]{:S(2)}) %all-to-all-start.1) | async-done | bytes 32800 | tf_op jit(solution)/shard_map/all_to_all | solution.py:421
  47.7 1.7 %collective-permute-start.5 = (bf16[32,5376]{1,0:T(8,128)(2,1)S(1)}, bf16[32,5376]{1,0:T(8,128)(2,1)S(1)}, u32[]{:S(2)}, u32[]{:S(2)}) collective-permute-start(bf16[32,5376]{1,0:T(8,128)(2,1)S(1)} %slice.44), channel_id=1, source_target_pairs={{0,32},{16,48},{32,64},{48,80},{64,96},{80,112},{96,0},{112,16},{1... | collective-permute-start | bytes 1032200 | tf_op jit(solution)/shard_map/ppermute | solution.py:403
  49.9 9.6 %shard_map.76 = (bf16[1024,5376]{1,0:T(8,128)(2,1)S(1)}, f32[3,1024,128]{2,1,0:T(8,128)S(1)}, f32[4,1024,128]{2,1,0:T(8,128)S(1)}, f32[3,8,128]{2,1,0:T(8,128)S(1)}, bf16[384,5376]{1,0:T(8,128)(2,1)S(1)}) custom-call(s32[2]{0:T(128)S(1)} %pad_add_fusion.pos, f32[128,64]{1,0:T(8,128)S(1)} %bitcast.29, bf16[1024,5376]{1,0:T(8,128)(2,1)} %source.1, ...), custom_call_target="tpu_custom_call" | custom-call | flops 1000 | bytes 1000 | tf_op jit(solution)/shard_map/pallas_call | solution.py:143
  59.5 2.0 %copy-done.2 = bf16[384,5376]{1,0:T(8,128)(2,1)} copy-done((bf16[384,5376]{1,0:T(8,128)(2,1)}, bf16[384,5376]{1,0:T(8,128)(2,1)S(1)}, u32[]{:S(2)}) %copy-start.2) | copy-done | bytes 4128792
  62.0 1.1 collective-permute-done.7.far_a2
  63.1 0.5 collective-permute-done.8.far_b2
  63.6 4.6 %shard_map.77 = (f32[1024,128]{1,0:T(8,128)S(1)}, f32[128,640]{1,0:T(8,128)S(1)}, bf16[128,5376]{1,0:T(8,128)(2,1)S(1)}) custom-call(s32[2]{0:T(128)S(1)} %pad_add_fusion.pos, bf16[1024,5376]{1,0:T(8,128)(2,1)S(1)} %get-tuple-element.37.w, f32[4,1024,128]{2,1,0:T(8,128)S(1)} %get-tuple-element.38.target, f32[3,8,128]{2,1,0:T(8,128)S(1)} %get-tuple-element.39.early, ...), custom_call_target="tpu_custom_call" | custom-call | flops 1409286144 | bytes 11010048 | tf_op jit(solution)/shard_map/pallas_call | solution.py:189
  68.6 16.5 %all_to_all.32 = f32[128,1,640]{2,1,0:T(1,128)S(1)} all-to-all(f32[128,1,640]{2,1,0:T(1,128)S(1)} %copy.10), channel_id=1, replica_groups=mesh['seq'=8,'vocab'=16] {'seq','vocab'}, dimensions={0} | all-to-all | bytes 655360 | tf_op jit(solution)/shard_map/all_to_all | solution.py:430
  85.1 2.4 %shard_map.78 = (f32[64,5376]{1,0:T(8,128)S(1)}, bf16[64,5376]{1,0:T(8,128)(2,1)S(1)}, bf16[1024,128]{1,0:T(8,128)(2,1)S(1)}, f32[4,8,128]{2,1,0:T(8,128)S(1)}, f32[8,128]{1,0:T(8,128)S(1)}) custom-call(s32[2]{0:T(128)S(1)} %pad_add_fusion.pos, f32[128,640]{1,0:T(8,128)S(1)} %bitcast.27, f32[1024,128]{1,0:T(8,128)S(1)} %get-tuple-element.43.logits, ...), custom_call_target="tpu_custom_call" | custom-call | flops 1409286144 | bytes 11010048 | tf_op jit(solution)/shard_map/pallas_call | solution.py:242
  87.6 1.0 shard_map.79
  88.6 1.1 collective-permute-done.9
  89.9 1.0 collective-permute-start.12
  90.9 1.1 collective-permute-start.11
  92.0 5.4 %shard_map.80 = (f32[192,5376]{1,0:T(8,128)S(1)}, bf16[192,5376]{1,0:T(8,128)(2,1)S(1)}) custom-call(s32[2]{0:T(128)S(1)} %pad_add_fusion.pos, bf16[384,1024]{1,0:T(8,128)(2,1)S(1)} %get-tuple-element.51.left, bf16[1024,5376]{1,0:T(8,128)(2,1)S(1)} %get-tuple-element.37.w), custom_call_target="tpu_custom_call" | custom-call | flops 4227858432 | bytes 11010048 | tf_op jit(solution)/shard_map/pallas_call | solution.py:299
  97.5 2.6 %collective-permute-done.12.lower = bf16[32,5376]{1,0:T(8,128)(2,1)S(1)} collective-permute-done((bf16[32,5376]{1,0:T(8,128)(2,1)S(1)}, bf16[32,5376]{1,0:T(8,128)(2,1)S(1)}, u32[]{:S(2)}, u32[]{:S(2)}) %collective-permute-start.12) | collective-permute-done | bytes 344096 | tf_op jit(solution)/shard_map/ppermute | solution.py:403
  100.1 1.8 %collective-permute-done.11.upper = bf16[32,5376]{1,0:T(8,128)(2,1)S(1)} collective-permute-done((bf16[32,5376]{1,0:T(8,128)(2,1)S(1)}, bf16[32,5376]{1,0:T(8,128)(2,1)S(1)}, u32[]{:S(2)}, u32[]{:S(2)}) %collective-permute-start.11) | collective-permute-done | bytes 344096 | tf_op jit(solution)/shard_map/ppermute | solution.py:403
  103.2 2.9 %collective-permute-start.14 = (bf16[64,5376]{1,0:T(8,128)(2,1)S(1)}, bf16[64,5376]{1,0:T(8,128)(2,1)S(1)}, u32[]{:S(2)}, u32[]{:S(2)}) collective-permute-start(bf16[64,5376]{1,0:T(8,128)(2,1)S(1)} %pad_maximum_fusion.1), channel_id=1, source_target_pairs={{0,96},{16,112},{32,0},{48,16},{64,32},{80,48},{96,64},{112,80},{1... | collective-permute-start | bytes 2064392 | tf_op jit(solution)/shard_map/ppermute | solution.py:403
  106.1 14.9 %collective-permute-done.13.from_left = bf16[64,5376]{1,0:T(8,128)(2,1)S(1)} collective-permute-done((bf16[64,5376]{1,0:T(8,128)(2,1)S(1)}, bf16[64,5376]{1,0:T(8,128)(2,1)S(1)}, u32[]{:S(2)}, u32[]{:S(2)}) %collective-permute-start.13) | collective-permute-done | bytes 688160 | tf_op jit(solution)/shard_map/ppermute | solution.py:403
  121.0 1.3 shard_map.82
  122.2 3.6 %all-to-all-start.3 = ((bf16[16,64,336]{2,1,0:T(8,128)(2,1)}), bf16[16,64,336]{2,1,0:T(8,128)(2,1)S(1)}, u32[]{:S(2)}, u32[]{:S(2)}) async-start(bf16[16,64,336]{2,1,0:T(8,128)(2,1)} %shard_map.82), calls=%async_computation.3 | async-start | bytes 1572864 | tf_op jit(solution)/shard_map/all_to_all | solution.py:452
  125.9 0.5 slice_bitcast_fusion.2
  126.4 2.2 %copy-done.3 = bf16[384,5376]{1,0:T(8,128)(2,1)S(1)} copy-done((bf16[384,5376]{1,0:T(8,128)(2,1)S(1)}, bf16[384,5376]{1,0:T(8,128)(2,1)}, u32[]{:S(2)}) %copy-start.3) | copy-done | bytes 4128792
  128.6 8.0 %shard_map.84 = bf16[1024,5376]{1,0:T(8,128)(2,1)} custom-call(bf16[1024,512]{1,0:T(8,128)(2,1)S(1)} %copy-done.5, bf16[384,5376]{1,0:T(8,128)(2,1)S(1)} %copy-done.3, bf16[128,5376]{1,0:T(8,128)(2,1)S(1)} %get-tuple-element.57.far), custom_call_target="tpu_custom_call" | custom-call | flops 5637144576 | bytes 16515072 | tf_op jit(solution)/shard_map/pallas_call | solution.py:324
  136.5 2.9 %all-to-all-done.3.parts = bf16[16,64,336]{2,1,0:T(8,128)(2,1)S(1)} async-done(((bf16[16,64,336]{2,1,0:T(8,128)(2,1)}), bf16[16,64,336]{2,1,0:T(8,128)(2,1)S(1)}, u32[]{:S(2)}, u32[]{:S(2)}) %all-to-all-start.3) | async-done | bytes 688160 | tf_op jit(solution)/shard_map/all_to_all | solution.py:452
  139.4 0.7 shard_map.83
  (43 shorter events, 4.4 us)
Async XLA Ops:
  0.6 9.0 %copy-start.1 = (s32[4,256]{1,0:T(4,128)S(1)}, s32[4,256]{1,0:T(4,128)}, u32[]{:S(2)}) copy-start(s32[4,256]{1,0:T(4,128)} %ids_ref.1) | copy-start | bytes 12292
  0.6 9.0 %copy-start = (f32[4,256]{1,0:T(4,128)S(1)}, f32[4,256]{1,0:T(4,128)}, u32[]{:S(2)}) copy-start(f32[4,256]{1,0:T(4,128)} %logits_ref.1) | copy-start | bytes 12292
  2.4 21.6 %all-to-all-start = ((bf16[16,64,336]{2,1,0:T(8,128)(2,1)}), bf16[16,64,336]{2,1,0:T(8,128)(2,1)S(1)}, u32[]{:S(2)}, u32[]{:S(2)}) async-start(bf16[16,64,336]{2,1,0:T(8,128)(2,1)} %broadcast_in_dim.2), calls=%async_computation | async-start | bytes 1572864 | tf_op jit(solution)/shard_map/all_to_all | solution.py:413
  25.4 21.4 %collective-permute-start.2 = (bf16[64,5376]{1,0:T(8,128)(2,1)S(1)}, bf16[64,5376]{1,0:T(8,128)(2,1)S(1)}, u32[]{:S(2)}, u32[]{:S(2)}) collective-permute-start(bf16[64,5376]{1,0:T(8,128)(2,1)S(1)} %reshape.16.own), channel_id=1, source_target_pairs={{0,96},{16,112},{32,0},{48,16},{64,32},{80,48},{96,64},{112,80},{1... | collective-permute-start | bytes 2064392 | tf_op jit(solution)/shard_map/ppermute | solution.py:403
  29.5 17.3 %collective-permute-start.1 = (bf16[64,5376]{1,0:T(8,128)(2,1)S(1)}, bf16[64,5376]{1,0:T(8,128)(2,1)S(1)}, u32[]{:S(2)}, u32[]{:S(2)}) collective-permute-start(bf16[64,5376]{1,0:T(8,128)(2,1)S(1)} %reshape.16.own), channel_id=1, source_target_pairs={{0,32},{16,48},{32,64},{48,80},{64,96},{80,112},{96,0},{112,16},{1... | collective-permute-start | bytes 2064392 | tf_op jit(solution)/shard_map/ppermute | solution.py:403
  29.5 17.3 %all-to-all-start.1 = ((f32[128,1,64]{2,1,0:T(1,128)}), f32[128,1,64]{2,1,0:T(1,128)S(1)}, u32[]{:S(2)}, u32[]{:S(2)}) async-start(f32[128,1,64]{2,1,0:T(1,128)} %bitcast.4), calls=%async_computation.1 | async-start | bytes 131072 | tf_op jit(solution)/shard_map/all_to_all | solution.py:421
  35.6 13.9 %collective-permute-start = (bf16[64,5376]{1,0:T(8,128)(2,1)S(1)}, bf16[64,5376]{1,0:T(8,128)(2,1)S(1)}, u32[]{:S(2)}, u32[]{:S(2)}) collective-permute-start(bf16[64,5376]{1,0:T(8,128)(2,1)S(1)} %reshape.16.own), channel_id=1, source_target_pairs={{0,16},{16,0},{32,48},{48,32},{64,80},{80,64},{96,112},{112,96},{1... | collective-permute-start | bytes 2064392 | tf_op jit(solution)/shard_map/ppermute | solution.py:403
  46.8 2.7 %collective-permute-start.3 = (bf16[64,5376]{1,0:T(8,128)(2,1)S(1)}, bf16[64,5376]{1,0:T(8,128)(2,1)S(1)}, u32[]{:S(2)}, u32[]{:S(2)}) collective-permute-start(bf16[64,5376]{1,0:T(8,128)(2,1)S(1)} %collective-permute-done.1.left), channel_id=1, source_target_pairs={{0,16},{16,0},{32,48},{48,32},{64,80},{80,64},{96,112},{112,96},{1... | collective-permute-start | bytes 2064392 | tf_op jit(solution)/shard_map/ppermute | solution.py:403
  46.8 3.1 %collective-permute-start.4 = (bf16[64,5376]{1,0:T(8,128)(2,1)S(1)}, bf16[64,5376]{1,0:T(8,128)(2,1)S(1)}, u32[]{:S(2)}, u32[]{:S(2)}) collective-permute-start(bf16[64,5376]{1,0:T(8,128)(2,1)S(1)} %collective-permute-done.2.right), channel_id=1, source_target_pairs={{0,16},{16,0},{32,48},{48,32},{64,80},{80,64},{96,112},{112,96},{1... | collective-permute-start | bytes 2064392 | tf_op jit(solution)/shard_map/ppermute | solution.py:403
  47.3 14.1 %collective-permute-start.6 = (bf16[32,5376]{1,0:T(8,128)(2,1)S(1)}, bf16[32,5376]{1,0:T(8,128)(2,1)S(1)}, u32[]{:S(2)}, u32[]{:S(2)}) collective-permute-start(bf16[32,5376]{1,0:T(8,128)(2,1)S(1)} %slice.45), channel_id=1, source_target_pairs={{0,96},{16,112},{32,0},{48,16},{64,32},{80,48},{96,64},{112,80},{1... | collective-permute-start | bytes 1032200 | tf_op jit(solution)/shard_map/ppermute | solution.py:403
  47.7 13.8 %collective-permute-start.5 = (bf16[32,5376]{1,0:T(8,128)(2,1)S(1)}, bf16[32,5376]{1,0:T(8,128)(2,1)S(1)}, u32[]{:S(2)}, u32[]{:S(2)}) collective-permute-start(bf16[32,5376]{1,0:T(8,128)(2,1)S(1)} %slice.44), channel_id=1, source_target_pairs={{0,32},{16,48},{32,64},{48,80},{64,96},{80,112},{96,0},{112,16},{1... | collective-permute-start | bytes 1032200 | tf_op jit(solution)/shard_map/ppermute | solution.py:403
  59.5 2.0 %copy-start.2 = (bf16[384,5376]{1,0:T(8,128)(2,1)}, bf16[384,5376]{1,0:T(8,128)(2,1)S(1)}, u32[]{:S(2)}) copy-start(bf16[384,5376]{1,0:T(8,128)(2,1)S(1)} %get-tuple-element.56.near) | copy-start | bytes 12386308
  61.5 1.7 %collective-permute-start.7 = (bf16[32,5376]{1,0:T(8,128)(2,1)S(1)}, bf16[32,5376]{1,0:T(8,128)(2,1)S(1)}, u32[]{:S(2)}, u32[]{:S(2)}) collective-permute-start(bf16[32,5376]{1,0:T(8,128)(2,1)S(1)} %collective-permute-done.5.far_a), channel_id=1, source_target_pairs={{0,16},{16,0},{32,48},{48,32},{64,80},{80,64},{96,112},{112,96},{1... | collective-permute-start | bytes 1032200 | tf_op jit(solution)/shard_map/ppermute | solution.py:403
  61.6 2.0 %collective-permute-start.8 = (bf16[32,5376]{1,0:T(8,128)(2,1)S(1)}, bf16[32,5376]{1,0:T(8,128)(2,1)S(1)}, u32[]{:S(2)}, u32[]{:S(2)}) collective-permute-start(bf16[32,5376]{1,0:T(8,128)(2,1)S(1)} %collective-permute-done.6.far_b), channel_id=1, source_target_pairs={{0,16},{16,0},{32,48},{48,32},{64,80},{80,64},{96,112},{112,96},{1... | collective-permute-start | bytes 1032200 | tf_op jit(solution)/shard_map/ppermute | solution.py:403
  87.5 2.2 %collective-permute-start.9 = (bf16[64,5376]{1,0:T(8,128)(2,1)S(1)}, bf16[64,5376]{1,0:T(8,128)(2,1)S(1)}, u32[]{:S(2)}, u32[]{:S(2)}) collective-permute-start(bf16[64,5376]{1,0:T(8,128)(2,1)S(1)} %get-tuple-element.50), channel_id=1, source_target_pairs={{0,16},{16,0},{32,48},{48,32},{64,80},{80,64},{96,112},{112,96},{1... | collective-permute-start | bytes 2064392 | tf_op jit(solution)/shard_map/ppermute | solution.py:403
  88.6 1.3 copy-start.4
  89.9 10.2 %collective-permute-start.12 = (bf16[32,5376]{1,0:T(8,128)(2,1)S(1)}, bf16[32,5376]{1,0:T(8,128)(2,1)S(1)}, u32[]{:S(2)}, u32[]{:S(2)}) collective-permute-start(bf16[32,5376]{1,0:T(8,128)(2,1)S(1)} %get-tuple-element.64), channel_id=1, source_target_pairs={{0,96},{16,112},{32,0},{48,16},{64,32},{80,48},{96,64},{112,80},{1... | collective-permute-start | bytes 1032200 | tf_op jit(solution)/shard_map/ppermute | solution.py:403
  90.9 11.0 %collective-permute-start.11 = (bf16[32,5376]{1,0:T(8,128)(2,1)S(1)}, bf16[32,5376]{1,0:T(8,128)(2,1)S(1)}, u32[]{:S(2)}, u32[]{:S(2)}) collective-permute-start(bf16[32,5376]{1,0:T(8,128)(2,1)S(1)} %get-tuple-element.65), channel_id=1, source_target_pairs={{0,32},{16,48},{32,64},{48,80},{64,96},{80,112},{96,0},{112,16},{1... | collective-permute-start | bytes 1032200 | tf_op jit(solution)/shard_map/ppermute | solution.py:403
  97.4 4.6 %collective-permute-start.10 = (bf16[192,5376]{1,0:T(8,128)(2,1)S(1)}, bf16[192,5376]{1,0:T(8,128)(2,1)S(1)}, u32[]{:S(2)}, u32[]{:S(2)}) collective-permute-start(bf16[192,5376]{1,0:T(8,128)(2,1)S(1)} %get-tuple-element.53), channel_id=1, source_target_pairs={{0,16},{16,0},{32,48},{48,32},{64,80},{80,64},{96,112},{112,96},{1... | collective-permute-start | bytes 6193160 | tf_op jit(solution)/shard_map/ppermute | solution.py:403
  102.7 18.3 %collective-permute-start.13 = (bf16[64,5376]{1,0:T(8,128)(2,1)S(1)}, bf16[64,5376]{1,0:T(8,128)(2,1)S(1)}, u32[]{:S(2)}, u32[]{:S(2)}) collective-permute-start(bf16[64,5376]{1,0:T(8,128)(2,1)S(1)} %pad_maximum_fusion), channel_id=1, source_target_pairs={{0,32},{16,48},{32,64},{48,80},{64,96},{80,112},{96,0},{112,16},{1... | collective-permute-start | bytes 2064392 | tf_op jit(solution)/shard_map/ppermute | solution.py:403
  103.2 23.2 %copy-start.5 = (bf16[1024,512]{1,0:T(8,128)(2,1)S(1)}, bf16[1024,512]{1,0:T(8,128)(2,1)}, u32[]{:S(2)}) copy-start(bf16[1024,512]{1,0:T(8,128)(2,1)} %copy-done.4) | copy-start | bytes 3145732
  103.2 17.8 %collective-permute-start.14 = (bf16[64,5376]{1,0:T(8,128)(2,1)S(1)}, bf16[64,5376]{1,0:T(8,128)(2,1)S(1)}, u32[]{:S(2)}, u32[]{:S(2)}) collective-permute-start(bf16[64,5376]{1,0:T(8,128)(2,1)S(1)} %pad_maximum_fusion.1), channel_id=1, source_target_pairs={{0,96},{16,112},{32,0},{48,16},{64,32},{80,48},{96,64},{112,80},{1... | collective-permute-start | bytes 2064392 | tf_op jit(solution)/shard_map/ppermute | solution.py:403
  122.2 17.2 %all-to-all-start.3 = ((bf16[16,64,336]{2,1,0:T(8,128)(2,1)}), bf16[16,64,336]{2,1,0:T(8,128)(2,1)S(1)}, u32[]{:S(2)}, u32[]{:S(2)}) async-start(bf16[16,64,336]{2,1,0:T(8,128)(2,1)} %shard_map.82), calls=%async_computation.3 | async-start | bytes 1572864 | tf_op jit(solution)/shard_map/all_to_all | solution.py:452
  126.4 2.2 %copy-start.3 = (bf16[384,5376]{1,0:T(8,128)(2,1)S(1)}, bf16[384,5376]{1,0:T(8,128)(2,1)}, u32[]{:S(2)}) copy-start(bf16[384,5376]{1,0:T(8,128)(2,1)} %copy-done.2) | copy-start | bytes 12386308

commit v3 on v2

--- a/solution.py
+++ b/solution.py
@@ -35,23 +35,38 @@
     prob = expo / jnp.sum(expo, axis=1, keepdims=True)
     ids = ids_ref[...]
     shift = vocab_rows.bit_length() - 1
-    owner_iota = lax.broadcasted_iota(jnp.int32, (owners, width), 0)
-    slot_iota = lax.broadcasted_iota(jnp.int32, (owners, width), 1)
+    owner_of = lax.shift_right_logical(ids, shift)
+    local_of = (ids - owner_of * vocab_rows + 1).astype(jnp.float32)
+    owner_of = owner_of.astype(jnp.float32)
+    owner_iota = lax.broadcasted_iota(jnp.int32, (owners, width), 0).astype(jnp.float32)
+    slot_iota = lax.broadcasted_iota(jnp.int32, (owners, width), 1).astype(jnp.float32)
     lane = lax.broadcasted_iota(jnp.int32, (owners, rows * 16), 1)
     out = jnp.zeros((owners, rows * 16), jnp.float32)
     for row in range(rows):
-        row_ids = jnp.broadcast_to(ids[row : row + 1, :], (owners, width))
         row_prob = jnp.broadcast_to(prob[row : row + 1, :], (owners, width))
-        owner = lax.shift_right_logical(row_ids, shift)
-        start = jnp.sum((owner < owner_iota).astype(jnp.int32), axis=1, keepdims=True)
-        place = jnp.where(owner == owner_iota, slot_iota - start, -1)
-        local = (row_ids - owner * vocab_rows + 1).astype(jnp.float32)
-        for slot in range(SLOTS):
+        owner = jnp.broadcast_to(owner_of[row : row + 1, :], (owners, width))
+        local = jnp.broadcast_to(local_of[row : row + 1, :], (owners, width))
+        same = owner == owner_iota
+        start = jnp.sum(jnp.where(owner < owner_iota, 1.0, 0.0), axis=1, keepdims=True)
+        place = jnp.where(same, slot_iota - start, -1.0)
+        for slot in range(2):
             hit = place == slot
             value = jnp.sum(jnp.where(hit, row_prob, 0.0), axis=1, keepdims=True)
             index = jnp.sum(jnp.where(hit, local, 0.0), axis=1, keepdims=True) - 1.0
-            out = out + jnp.where(lane == row * 16 + slot, value, 0.0)
-            out = out + jnp.where(lane == row * 16 + 8 + slot, index, 0.0)
+            out = out + jnp.where(lane == row * 16 + slot, value, jnp.where(lane == row * 16 + 8 + slot, index, 0.0))
+        many = jnp.sum(jnp.where(same, 1.0, 0.0), axis=1, keepdims=True) > 2.0
+        first = jnp.sum(jnp.where(many, start, 0.0), axis=0, keepdims=True)
+        hot_place = slot_iota[:1] - first
+        hot_index = local_of[row : row + 1, :]
+        extra = jnp.zeros((1, rows * 16), jnp.float32)
+        for slot in range(2, SLOTS):
+            hit = hot_place == slot
+            value = jnp.sum(jnp.where(hit, prob[row : row + 1, :], 0.0), axis=1, keepdims=True)
+            index = jnp.sum(jnp.where(hit, hot_index, 0.0), axis=1, keepdims=True)
+            at = lane[:1]
+            extra = extra + jnp.where(at == row * 16 + slot, value, jnp.where(at == row * 16 + 8 + slot, index, 0.0))
+        empty = (lane >= row * 16 + 10) & (lane < row * 16 + 8 + SLOTS)
+        out = out + jnp.where(many, extra, 0.0) - empty.astype(jnp.float32)
     out_ref[...] = out
 
 
@@ -63,6 +78,42 @@
         compiler_params=params(),
         cost_estimate=cost(4e6, 40000),
     )(teacher_logits, teacher_ids)
+
+
+def copies_kernel(block, out):
+    for index in range(out.shape[0]):
+        out[index] = block[...]
+
+
+def copies_of(block, count):
+    return pl.pallas_call(
+        copies_kernel,
+        in_specs=[WHOLE],
+        out_specs=WHOLE,
+        out_shape=jax.ShapeDtypeStruct((count, *block.shape), block.dtype),
+        compiler_params=params(),
+        cost_estimate=cost(1000, 1e6),
+    )(block)
+
+
+def join_kernel(parts, out, rows):
+    part = parts.shape[2]
+    for index in range(parts.shape[0]):
+        rows[:, index * part : (index + 1) * part] = parts[index].astype(jnp.float32)
+    out[...] = rows[...].astype(jnp.bfloat16)
+
+
+def join_parts(parts):
+    count, rows, part = parts.shape
+    return pl.pallas_call(
+        join_kernel,
+        in_specs=[WHOLE],
+        out_specs=WHOLE,
+        out_shape=jax.ShapeDtypeStruct((rows, count * part), parts.dtype),
+        scratch_shapes=[pltpu.VMEM((rows, count * part), jnp.float32)],
+        compiler_params=params(),
+        cost_estimate=cost(1e6, 2e6),
+    )(parts)
 
 
 def dot_nt(a, b):
@@ -80,17 +131,7 @@
     return jnp.where(row == 0, lse, jnp.where(row == 1, mean, jnp.where(row == 2, cross, 0.0)))
 
 
-def load_blocks(pieces, dest, sems):
-    copies = [
-        pltpu.make_async_copy(src, dest.at[pl.ds(pl.multiple_of(row, 32), src.shape[0])], sems.at[k])
-        for k, (src, row) in enumerate(pieces)
-    ]
-    for copy in copies:
-        copy.start()
-    return copies
-
-
-def first_kernel(pos, got, source, own, own2, left, left2, right, right2, w, out, target, stats, held, teach, sems):
+def first_kernel(pos, got, source, own, own2, left, left2, right, right2, w, out, target, held, teach, sems):
     z, core = pos[0], pos[1]
     count = sems.shape[0]
     chunk = source.shape[0] // count
@@ -134,8 +175,6 @@
         logits = dot_nt(w[at], held[...])
         for slot in range(3):
             out[slot, at] = logits[:, slot * LANES : (slot + 1) * LANES]
-    for slot in range(3):
-        stats[slot] = local_stats(out[slot], target[slot])
 
 
 def first_logits(pos, got, source, blocks):
@@ -143,12 +182,11 @@
     return pl.pallas_call(
         first_kernel,
         in_specs=[SCALARS, WHOLE, FAR] + [WHOLE] * 6,
-        out_specs=[WHOLE] * 5,
+        out_specs=[WHOLE] * 4,
         out_shape=[
             pltpu.VMEM((vocab, width), jnp.bfloat16),
             jax.ShapeDtypeStruct((3, vocab, LANES), jnp.float32),
             jax.ShapeDtypeStruct((4, vocab, LANES), jnp.float32),
-            jax.ShapeDtypeStruct((3, 8, LANES), jnp.float32),
             jax.ShapeDtypeStruct((3 * LANES, width), jnp.bfloat16),
         ],
         scratch_shapes=[pltpu.VMEM((4, 16, LANES), jnp.float32), pltpu.SemaphoreType.DMA((2,))],
@@ -157,45 +195,61 @@
     )(pos, got, pltpu.with_memory_space_constraint(source, pltpu.HBM), *blocks)
 
 
-def last_kernel(pos, w, target, early, far_a, far_b, far_a2, far_b2, out, send, held, table, sems):
+def spread_stats(info):
+    lane = lax.broadcasted_iota(jnp.int32, (32, LANES), 1)
+    row = lax.broadcasted_iota(jnp.int32, (32, LANES), 0)
+    extra = jnp.zeros((32, LANES), jnp.float32)
+    for kind in range(3):
+        for token in range(4):
+            value = jnp.sum(jnp.where(lane == row * 4 + token, info[kind : kind + 1], 0.0), axis=1, keepdims=True)
+            extra = extra + jnp.where(lane == kind * 4 + token, value, 0.0)
+    return extra
+
+
+def fill_send(send, block, info):
+    send[:, pl.ds(pl.multiple_of(block * LANES, LANES), LANES)] = jnp.broadcast_to(info[0:1], (LANES, LANES))
+    send[pl.ds(pl.multiple_of(block * 32, 32), 32), 4 * LANES : 5 * LANES] = spread_stats(info)
+
+
+def stats_kernel(pos, logits, target, send):
+    for slot in range(3):
+        fill_send(send, (pos[0] + OFFSETS[slot]) % 4, local_stats(logits[slot], target[slot]))
+
+
+def near_stats(pos, logits, target):
+    return pl.pallas_call(
+        stats_kernel,
+        in_specs=[SCALARS] + [WHOLE] * 2,
+        out_specs=WHOLE,
+        out_shape=jax.ShapeDtypeStruct((LANES, 5 * LANES), jnp.float32),
+        compiler_params=params(),
+        cost_estimate=cost(1000, 1000),
+    )(pos, logits, target)
+
+
+def last_kernel(pos, w, target, early, far_a, far_b, far_a2, far_b2, out, send, held):
     z, core = pos[0], pos[1]
     mine, other = core * 64, (1 - core) * 64
-    copies = load_blocks(
-        [(far_a, mine), (far_b, mine + 32), (far_a2, other), (far_b2, other + 32)], held, sems
-    )
-    for copy in copies:
-        copy.wait()
+    for block, row in ((far_a, mine), (far_b, mine + 32), (far_a2, other), (far_b2, other + 32)):
+        held[pl.ds(pl.multiple_of(row, 32), 32)] = block[...]
     out[...] = dot_nt(w[...], held[...])
-    for slot in range(3):
-        table[(z + OFFSETS[slot]) % 4] = early[slot]
-    table[(z + OFFSETS[3]) % 4] = local_stats(out[...], target[3])
-    lane = lax.broadcasted_iota(jnp.int32, (32, LANES), 1)
-    row = lax.broadcasted_iota(jnp.int32, (32, LANES), 0)
-    for block in range(4):
-        info = table[block]
-        send[:, block * LANES : (block + 1) * LANES] = jnp.broadcast_to(info[0:1], (LANES, LANES))
-        extra = jnp.zeros((32, LANES), jnp.float32)
-        for kind in range(3):
-            for token in range(4):
-                value = jnp.sum(
-                    jnp.where(lane == row * 4 + token, info[kind : kind + 1], 0.0), axis=1, keepdims=True
-                )
-                extra = extra + jnp.where(lane == kind * 4 + token, value, 0.0)
-        send[block * 32 : (block + 1) * 32, 4 * LANES : 5 * LANES] = extra
+    for block in range(5):
+        at = slice(block * LANES, (block + 1) * LANES)
+        send[:, at] = early[:, at]
+    fill_send(send, (z + OFFSETS[3]) % 4, local_stats(out[...], target[3]))
 
 
 def last_logits(pos, w, target, early, blocks):
     vocab, width = w.shape
     return pl.pallas_call(
         last_kernel,
-        in_specs=[SCALARS] + [WHOLE] * 3 + [ANY] * 4,
+        in_specs=[SCALARS] + [WHOLE] * 7,
         out_specs=[WHOLE] * 3,
         out_shape=[
             jax.ShapeDtypeStruct((vocab, LANES), jnp.float32),
             jax.ShapeDtypeStruct((LANES, 5 * LANES), jnp.float32),
             jax.ShapeDtypeStruct((LANES, width), jnp.bfloat16),
         ],
-        scratch_shapes=[pltpu.VMEM((4, 8, LANES), jnp.float32), pltpu.SemaphoreType.DMA((4,))],
         compiler_params=params(),
         cost_estimate=cost(2 * vocab * width * 128, vocab * width * 2),
     )(pos, w, target, early, *blocks)
@@ -256,13 +310,22 @@
     )(pos, stats, logits, target, w)
 
 
-def grads_kernel(pos, logits, target, lse, far, wide_out, left_out):
+def grads_kernel(pos, logits, target, lse, far, wide_out, first_out, second_out, own_out):
     z = pos[0]
     for slot in range(3):
         row = lse[(z + OFFSETS[slot]) % 4]
         grad = grad_of(logits[slot], row[0:1], target[slot])
         wide_out[:, slot * LANES : (slot + 1) * LANES] = grad.astype(jnp.bfloat16)
-        left_out[slot * LANES : (slot + 1) * LANES, :] = grad.T.astype(jnp.bfloat16)
+        flipped = grad.T.astype(jnp.bfloat16)
+        if slot == 0:
+            own_out[...] = flipped
+        else:
+            for core in range(2):
+                low = flipped[core * 64 : core * 64 + 32]
+                high = flipped[core * 64 + 32 : core * 64 + 64]
+                to = slice(core * 64 + (slot - 1) * 32, core * 64 + slot * 32)
+                first_out[to, :] = low if slot == 1 else high
+                second_out[to, :] = high if slot == 1 else low
     wide_out[:, 3 * LANES :] = far[...]
 
 
@@ -271,11 +334,9 @@
     return pl.pallas_call(
         grads_kernel,
         in_specs=[SCALARS] + [WHOLE] * 4,
-        out_specs=[WHOLE] * 2,
-        out_shape=[
-            jax.ShapeDtypeStruct((vocab, 4 * LANES), jnp.bfloat16),
-            jax.ShapeDtypeStruct((3 * LANES, vocab), jnp.bfloat16),
-        ],
+        out_specs=[WHOLE] * 4,
+        out_shape=[jax.ShapeDtypeStruct((vocab, 4 * LANES), jnp.bfloat16)]
+        + [jax.ShapeDtypeStruct((LANES, vocab), jnp.bfloat16)] * 3,
         compiler_params=params(),
         cost_estimate=cost(2e6, 5e6),
     )(pos, logits, target, lse, far)
@@ -286,7 +347,7 @@
     for tile in range(w.shape[1] // COLS):
         at = slice(tile * COLS, (tile + 1) * COLS)
         acc[...] = jnp.dot(left[...], w[:, at], preferred_element_type=jnp.float32)
-        for slot in range(3):
+        for slot in range(left.shape[0] // LANES):
             to = slice(slot * 64, (slot + 1) * 64)
             mine_out[to, at] = acc[pl.ds(pl.multiple_of(slot * 128 + core * 64, 64), 64)]
             part = acc[pl.ds(pl.multiple_of(slot * 128 + (1 - core) * 64, 64), 64)]
@@ -348,22 +409,41 @@
     )(upper, lower)
 
 
-def fold_kernel(near, from_left, from_right, out, total):
-    rows = from_left.shape[0]
-    total[...] = near[:rows] + from_left[...].astype(jnp.float32) + from_right[...].astype(jnp.float32)
+def gather_own_kernel(mine, swap, left_b, right_b, out):
+    half = left_b.shape[0]
+    f32 = jnp.float32
+    out[:half] = mine[:half] + swap[:half].astype(f32) + left_b[...].astype(f32)
+    out[half:] = mine[half:] + swap[half:].astype(f32) + right_b[...].astype(f32)
+
+
+def gather_own(*pieces):
+    return pl.pallas_call(
+        gather_own_kernel,
+        in_specs=[WHOLE] * 4,
+        out_specs=WHOLE,
+        out_shape=jax.ShapeDtypeStruct(pieces[0].shape, jnp.float32),
+        compiler_params=params(),
+        cost_estimate=cost(1e11, 1e9),
+    )(*pieces)
+
+
+def fold_kernel(near, right_a, left_a, out, total):
+    half = right_a.shape[0]
+    total[:half] = (near[:half] + right_a[...].astype(jnp.float32)).astype(jnp.bfloat16)
+    total[half:] = (near[half:] + left_a[...].astype(jnp.float32)).astype(jnp.bfloat16)
     part = out.shape[2]
     for index in range(out.shape[0]):
-        out[index] = total[:, index * part : (index + 1) * part].astype(jnp.bfloat16)
+        out[index] = total[:, index * part : (index + 1) * part]
 
 
 def fold(count, pieces):
-    rows, width = pieces[1].shape
+    rows, width = pieces[0].shape
     return pl.pallas_call(
         fold_kernel,
         in_specs=[WHOLE] * 3,
         out_specs=WHOLE,
         out_shape=jax.ShapeDtypeStruct((count, rows, width // count), jnp.bfloat16),
-        scratch_shapes=[pltpu.VMEM((rows, width), jnp.float32)],
+        scratch_shapes=[pltpu.VMEM((rows, width), jnp.bfloat16)],
         compiler_params=params(),
         cost_estimate=cost(2e6, 4e6),
     )(*pieces)
@@ -409,46 +489,57 @@
     bf16 = jnp.bfloat16
     half = tok_rows // 2
 
-    spread = jnp.broadcast_to(hidden[None], (vocab_count, tok_rows, feat_part))
+    hidden, pos = lax.optimization_barrier((hidden, pos))
+    spread = copies_of(hidden, vocab_count)
     spread = lax.all_to_all(spread, "vocab", split_axis=0, concat_axis=0, tiled=True)
-    teach = teacher_rows(owners, vocab_rows, teacher_logits, teacher_ids)
-    spread, (teach, pos) = lax.optimization_barrier((spread, (teach, pos)))
-    own = spread.transpose(1, 0, 2).reshape(tok_rows, width)
+    own = join_parts(spread)
     left = move(own, up)
     right = move(own, down)
     own2 = move(own, twin)
-    teach = after(teach, own)
+    teacher_logits, own = lax.optimization_barrier((teacher_logits, own))
+    teach = teacher_rows(owners, vocab_rows, teacher_logits, teacher_ids)
     got = lax.all_to_all(teach, BOTH, split_axis=0, concat_axis=0, tiled=True)
     left, right = after((left, right), got)
     far_a = move(left[:half], up)
     far_b = move(right[half:], down)
     near_blocks = (own, own2, left, move(left, twin), right, move(right, twin))
-    weight, logits, target, early, near_rows = first_logits(pos, got, head_weight, near_blocks)
-    far_a, far_b = after((far_a, far_b), early)
+    weight, logits, target, near_rows = first_logits(pos, got, head_weight, near_blocks)
+    far_a, far_b = after((far_a, far_b), logits)
+    early = near_stats(pos, logits, target)
     far_blocks = (far_a, far_b, move(far_a, twin), move(far_b, twin))
     far_logits, send, far_rows = last_logits(pos, weight, target, early, far_blocks)
     stats = lax.all_to_all(send, BOTH, split_axis=0, concat_axis=0, tiled=True)
 
     far_mine, far_other, grad_far, lse, loss = far_grad(pos, stats, far_logits, target, weight)
     far_swap = move(far_other, twin)
-    wide, near_left = near_grads(pos, logits, target, lse, grad_far)
+    wide, first_left, second_left, own_left = near_grads(pos, logits, target, lse, grad_far)
+    first_mine, first_other = near_grad(pos, first_left, weight)
+    first_swap = move(first_other, twin)
     far_sum = (far_mine + far_swap.astype(f32)).astype(bf16)
     go_up = move(far_sum[:half], up)
     go_down = move(far_sum[half:], down)
-    near_left = after(near_left, far_sum)
-    mine, other = near_grad(pos, near_left, weight)
-    swap = move(other, twin)
+    second_left = after(second_left, far_sum, first_other)
+    second_mine, second_other = near_grad(pos, second_left, weight)
+    second_swap = move(second_other, twin)
+    own_left = after(own_left, second_other)
+    own_mine, own_other = near_grad(pos, own_left, weight)
+    own_swap = move(own_other, twin)
+    first_sum = (first_mine + first_swap.astype(f32)).astype(bf16)
+    left_b_part, right_b_part = first_sum[:half], first_sum[half:]
+    left_b = move(left_b_part, down)
+    right_b = move(right_b_part, up)
+    second_sum = second_mine + second_swap.astype(f32)
+    go_up, go_down = after((go_up, go_down), right_b_part, left_b_part)
     passed = widen(go_up, go_down)
-    swap = after(swap, passed)
-    near_sum = mine + swap.astype(f32)
-    to_right = near_sum[2 * tok_rows :]
-    to_right = jnp.concatenate([to_right[:half] + passed[0], to_right[half:]]).astype(bf16)
-    to_left = near_sum[tok_rows : 2 * tok_rows]
-    to_left = jnp.concatenate([to_left[:half], to_left[half:] + passed[1]]).astype(bf16)
-    from_left = move(to_right, up)
-    from_right = move(to_left, down)
-    grad_weight = weight_grad(wide, near_rows, far_rows)
-    parts = fold(vocab_count, (near_sum, from_left, from_right))
+    left_a_part = (second_sum[:half] + passed[1]).astype(bf16)
+    right_a_part = (second_sum[half:] + passed[0]).astype(bf16)
+    left_a = move(left_a_part, down)
+    right_a = move(right_a_part, up)
+    grad_weight = weight_grad(after(wide, left_a_part, right_a_part), near_rows, far_rows)
+    left_b, right_b = after((left_b, right_b), grad_weight)
+    gathered = gather_own(own_mine, own_swap, left_b, right_b)
+    (right_a, left_a), gathered = lax.optimization_barrier(((right_a, left_a), gathered))
+    parts = fold(vocab_count, (gathered, right_a, left_a))
     parts = lax.all_to_all(parts, "vocab", split_axis=0, concat_axis=0, tiled=True)
     grad_hidden = sum_parts(parts)
     rows = teacher_logits.shape[0]

time: 141 us -> 134 us (0.950)
  blocking collectives: 16.5 us -> 37.9 us
  waiting for transfers between devices: 49 us -> 29.7 us
  local copies, waits for them, and re-layouts: 8.31 us -> 1.83 us
  starting transfers between devices: 29.7 us -> 26 us
  Pallas kernels: 34.9 us -> 37.1 us
    all_to_all x0 -> x1, blocking collectives: none -> 21.3 us  [body(): lax.all_to_all(spread, 'vocab', split_axis=0, concat_axis=0, tiled=True)]
    ppermute x15 -> x19, waiting for transfers between devices: 22.5 us -> 7.8 us  [move(): return lax.ppermute(x, 'seq', perm)]
    all_to_all x1 -> x0, waiting for transfers between devices: 12.4 us -> none  [body(): lax.all_to_all(spread, 'vocab', split_axis=0, concat_axis=0, tiled=True)]
    all_to_all x1, waiting for transfers between devices: 2.91 us -> 12.6 us  [body(): lax.all_to_all(parts, 'vocab', split_axis=0, concat_axis=0, tiled=True)]
    all_to_all x1 -> x0, starting transfers between devices: 7.12 us -> none  [body(): lax.all_to_all(spread, 'vocab', split_axis=0, concat_axis=0, tiled=True)]
    ppermute x15 -> x19, starting transfers between devices: 13 us -> 17.3 us  [move(): return lax.ppermute(x, 'seq', perm)]
    unnamed x13 -> x7, local copies, waits for them, and re-layouts: 4.19 us -> 0.83 us
    broadcast_in_dim x1 -> x0, local copies, waits for them, and re-layouts: 1.79 us -> none  [body(): spread = jnp.broadcast_to(hidden[None], (vocab_count, tok_rows, feat_part))]
  transfers between devices with their start and end apart: 18 -> 21, of which waited for: 10 -> 6; matrix products, arithmetic and copies ran while one was open for 0% -> 1% of each run, Pallas kernels for 19% -> 21%
where the time goes in v3:
time: 134 us
  blocking collectives  37.9 us (28%)
  Pallas kernels  37.1 us (28%)
  waiting for transfers between devices  29.7 us (22%)
  starting transfers between devices  26 us (19%)
  local copies, waits for them, and re-layouts  1.83 us (1%)
    all_to_all x1, blocking collectives, body(): lax.all_to_all(spread, 'vocab', split_axis=0, concat_axis=0, tiled=True)  21.3 us
    ppermute x19, starting transfers between devices, move(): return lax.ppermute(x, 'seq', perm)  17.3 us
    all_to_all x1, blocking collectives, body(): stats = lax.all_to_all(send, BOTH, split_axis=0, concat_axis=0, tiled=True)  16.7 us
    all_to_all x1, waiting for transfers between devices, body(): lax.all_to_all(parts, 'vocab', split_axis=0, concat_axis=0, tiled=True)  12.6 us
    all_to_all x1, waiting for transfers between devices, body(): got = lax.all_to_all(teach, BOTH, split_axis=0, concat_axis=0, tiled=True)  9.36 us
    pallas_call x1, Pallas kernels, first_logits(): pl.pallas_call(first_kernel, in_specs=[SCALARS, WHOLE, FAR] + [WHOLE] * 6...  9.15 us
    pallas_call x1, Pallas kernels, weight_grad(): pl.pallas_call(weight_kernel, grid=(vocab // rows,), in_specs=[pl.BlockSp...  7.96 us
    ppermute x19, waiting for transfers between devices, move(): return lax.ppermute(x, 'seq', perm)  7.8 us
  transfers between devices with their start and end apart: 21, of which 6 were waited for; matrix products, arithmetic and copies ran while one was open for 1% of the time, Pallas kernels for 21%

profile of v3, /device:TPU:0, one launch (start us, length us, event | category | flops | bytes accessed | tf_op | source)
XLA Modules:
  0.0 134.1 jit_solution(9808332191684556717)
XLA Ops:
  0.7 0.8 copy-done
  1.6 21.3 %all_to_all.32.parts = bf16[16,64,336]{2,1,0:T(8,128)(2,1)S(1)} all-to-all(bf16[16,64,336]{2,1,0:T(8,128)(2,1)S(1)} %shard_map.75), channel_id=1, replica_groups=mesh['seq'=8,'vocab'=16] {'vocab'}, dimensions={0} | all-to-all | bytes 1376256 | tf_op jit(solution)/shard_map/all_to_all | solution.py:494
  23.2 2.0 %collective-permute-start.1 = (bf16[64,5376]{1,0:T(8,128)(2,1)S(1)}, bf16[64,5376]{1,0:T(8,128)(2,1)S(1)}, u32[]{:S(2)}, u32[]{:S(2)}) collective-permute-start(bf16[64,5376]{1,0:T(8,128)(2,1)S(1)} %shard_map.76.own), channel_id=1, source_target_pairs={{0,32},{16,48},{32,64},{48,80},{64,96},{80,112},{96,0},{112,16},{1... | collective-permute-start | bytes 2064392 | tf_op jit(solution)/shard_map/ppermute | solution.py:483
  25.2 2.2 %collective-permute-start.2 = (bf16[64,5376]{1,0:T(8,128)(2,1)S(1)}, bf16[64,5376]{1,0:T(8,128)(2,1)S(1)}, u32[]{:S(2)}, u32[]{:S(2)}) collective-permute-start(bf16[64,5376]{1,0:T(8,128)(2,1)S(1)} %shard_map.76.own), channel_id=1, source_target_pairs={{0,96},{16,112},{32,0},{48,16},{64,32},{80,48},{96,64},{112,80},{1... | collective-permute-start | bytes 2064392 | tf_op jit(solution)/shard_map/ppermute | solution.py:483
  27.4 1.6 %shard_map.77 = f32[128,64]{1,0:T(8,128)} custom-call(f32[4,256]{1,0:T(4,128)S(1)} %copy-done.1, s32[4,256]{1,0:T(4,128)S(1)} %copy-done.2), custom_call_target="tpu_custom_call" | custom-call | flops 4000000 | bytes 40000 | tf_op jit(solution)/shard_map/pallas_call | solution.py:75
  29.0 5.0 %all-to-all-start.1 = ((f32[128,1,64]{2,1,0:T(1,128)}), f32[128,1,64]{2,1,0:T(1,128)S(1)}, u32[]{:S(2)}, u32[]{:S(2)}) async-start(f32[128,1,64]{2,1,0:T(1,128)} %bitcast.3), calls=%async_computation.1 | async-start | bytes 131072 | tf_op jit(solution)/shard_map/all_to_all | solution.py:501
  34.1 9.4 %all-to-all-done.1 = f32[128,1,64]{2,1,0:T(1,128)S(1)} async-done(((f32[128,1,64]{2,1,0:T(1,128)}), f32[128,1,64]{2,1,0:T(1,128)S(1)}, u32[]{:S(2)}, u32[]{:S(2)}) %all-to-all-start.1) | async-done | bytes 32800 | tf_op jit(solution)/shard_map/all_to_all | solution.py:501
  43.5 0.5 collective-permute-start.4
  44.0 1.2 collective-permute-start.5
  45.2 2.1 %collective-permute-start.6 = (bf16[32,5376]{1,0:T(8,128)(2,1)S(1)}, bf16[32,5376]{1,0:T(8,128)(2,1)S(1)}, u32[]{:S(2)}, u32[]{:S(2)}) collective-permute-start(bf16[32,5376]{1,0:T(8,128)(2,1)S(1)} %slice.37), channel_id=1, source_target_pairs={{0,96},{16,112},{32,0},{48,16},{64,32},{80,48},{96,64},{112,80},{1... | collective-permute-start | bytes 1032200 | tf_op jit(solution)/shard_map/ppermute | solution.py:483
  47.4 9.2 %shard_map.78 = (bf16[1024,5376]{1,0:T(8,128)(2,1)S(1)}, f32[3,1024,128]{2,1,0:T(8,128)S(1)}, f32[4,1024,128]{2,1,0:T(8,128)S(1)}, bf16[384,5376]{1,0:T(8,128)(2,1)S(1)}) custom-call(s32[2]{0:T(128)S(1)} %pad_add_fusion.pos, f32[128,64]{1,0:T(8,128)S(1)} %bitcast.28, bf16[1024,5376]{1,0:T(8,128)(2,1)} %source.1, bf16[64,5376]{1,0:T(8,128)(2,1)S(1)} %shard_map.76.own, ...), custom_call_target="tpu_custom_call" | custom-call | flops 1000 | bytes 1000 | tf_op jit(solution)/shard_map/pallas_call | solution.py:182
  57.1 1.4 %shard_map.79.early = f32[128,640]{1,0:T(8,128)S(1)} custom-call(s32[2]{0:T(128)S(1)} %pad_add_fusion.pos, f32[3,1024,128]{2,1,0:T(8,128)S(1)} %get-tuple-element.52.logits, f32[4,1024,128]{2,1,0:T(8,128)S(1)} %get-tuple-element.51.target), custom_call_target="tpu_custom_call" | custom-call | flops 1000 | bytes 1000 | tf_op jit(solution)/shard_map/pallas_call | solution.py:220
  58.8 4.0 %shard_map.80 = (f32[1024,128]{1,0:T(8,128)S(1)}, f32[128,640]{1,0:T(8,128)S(1)}, bf16[128,5376]{1,0:T(8,128)(2,1)S(1)}) custom-call(s32[2]{0:T(128)S(1)} %pad_add_fusion.pos, bf16[1024,5376]{1,0:T(8,128)(2,1)S(1)} %get-tuple-element.50.w, f32[4,1024,128]{2,1,0:T(8,128)S(1)} %get-tuple-element.51.target, f32[128,640]{1,0:T(8,128)S(1)} %shard_map.79.early, ...), custom_call_target="tpu_custom_call" | custom-call | flops 1409286144 | bytes 11010048 | tf_op jit(solution)/shard_map/pallas_call | solution.py:244
  63.1 16.7 %all_to_all.33 = f32[128,1,640]{2,1,0:T(1,128)S(1)} all-to-all(f32[128,1,640]{2,1,0:T(1,128)S(1)} %copy.9), channel_id=1, replica_groups=mesh['seq'=8,'vocab'=16] {'seq','vocab'}, dimensions={0} | all-to-all | bytes 655360 | tf_op jit(solution)/shard_map/all_to_all | solution.py:511
  79.8 2.5 %shard_map.81 = (f32[64,5376]{1,0:T(8,128)S(1)}, bf16[64,5376]{1,0:T(8,128)(2,1)S(1)}, bf16[1024,128]{1,0:T(8,128)(2,1)S(1)}, f32[4,8,128]{2,1,0:T(8,128)S(1)}, f32[8,128]{1,0:T(8,128)S(1)}) custom-call(s32[2]{0:T(128)S(1)} %pad_add_fusion.pos, f32[128,640]{1,0:T(8,128)S(1)} %bitcast.26, f32[1024,128]{1,0:T(8,128)S(1)} %get-tuple-element.56.logits, ...), custom_call_target="tpu_custom_call" | custom-call | flops 1409286144 | bytes 11010048 | tf_op jit(solution)/shard_map/pallas_call | solution.py:296
  82.4 1.0 shard_map.82
  83.4 2.3 %shard_map.83 = (f32[64,5376]{1,0:T(8,128)S(1)}, bf16[64,5376]{1,0:T(8,128)(2,1)S(1)}) custom-call(s32[2]{0:T(128)S(1)} %pad_add_fusion.pos, bf16[128,1024]{1,0:T(8,128)(2,1)S(1)} %get-tuple-element.63.left, bf16[1024,5376]{1,0:T(8,128)(2,1)S(1)} %get-tuple-element.50.w), custom_call_target="tpu_custom_call" | custom-call | flops 1409286144 | bytes 11010048 | tf_op jit(solution)/shard_map/pallas_call | solution.py:360
  85.7 0.6 collective-permute-start.13
  86.5 0.9 collective-permute-start.11
  87.4 2.4 %collective-permute-start.12 = (bf16[32,5376]{1,0:T(8,128)(2,1)S(1)}, bf16[32,5376]{1,0:T(8,128)(2,1)S(1)}, u32[]{:S(2)}, u32[]{:S(2)}) collective-permute-start(bf16[32,5376]{1,0:T(8,128)(2,1)S(1)} %get-tuple-element.88), channel_id=1, source_target_pairs={{0,96},{16,112},{32,0},{48,16},{64,32},{80,48},{96,64},{112,80},{1... | collective-permute-start | bytes 1032200 | tf_op jit(solution)/shard_map/ppermute | solution.py:483
  90.0 2.3 %shard_map.84 = (f32[64,5376]{1,0:T(8,128)S(1)}, bf16[64,5376]{1,0:T(8,128)(2,1)S(1)}) custom-call(s32[2]{0:T(128)S(1)} %pad_add_fusion.pos, bf16[128,1024]{1,0:T(8,128)(2,1)S(1)} %get-tuple-element.65.left, bf16[1024,5376]{1,0:T(8,128)(2,1)S(1)} %get-tuple-element.50.w), custom_call_target="tpu_custom_call" | custom-call | flops 1409286144 | bytes 11010048 | tf_op jit(solution)/shard_map/pallas_call | solution.py:360
  92.6 2.3 %shard_map.86 = (f32[64,5376]{1,0:T(8,128)S(1)}, bf16[64,5376]{1,0:T(8,128)(2,1)S(1)}) custom-call(s32[2]{0:T(128)S(1)} %pad_add_fusion.pos, bf16[128,1024]{1,0:T(8,128)(2,1)S(1)} %get-tuple-element.72.left, bf16[1024,5376]{1,0:T(8,128)(2,1)S(1)} %get-tuple-element.50.w), custom_call_target="tpu_custom_call" | custom-call | flops 1409286144 | bytes 11010048 | tf_op jit(solution)/shard_map/pallas_call | solution.py:360
  94.9 0.6 collective-permute-start.16
  95.5 2.2 %collective-permute-done.11.upper = bf16[32,5376]{1,0:T(8,128)(2,1)S(1)} collective-permute-done((bf16[32,5376]{1,0:T(8,128)(2,1)S(1)}, bf16[32,5376]{1,0:T(8,128)(2,1)S(1)}, u32[]{:S(2)}, u32[]{:S(2)}) %collective-permute-start.11) | collective-permute-done | bytes 344096 | tf_op jit(solution)/shard_map/ppermute | solution.py:483
  98.5 3.8 %collective-permute-start.15 = (bf16[32,5376]{1,0:T(8,128)(2,1)S(1)}, bf16[32,5376]{1,0:T(8,128)(2,1)S(1)}, u32[]{:S(2)}, u32[]{:S(2)}) collective-permute-start(bf16[32,5376]{1,0:T(8,128)(2,1)S(1)} %get-tuple-element.84), channel_id=1, source_target_pairs={{0,96},{16,112},{32,0},{48,16},{64,32},{80,48},{96,64},{112,80},{1... | collective-permute-start | bytes 1032200 | tf_op jit(solution)/shard_map/ppermute | solution.py:483
  102.2 8.0 %shard_map.87 = bf16[1024,5376]{1,0:T(8,128)(2,1)} custom-call(bf16[1024,512]{1,0:T(8,128)(2,1)S(1)} %get-tuple-element.76.grad, bf16[384,5376]{1,0:T(8,128)(2,1)S(1)} %get-tuple-element.77.near, bf16[128,5376]{1,0:T(8,128)(2,1)S(1)} %get-tuple-element.78.far), custom_call_target="tpu_custom_call" | custom-call | flops 5637144576 | bytes 16515072 | tf_op jit(solution)/shard_map/pallas_call | solution.py:385
  110.4 5.1 %collective-permute-done.14.right_a = bf16[32,5376]{1,0:T(8,128)(2,1)S(1)} collective-permute-done((bf16[32,5376]{1,0:T(8,128)(2,1)S(1)}, bf16[32,5376]{1,0:T(8,128)(2,1)S(1)}, u32[]{:S(2)}, u32[]{:S(2)}) %collective-permute-start.14) | collective-permute-done | bytes 344096 | tf_op jit(solution)/shard_map/ppermute | solution.py:483
  115.5 1.2 shard_map.89
  116.7 3.6 %all-to-all-start.3 = ((bf16[16,64,336]{2,1,0:T(8,128)(2,1)}), bf16[16,64,336]{2,1,0:T(8,128)(2,1)S(1)}, u32[]{:S(2)}, u32[]{:S(2)}) async-start(bf16[16,64,336]{2,1,0:T(8,128)(2,1)} %shard_map.89), calls=%async_computation.3 | async-start | bytes 1572864 | tf_op jit(solution)/shard_map/all_to_all | solution.py:543
  120.3 0.5 slice_bitcast_fusion.2
  120.8 12.6 %all-to-all-done.3.parts = bf16[16,64,336]{2,1,0:T(8,128)(2,1)S(1)} async-done(((bf16[16,64,336]{2,1,0:T(8,128)(2,1)}), bf16[16,64,336]{2,1,0:T(8,128)(2,1)S(1)}, u32[]{:S(2)}, u32[]{:S(2)}) %all-to-all-start.3) | async-done | bytes 688160 | tf_op jit(solution)/shard_map/all_to_all | solution.py:543
  133.4 0.7 shard_map.90
  (46 shorter events, 3.5 us)
Async XLA Ops:
  0.7 0.8 copy-start
  1.6 25.8 %copy-start.1 = (f32[4,256]{1,0:T(4,128)S(1)}, f32[4,256]{1,0:T(4,128)}, u32[]{:S(2)}) copy-start(f32[4,256]{1,0:T(4,128)} %logits_ref) | copy-start | bytes 12292
  1.6 25.8 %copy-start.2 = (s32[4,256]{1,0:T(4,128)S(1)}, s32[4,256]{1,0:T(4,128)}, u32[]{:S(2)}) copy-start(s32[4,256]{1,0:T(4,128)} %ids_ref.1) | copy-start | bytes 12292
  23.2 20.3 %collective-permute-start.1 = (bf16[64,5376]{1,0:T(8,128)(2,1)S(1)}, bf16[64,5376]{1,0:T(8,128)(2,1)S(1)}, u32[]{:S(2)}, u32[]{:S(2)}) collective-permute-start(bf16[64,5376]{1,0:T(8,128)(2,1)S(1)} %shard_map.76.own), channel_id=1, source_target_pairs={{0,32},{16,48},{32,64},{48,80},{64,96},{80,112},{96,0},{112,16},{1... | collective-permute-start | bytes 2064392 | tf_op jit(solution)/shard_map/ppermute | solution.py:483
  25.2 18.3 %collective-permute-start.2 = (bf16[64,5376]{1,0:T(8,128)(2,1)S(1)}, bf16[64,5376]{1,0:T(8,128)(2,1)S(1)}, u32[]{:S(2)}, u32[]{:S(2)}) collective-permute-start(bf16[64,5376]{1,0:T(8,128)(2,1)S(1)} %shard_map.76.own), channel_id=1, source_target_pairs={{0,96},{16,112},{32,0},{48,16},{64,32},{80,48},{96,64},{112,80},{1... | collective-permute-start | bytes 2064392 | tf_op jit(solution)/shard_map/ppermute | solution.py:483
  29.0 14.5 %all-to-all-start.1 = ((f32[128,1,64]{2,1,0:T(1,128)}), f32[128,1,64]{2,1,0:T(1,128)S(1)}, u32[]{:S(2)}, u32[]{:S(2)}) async-start(f32[128,1,64]{2,1,0:T(1,128)} %bitcast.3), calls=%async_computation.1 | async-start | bytes 131072 | tf_op jit(solution)/shard_map/all_to_all | solution.py:501
  34.0 13.3 %collective-permute-start = (bf16[64,5376]{1,0:T(8,128)(2,1)S(1)}, bf16[64,5376]{1,0:T(8,128)(2,1)S(1)}, u32[]{:S(2)}, u32[]{:S(2)}) collective-permute-start(bf16[64,5376]{1,0:T(8,128)(2,1)S(1)} %shard_map.76.own), channel_id=1, source_target_pairs={{0,16},{16,0},{32,48},{48,32},{64,80},{80,64},{96,112},{112,96},{1... | collective-permute-start | bytes 2064392 | tf_op jit(solution)/shard_map/ppermute | solution.py:483
  43.5 3.9 %collective-permute-start.3 = (bf16[64,5376]{1,0:T(8,128)(2,1)S(1)}, bf16[64,5376]{1,0:T(8,128)(2,1)S(1)}, u32[]{:S(2)}, u32[]{:S(2)}) collective-permute-start(bf16[64,5376]{1,0:T(8,128)(2,1)S(1)} %collective-permute-done.1.left), channel_id=1, source_target_pairs={{0,16},{16,0},{32,48},{48,32},{64,80},{80,64},{96,112},{112,96},{1... | collective-permute-start | bytes 2064392 | tf_op jit(solution)/shard_map/ppermute | solution.py:483
  43.5 3.9 %collective-permute-start.4 = (bf16[64,5376]{1,0:T(8,128)(2,1)S(1)}, bf16[64,5376]{1,0:T(8,128)(2,1)S(1)}, u32[]{:S(2)}, u32[]{:S(2)}) collective-permute-start(bf16[64,5376]{1,0:T(8,128)(2,1)S(1)} %collective-permute-done.2.right), channel_id=1, source_target_pairs={{0,16},{16,0},{32,48},{48,32},{64,80},{80,64},{96,112},{112,96},{1... | collective-permute-start | bytes 2064392 | tf_op jit(solution)/shard_map/ppermute | solution.py:483
  44.0 12.5 %collective-permute-start.5 = (bf16[32,5376]{1,0:T(8,128)(2,1)S(1)}, bf16[32,5376]{1,0:T(8,128)(2,1)S(1)}, u32[]{:S(2)}, u32[]{:S(2)}) collective-permute-start(bf16[32,5376]{1,0:T(8,128)(2,1)S(1)} %slice.36), channel_id=1, source_target_pairs={{0,32},{16,48},{32,64},{48,80},{64,96},{80,112},{96,0},{112,16},{1... | collective-permute-start | bytes 1032200 | tf_op jit(solution)/shard_map/ppermute | solution.py:483
  45.2 11.3 %collective-permute-start.6 = (bf16[32,5376]{1,0:T(8,128)(2,1)S(1)}, bf16[32,5376]{1,0:T(8,128)(2,1)S(1)}, u32[]{:S(2)}, u32[]{:S(2)}) collective-permute-start(bf16[32,5376]{1,0:T(8,128)(2,1)S(1)} %slice.37), channel_id=1, source_target_pairs={{0,96},{16,112},{32,0},{48,16},{64,32},{80,48},{96,64},{112,80},{1... | collective-permute-start | bytes 1032200 | tf_op jit(solution)/shard_map/ppermute | solution.py:483
  56.5 2.0 %collective-permute-start.7 = (bf16[32,5376]{1,0:T(8,128)(2,1)S(1)}, bf16[32,5376]{1,0:T(8,128)(2,1)S(1)}, u32[]{:S(2)}, u32[]{:S(2)}) collective-permute-start(bf16[32,5376]{1,0:T(8,128)(2,1)S(1)} %collective-permute-done.5.far_a), channel_id=1, source_target_pairs={{0,16},{16,0},{32,48},{48,32},{64,80},{80,64},{96,112},{112,96},{1... | collective-permute-start | bytes 1032200 | tf_op jit(solution)/shard_map/ppermute | solution.py:483
  56.6 2.1 %collective-permute-start.8 = (bf16[32,5376]{1,0:T(8,128)(2,1)S(1)}, bf16[32,5376]{1,0:T(8,128)(2,1)S(1)}, u32[]{:S(2)}, u32[]{:S(2)}) collective-permute-start(bf16[32,5376]{1,0:T(8,128)(2,1)S(1)} %collective-permute-done.6.far_b), channel_id=1, source_target_pairs={{0,16},{16,0},{32,48},{48,32},{64,80},{80,64},{96,112},{112,96},{1... | collective-permute-start | bytes 1032200 | tf_op jit(solution)/shard_map/ppermute | solution.py:483
  82.3 4.0 %collective-permute-start.9 = (bf16[64,5376]{1,0:T(8,128)(2,1)S(1)}, bf16[64,5376]{1,0:T(8,128)(2,1)S(1)}, u32[]{:S(2)}, u32[]{:S(2)}) collective-permute-start(bf16[64,5376]{1,0:T(8,128)(2,1)S(1)} %get-tuple-element.62), channel_id=1, source_target_pairs={{0,16},{16,0},{32,48},{48,32},{64,80},{80,64},{96,112},{112,96},{1... | collective-permute-start | bytes 2064392 | tf_op jit(solution)/shard_map/ppermute | solution.py:483
  85.7 4.1 %collective-permute-start.13 = (bf16[64,5376]{1,0:T(8,128)(2,1)S(1)}, bf16[64,5376]{1,0:T(8,128)(2,1)S(1)}, u32[]{:S(2)}, u32[]{:S(2)}) collective-permute-start(bf16[64,5376]{1,0:T(8,128)(2,1)S(1)} %get-tuple-element.64), channel_id=1, source_target_pairs={{0,16},{16,0},{32,48},{48,32},{64,80},{80,64},{96,112},{112,96},{1... | collective-permute-start | bytes 2064392 | tf_op jit(solution)/shard_map/ppermute | solution.py:483
  86.5 11.3 %collective-permute-start.11 = (bf16[32,5376]{1,0:T(8,128)(2,1)S(1)}, bf16[32,5376]{1,0:T(8,128)(2,1)S(1)}, u32[]{:S(2)}, u32[]{:S(2)}) collective-permute-start(bf16[32,5376]{1,0:T(8,128)(2,1)S(1)} %get-tuple-element.89), channel_id=1, source_target_pairs={{0,32},{16,48},{32,64},{48,80},{64,96},{80,112},{96,0},{112,16},{1... | collective-permute-start | bytes 1032200 | tf_op jit(solution)/shard_map/ppermute | solution.py:483
  87.4 10.6 %collective-permute-start.12 = (bf16[32,5376]{1,0:T(8,128)(2,1)S(1)}, bf16[32,5376]{1,0:T(8,128)(2,1)S(1)}, u32[]{:S(2)}, u32[]{:S(2)}) collective-permute-start(bf16[32,5376]{1,0:T(8,128)(2,1)S(1)} %get-tuple-element.88), channel_id=1, source_target_pairs={{0,96},{16,112},{32,0},{48,16},{64,32},{80,48},{96,64},{112,80},{1... | collective-permute-start | bytes 1032200 | tf_op jit(solution)/shard_map/ppermute | solution.py:483
  92.3 5.8 %collective-permute-start.10 = (bf16[64,5376]{1,0:T(8,128)(2,1)S(1)}, bf16[64,5376]{1,0:T(8,128)(2,1)S(1)}, u32[]{:S(2)}, u32[]{:S(2)}) collective-permute-start(bf16[64,5376]{1,0:T(8,128)(2,1)S(1)} %get-tuple-element.67), channel_id=1, source_target_pairs={{0,16},{16,0},{32,48},{48,32},{64,80},{80,64},{96,112},{112,96},{1... | collective-permute-start | bytes 2064392 | tf_op jit(solution)/shard_map/ppermute | solution.py:483
  94.9 15.3 %collective-permute-start.16 = (bf16[64,5376]{1,0:T(8,128)(2,1)S(1)}, bf16[64,5376]{1,0:T(8,128)(2,1)S(1)}, u32[]{:S(2)}, u32[]{:S(2)}) collective-permute-start(bf16[64,5376]{1,0:T(8,128)(2,1)S(1)} %get-tuple-element.74), channel_id=1, source_target_pairs={{0,16},{16,0},{32,48},{48,32},{64,80},{80,64},{96,112},{112,96},{1... | collective-permute-start | bytes 2064392 | tf_op jit(solution)/shard_map/ppermute | solution.py:483
  95.5 14.7 %collective-permute-start.17 = (bf16[32,5376]{1,0:T(8,128)(2,1)S(1)}, bf16[32,5376]{1,0:T(8,128)(2,1)S(1)}, u32[]{:S(2)}, u32[]{:S(2)}) collective-permute-start(bf16[32,5376]{1,0:T(8,128)(2,1)S(1)} %get-tuple-element.86), channel_id=1, source_target_pairs={{0,96},{16,112},{32,0},{48,16},{64,32},{80,48},{96,64},{112,80},{1... | collective-permute-start | bytes 1032200 | tf_op jit(solution)/shard_map/ppermute | solution.py:483
  97.7 12.5 %collective-permute-start.18 = (bf16[32,5376]{1,0:T(8,128)(2,1)S(1)}, bf16[32,5376]{1,0:T(8,128)(2,1)S(1)}, u32[]{:S(2)}, u32[]{:S(2)}) collective-permute-start(bf16[32,5376]{1,0:T(8,128)(2,1)S(1)} %get-tuple-element.87), channel_id=1, source_target_pairs={{0,32},{16,48},{32,64},{48,80},{64,96},{80,112},{96,0},{112,16},{1... | collective-permute-start | bytes 1032200 | tf_op jit(solution)/shard_map/ppermute | solution.py:483
  98.4 17.1 %collective-permute-start.14 = (bf16[32,5376]{1,0:T(8,128)(2,1)S(1)}, bf16[32,5376]{1,0:T(8,128)(2,1)S(1)}, u32[]{:S(2)}, u32[]{:S(2)}) collective-permute-start(bf16[32,5376]{1,0:T(8,128)(2,1)S(1)} %get-tuple-element.85), channel_id=1, source_target_pairs={{0,32},{16,48},{32,64},{48,80},{64,96},{80,112},{96,0},{112,16},{1... | collective-permute-start | bytes 1032200 | tf_op jit(solution)/shard_map/ppermute | solution.py:483
  98.5 17.0 %collective-permute-start.15 = (bf16[32,5376]{1,0:T(8,128)(2,1)S(1)}, bf16[32,5376]{1,0:T(8,128)(2,1)S(1)}, u32[]{:S(2)}, u32[]{:S(2)}) collective-permute-start(bf16[32,5376]{1,0:T(8,128)(2,1)S(1)} %get-tuple-element.84), channel_id=1, source_target_pairs={{0,96},{16,112},{32,0},{48,16},{64,32},{80,48},{96,64},{112,80},{1... | collective-permute-start | bytes 1032200 | tf_op jit(solution)/shard_map/ppermute | solution.py:483
  116.7 16.7 %all-to-all-start.3 = ((bf16[16,64,336]{2,1,0:T(8,128)(2,1)}), bf16[16,64,336]{2,1,0:T(8,128)(2,1)S(1)}, u32[]{:S(2)}, u32[]{:S(2)}) async-start(bf16[16,64,336]{2,1,0:T(8,128)(2,1)} %shard_map.89), calls=%async_computation.3 | async-start | bytes 1572864 | tf_op jit(solution)/shard_map/all_to_all | solution.py:543

commit v4 on v3

--- a/solution.py
+++ b/solution.py
@@ -9,7 +9,6 @@
 
 loss_scale = 64.0
 SLOTS = 6
-OFFSETS = (0, 3, 1, 2)
 LANES = 128
 COLS = 768
 ANY = pl.BlockSpec(memory_space=pl.ANY)
@@ -18,6 +17,11 @@
 SCALARS = pl.BlockSpec(memory_space=pltpu.SMEM)
 VMEM_LIMIT = 16 * 1024 * 1024
 BOTH = ("seq", "vocab")
+
+
+def plane(pos, slot):
+    z, core = pos[0], pos[1]
+    return (z + (0, 3 - 2 * core, 1 + 2 * core, 2)[slot]) % 4
 
 
 def params():
@@ -131,19 +135,19 @@
     return jnp.where(row == 0, lse, jnp.where(row == 1, mean, jnp.where(row == 2, cross, 0.0)))
 
 
-def first_kernel(pos, got, source, own, own2, left, left2, right, right2, w, out, target, held, teach, sems):
-    z, core = pos[0], pos[1]
-    count = sems.shape[0]
-    chunk = source.shape[0] // count
+def first_kernel(pos, got, source, own, own2, next1, next2, w, out, target, held, teach, sems):
+    core = pos[1]
+    pieces = (slice(0, 1024),)
     copies = [
-        pltpu.make_async_copy(source.at[pl.ds(k * chunk, chunk)], w.at[pl.ds(k * chunk, chunk)], sems.at[k])
-        for k in range(count)
+        pltpu.make_async_copy(
+            source.at[pl.ds(at.start, at.stop - at.start)], w.at[pl.ds(at.start, at.stop - at.start)], sems.at[k]
+        )
+        for k, at in enumerate(pieces)
     ]
-    for copy in copies:
-        copy.start()
-    for slot, mine, other in ((0, own, own2), (1, left, left2), (2, right, right2)):
-        held[pl.ds(pl.multiple_of(slot * 128 + core * 64, 64), 64)] = mine[...]
-        held[pl.ds(pl.multiple_of(slot * 128 + (1 - core) * 64, 64), 64)] = other[...]
+    copies[0].start()
+    mine, other = core * 64, (1 - core) * 64
+    for block, row in ((own, mine), (own2, other), (next1, 128 + mine), (next2, 128 + other)):
+        held[pl.ds(pl.multiple_of(row, 64), 64)] = block[...]
     flipped = got[...].T
     source_row = lax.broadcasted_iota(jnp.int32, (LANES, 4 * LANES), 0)
     token = lax.broadcasted_iota(jnp.int32, (LANES, 4 * LANES), 1)
@@ -156,24 +160,31 @@
         )
     for block in range(4):
         teach[block] = spread[:, block * LANES : (block + 1) * LANES]
-    rows = 64
-
-    @pl.loop(0, w.shape[0] // rows)
-    def _(step):
-        base = pl.multiple_of(step * rows, rows)
-        word = (lax.broadcasted_iota(jnp.int32, (rows, LANES), 0) + step * rows).astype(jnp.float32)
-        for slot in range(4):
-            info = teach[(z + OFFSETS[slot]) % 4]
+    rows = 32
+    low_iota = lax.broadcasted_iota(jnp.int32, (rows, LANES), 0).astype(jnp.float32)
+    for slot in range(4):
+        info = teach[plane(pos, slot)]
+        groups, values = [], []
+        for k in range(SLOTS):
+            index = info[8 + k : 9 + k]
+            group = jnp.floor(index * (1.0 / rows))
+            groups.append(group)
+            values.append(jnp.where(low_iota == index - group * rows, info[k : k + 1], 0.0))
+
+        @pl.loop(0, w.shape[0] // rows, unroll=4)
+        def _(step):
+            number = jnp.full((1, LANES), step, jnp.int32).astype(jnp.float32)
             dense = jnp.zeros((rows, LANES), jnp.float32)
-            for k in range(SLOTS):
-                dense = dense + jnp.where(word == info[8 + k : 9 + k], info[k : k + 1], 0.0)
-            target[slot, pl.ds(base, rows)] = dense
-
-    for k in range(count):
+            for group, value in zip(groups, values):
+                dense = dense + jnp.where(group == number, value, 0.0)
+            target[slot, pl.ds(pl.multiple_of(step * rows, rows), rows)] = dense
+
+    for k, at in enumerate(pieces):
         copies[k].wait()
-        at = slice(k * chunk, (k + 1) * chunk)
+        if k + 1 < len(pieces):
+            copies[k + 1].start()
         logits = dot_nt(w[at], held[...])
-        for slot in range(3):
+        for slot in range(2):
             out[slot, at] = logits[:, slot * LANES : (slot + 1) * LANES]
 
 
@@ -181,17 +192,17 @@
     vocab, width = source.shape
     return pl.pallas_call(
         first_kernel,
-        in_specs=[SCALARS, WHOLE, FAR] + [WHOLE] * 6,
+        in_specs=[SCALARS, WHOLE, FAR] + [WHOLE] * 4,
         out_specs=[WHOLE] * 4,
         out_shape=[
             pltpu.VMEM((vocab, width), jnp.bfloat16),
-            jax.ShapeDtypeStruct((3, vocab, LANES), jnp.float32),
+            jax.ShapeDtypeStruct((2, vocab, LANES), jnp.float32),
             jax.ShapeDtypeStruct((4, vocab, LANES), jnp.float32),
-            jax.ShapeDtypeStruct((3 * LANES, width), jnp.bfloat16),
+            jax.ShapeDtypeStruct((2 * LANES, width), jnp.bfloat16),
         ],
-        scratch_shapes=[pltpu.VMEM((4, 16, LANES), jnp.float32), pltpu.SemaphoreType.DMA((2,))],
-        compiler_params=params(),
-        cost_estimate=cost(1000, 1000),
+        scratch_shapes=[pltpu.VMEM((4, 16, LANES), jnp.float32), pltpu.SemaphoreType.DMA((1,))],
+        compiler_params=params(),
+        cost_estimate=cost(1e11, 1e9),
     )(pos, got, pltpu.with_memory_space_constraint(source, pltpu.HBM), *blocks)
 
 
@@ -212,8 +223,8 @@
 
 
 def stats_kernel(pos, logits, target, send):
-    for slot in range(3):
-        fill_send(send, (pos[0] + OFFSETS[slot]) % 4, local_stats(logits[slot], target[slot]))
+    for slot in range(2):
+        fill_send(send, plane(pos, slot), local_stats(logits[slot], target[slot]))
 
 
 def near_stats(pos, logits, target):
@@ -227,16 +238,19 @@
     )(pos, logits, target)
 
 
-def last_kernel(pos, w, target, early, far_a, far_b, far_a2, far_b2, out, send, held):
-    z, core = pos[0], pos[1]
+def last_kernel(pos, w, target, early, back1, back2, far, far2, out, send, held):
+    core = pos[1]
     mine, other = core * 64, (1 - core) * 64
-    for block, row in ((far_a, mine), (far_b, mine + 32), (far_a2, other), (far_b2, other + 32)):
-        held[pl.ds(pl.multiple_of(row, 32), 32)] = block[...]
-    out[...] = dot_nt(w[...], held[...])
+    for block, row in ((back1, other), (back2, mine), (far, 128 + mine), (far2, 128 + other)):
+        held[pl.ds(pl.multiple_of(row, 64), 64)] = block[...]
+    logits = dot_nt(w[...], held[...])
     for block in range(5):
         at = slice(block * LANES, (block + 1) * LANES)
         send[:, at] = early[:, at]
-    fill_send(send, (z + OFFSETS[3]) % 4, local_stats(out[...], target[3]))
+    for slot in range(2):
+        out[slot] = logits[:, slot * LANES : (slot + 1) * LANES]
+    for slot in range(2):
+        fill_send(send, plane(pos, 2 + slot), local_stats(out[slot], target[2 + slot]))
 
 
 def last_logits(pos, w, target, early, blocks):
@@ -246,12 +260,12 @@
         in_specs=[SCALARS] + [WHOLE] * 7,
         out_specs=[WHOLE] * 3,
         out_shape=[
-            jax.ShapeDtypeStruct((vocab, LANES), jnp.float32),
+            jax.ShapeDtypeStruct((2, vocab, LANES), jnp.float32),
             jax.ShapeDtypeStruct((LANES, 5 * LANES), jnp.float32),
-            jax.ShapeDtypeStruct((LANES, width), jnp.bfloat16),
+            jax.ShapeDtypeStruct((2 * LANES, width), jnp.bfloat16),
         ],
         compiler_params=params(),
-        cost_estimate=cost(2 * vocab * width * 128, vocab * width * 2),
+        cost_estimate=cost(2 * vocab * width * 256, vocab * width * 2),
     )(pos, w, target, early, *blocks)
 
 
@@ -259,14 +273,17 @@
     return loss_scale * (jnp.exp(logits - lse) - target)
 
 
-def split_rows(pos, acc, at, base, mine_out, other_out):
-    core = pos[1]
-    mine_out[:, at] = acc[pl.ds(pl.multiple_of(base + core * 64, 64), 64)]
-    other_out[:, at] = acc[pl.ds(pl.multiple_of(base + (1 - core) * 64, 64), 64)].astype(jnp.bfloat16)
-
-
-def far_grad_kernel(pos, stats, logits, target, w, mine_out, other_out, grad_out, lse_out, loss_out, acc):
-    z = pos[0]
+def split_dot(left, w, mine_out, other_out):
+    for tile in range(w.shape[1] // COLS):
+        at = slice(tile * COLS, (tile + 1) * COLS)
+        grad = jnp.dot(left[...], w[:, at], preferred_element_type=jnp.float32)
+        for slot in range(left.shape[0] // LANES):
+            to, base = slice(slot * 64, (slot + 1) * 64), slot * LANES
+            mine_out[to, at] = grad[base : base + 64]
+            other_out[to, at] = grad[base + 64 : base + LANES].astype(jnp.bfloat16)
+
+
+def far_grad_kernel(pos, stats, logits, target, w, mine_out, other_out, grad_out, lse_out, loss_out, flipped, left):
     parts = stats[:, : 4 * LANES]
     peak = jnp.max(parts, axis=0, keepdims=True)
     lse = peak + jnp.log(jnp.sum(jnp.exp(parts - peak), axis=0, keepdims=True))
@@ -281,14 +298,14 @@
     lse4 = peak + jnp.log(total)
     row = lax.broadcasted_iota(jnp.int32, (8, LANES), 0)
     loss_out[...] = jnp.where(row == 0, lse4 - cross, lse4 - mean)
-    far = lse_out[(z + OFFSETS[3]) % 4]
-    grad = grad_of(logits[...], far[0:1], target[3])
+    far = lse_out[plane(pos, 3)]
+    grad = grad_of(logits[1], far[0:1], target[3])
     grad_out[...] = grad.astype(jnp.bfloat16)
-    left = grad.T.astype(jnp.bfloat16)
-    for tile in range(w.shape[1] // COLS):
-        at = slice(tile * COLS, (tile + 1) * COLS)
-        acc[...] = jnp.dot(left, w[:, at], preferred_element_type=jnp.float32)
-        split_rows(pos, acc, at, 0, mine_out, other_out)
+    core = pos[1]
+    flipped[...] = grad.T.astype(jnp.bfloat16)
+    left[:64, :] = flipped[pl.ds(pl.multiple_of(core * 64, 64), 64)]
+    left[64:, :] = flipped[pl.ds(pl.multiple_of((1 - core) * 64, 64), 64)]
+    split_dot(left, w, mine_out, other_out)
 
 
 def far_grad(pos, stats, logits, target, w):
@@ -304,71 +321,67 @@
             jax.ShapeDtypeStruct((4, 8, LANES), jnp.float32),
             jax.ShapeDtypeStruct((8, LANES), jnp.float32),
         ],
-        scratch_shapes=[pltpu.VMEM((LANES, COLS), jnp.float32)],
+        scratch_shapes=[pltpu.VMEM((LANES, vocab), jnp.bfloat16)] * 2,
         compiler_params=params(),
         cost_estimate=cost(2 * vocab * width * 128, vocab * width * 2),
     )(pos, stats, logits, target, w)
 
 
-def grads_kernel(pos, logits, target, lse, far, wide_out, first_out, second_out, own_out):
-    z = pos[0]
-    for slot in range(3):
-        row = lse[(z + OFFSETS[slot]) % 4]
-        grad = grad_of(logits[slot], row[0:1], target[slot])
+def grads_kernel(pos, logits, last, target, lse, far, wide_out, first_out, second_out, flipped):
+    core = pos[1]
+    mine, other = pl.ds(pl.multiple_of(core * 64, 64), 64), pl.ds(pl.multiple_of((1 - core) * 64, 64), 64)
+    for slot in (2, 1, 0):
+        part = last[0] if slot == 2 else logits[slot]
+        grad = grad_of(part, lse[plane(pos, slot)][0:1], target[slot])
         wide_out[:, slot * LANES : (slot + 1) * LANES] = grad.astype(jnp.bfloat16)
-        flipped = grad.T.astype(jnp.bfloat16)
-        if slot == 0:
-            own_out[...] = flipped
+        flipped[...] = grad.T.astype(jnp.bfloat16)
+        if slot == 2:
+            first_out[:64, :] = flipped[other]
+            second_out[:64, :] = flipped[mine]
+        elif slot == 1:
+            first_out[64:, :] = flipped[mine]
+            second_out[64:128, :] = flipped[other]
         else:
-            for core in range(2):
-                low = flipped[core * 64 : core * 64 + 32]
-                high = flipped[core * 64 + 32 : core * 64 + 64]
-                to = slice(core * 64 + (slot - 1) * 32, core * 64 + slot * 32)
-                first_out[to, :] = low if slot == 1 else high
-                second_out[to, :] = high if slot == 1 else low
+            second_out[128:192, :] = flipped[mine]
+            second_out[192:, :] = flipped[other]
     wide_out[:, 3 * LANES :] = far[...]
 
 
-def near_grads(pos, logits, target, lse, far):
+def near_grads(pos, logits, last, target, lse, far):
     vocab = far.shape[0]
     return pl.pallas_call(
         grads_kernel,
-        in_specs=[SCALARS] + [WHOLE] * 4,
-        out_specs=[WHOLE] * 4,
-        out_shape=[jax.ShapeDtypeStruct((vocab, 4 * LANES), jnp.bfloat16)]
-        + [jax.ShapeDtypeStruct((LANES, vocab), jnp.bfloat16)] * 3,
+        in_specs=[SCALARS] + [WHOLE] * 5,
+        out_specs=[WHOLE] * 3,
+        out_shape=[
+            jax.ShapeDtypeStruct((vocab, 4 * LANES), jnp.bfloat16),
+            jax.ShapeDtypeStruct((LANES, vocab), jnp.bfloat16),
+            jax.ShapeDtypeStruct((2 * LANES, vocab), jnp.bfloat16),
+        ],
+        scratch_shapes=[pltpu.VMEM((LANES, vocab), jnp.bfloat16)],
         compiler_params=params(),
         cost_estimate=cost(2e6, 5e6),
-    )(pos, logits, target, lse, far)
-
-
-def near_kernel(pos, left, w, mine_out, other_out, acc):
-    core = pos[1]
-    for tile in range(w.shape[1] // COLS):
-        at = slice(tile * COLS, (tile + 1) * COLS)
-        acc[...] = jnp.dot(left[...], w[:, at], preferred_element_type=jnp.float32)
-        for slot in range(left.shape[0] // LANES):
-            to = slice(slot * 64, (slot + 1) * 64)
-            mine_out[to, at] = acc[pl.ds(pl.multiple_of(slot * 128 + core * 64, 64), 64)]
-            part = acc[pl.ds(pl.multiple_of(slot * 128 + (1 - core) * 64, 64), 64)]
-            other_out[to, at] = part.astype(jnp.bfloat16)
-
-
-def near_grad(pos, left, w):
+    )(pos, logits, last, target, lse, far)
+
+
+def near_kernel(left, w, mine_out, other_out):
+    split_dot(left, w, mine_out, other_out)
+
+
+def near_grad(left, w):
     vocab, width = w.shape
     tokens = left.shape[0]
     return pl.pallas_call(
         near_kernel,
-        in_specs=[SCALARS] + [WHOLE] * 2,
+        in_specs=[WHOLE] * 2,
         out_specs=[WHOLE] * 2,
         out_shape=[
             jax.ShapeDtypeStruct((tokens // 2, width), jnp.float32),
             jax.ShapeDtypeStruct((tokens // 2, width), jnp.bfloat16),
         ],
-        scratch_shapes=[pltpu.VMEM((tokens, COLS), jnp.float32)],
         compiler_params=params(),
         cost_estimate=cost(2 * vocab * width * tokens, vocab * width * 2),
-    )(pos, left, w)
+    )(left, w)
 
 
 def weight_kernel(grad, near, far, out):
@@ -393,60 +406,56 @@
     )(grad, near, far)
 
 
-def widen_kernel(upper, lower, out):
-    out[0] = upper[...].astype(jnp.float32)
-    out[1] = lower[...].astype(jnp.float32)
-
-
-def widen(upper, lower):
+def widen_kernel(block, out):
+    out[...] = block[...].astype(jnp.float32)
+
+
+def widen(block):
     return pl.pallas_call(
         widen_kernel,
-        in_specs=[WHOLE] * 2,
-        out_specs=WHOLE,
-        out_shape=jax.ShapeDtypeStruct((2, *upper.shape), jnp.float32),
+        in_specs=[WHOLE],
+        out_specs=WHOLE,
+        out_shape=jax.ShapeDtypeStruct(block.shape, jnp.float32),
         compiler_params=params(),
         cost_estimate=cost(1e11, 1e9),
-    )(upper, lower)
-
-
-def gather_own_kernel(mine, swap, left_b, right_b, out):
-    half = left_b.shape[0]
+    )(block)
+
+
+def gather_own_kernel(mine, swap, across, out):
+    rows = out.shape[0]
     f32 = jnp.float32
-    out[:half] = mine[:half] + swap[:half].astype(f32) + left_b[...].astype(f32)
-    out[half:] = mine[half:] + swap[half:].astype(f32) + right_b[...].astype(f32)
-
-
-def gather_own(*pieces):
+    out[...] = mine[rows:] + swap[rows:].astype(f32) + across[...].astype(f32)
+
+
+def gather_own(mine, swap, across):
     return pl.pallas_call(
         gather_own_kernel,
-        in_specs=[WHOLE] * 4,
-        out_specs=WHOLE,
-        out_shape=jax.ShapeDtypeStruct(pieces[0].shape, jnp.float32),
+        in_specs=[WHOLE] * 3,
+        out_specs=WHOLE,
+        out_shape=jax.ShapeDtypeStruct(across.shape, jnp.float32),
         compiler_params=params(),
         cost_estimate=cost(1e11, 1e9),
-    )(*pieces)
-
-
-def fold_kernel(near, right_a, left_a, out, total):
-    half = right_a.shape[0]
-    total[:half] = (near[:half] + right_a[...].astype(jnp.float32)).astype(jnp.bfloat16)
-    total[half:] = (near[half:] + left_a[...].astype(jnp.float32)).astype(jnp.bfloat16)
+    )(mine, swap, across)
+
+
+def fold_kernel(near, arrived, out, total):
+    total[...] = (near[...] + arrived[...].astype(jnp.float32)).astype(jnp.bfloat16)
     part = out.shape[2]
     for index in range(out.shape[0]):
         out[index] = total[:, index * part : (index + 1) * part]
 
 
-def fold(count, pieces):
-    rows, width = pieces[0].shape
+def fold(count, near, arrived):
+    rows, width = near.shape
     return pl.pallas_call(
         fold_kernel,
-        in_specs=[WHOLE] * 3,
+        in_specs=[WHOLE] * 2,
         out_specs=WHOLE,
         out_shape=jax.ShapeDtypeStruct((count, rows, width // count), jnp.bfloat16),
         scratch_shapes=[pltpu.VMEM((rows, width), jnp.bfloat16)],
         compiler_params=params(),
         cost_estimate=cost(2e6, 4e6),
-    )(*pieces)
+    )(near, arrived)
 
 
 def sum_kernel(parts, out):
@@ -475,8 +484,8 @@
     tok_rows, feat_part = hidden.shape
     seq_index = lax.axis_index("seq")
     pos = jnp.stack([seq_index // 2, seq_index % 2]).astype(jnp.int32)
-    up = [(i, (i + 2) % seq_count) for i in range(seq_count)]
-    down = [(i, (i - 2) % seq_count) for i in range(seq_count)]
+    ring = [(i, (i + 2 - 4 * (i % 2)) % seq_count) for i in range(seq_count)]
+    cross = [(i, (i + 2 - 4 * (i % 2)) % seq_count ^ 1) for i in range(seq_count)]
     twin = [(i, i ^ 1) for i in range(seq_count)]
 
     def move(x, perm):
@@ -487,63 +496,54 @@
 
     f32 = jnp.float32
     bf16 = jnp.bfloat16
-    half = tok_rows // 2
 
     hidden, pos = lax.optimization_barrier((hidden, pos))
     spread = copies_of(hidden, vocab_count)
     spread = lax.all_to_all(spread, "vocab", split_axis=0, concat_axis=0, tiled=True)
     own = join_parts(spread)
-    left = move(own, up)
-    right = move(own, down)
+    next1 = move(own, ring)
     own2 = move(own, twin)
-    teacher_logits, own = lax.optimization_barrier((teacher_logits, own))
+    next2 = move(own2, ring)
+    teacher_logits, own2 = lax.optimization_barrier((teacher_logits, own2))
     teach = teacher_rows(owners, vocab_rows, teacher_logits, teacher_ids)
     got = lax.all_to_all(teach, BOTH, split_axis=0, concat_axis=0, tiled=True)
-    left, right = after((left, right), got)
-    far_a = move(left[:half], up)
-    far_b = move(right[half:], down)
-    near_blocks = (own, own2, left, move(left, twin), right, move(right, twin))
+    far = move(next1, ring)
+    near_blocks = (own, own2, next1, next2)
     weight, logits, target, near_rows = first_logits(pos, got, head_weight, near_blocks)
-    far_a, far_b = after((far_a, far_b), logits)
+    back = (move(next1, twin), move(next2, twin))
+    far = after(far, logits)
     early = near_stats(pos, logits, target)
-    far_blocks = (far_a, far_b, move(far_a, twin), move(far_b, twin))
-    far_logits, send, far_rows = last_logits(pos, weight, target, early, far_blocks)
+    last, send, last_rows = last_logits(pos, weight, target, early, (*back, far, move(far, twin)))
     stats = lax.all_to_all(send, BOTH, split_axis=0, concat_axis=0, tiled=True)
 
-    far_mine, far_other, grad_far, lse, loss = far_grad(pos, stats, far_logits, target, weight)
+    far_mine, far_other, grad_far, lse, loss = far_grad(pos, stats, last, target, weight)
     far_swap = move(far_other, twin)
-    wide, first_left, second_left, own_left = near_grads(pos, logits, target, lse, grad_far)
-    first_mine, first_other = near_grad(pos, first_left, weight)
+    wide, first_left, second_left = near_grads(pos, logits, last, target, lse, grad_far)
+    first_mine, first_other = near_grad(first_left, weight)
     first_swap = move(first_other, twin)
     far_sum = (far_mine + far_swap.astype(f32)).astype(bf16)
-    go_up = move(far_sum[:half], up)
-    go_down = move(far_sum[half:], down)
+    passed = move(far_sum, ring)
     second_left = after(second_left, far_sum, first_other)
-    second_mine, second_other = near_grad(pos, second_left, weight)
+    second_mine, second_other = near_grad(second_left, weight)
     second_swap = move(second_other, twin)
-    own_left = after(own_left, second_other)
-    own_mine, own_other = near_grad(pos, own_left, weight)
-    own_swap = move(own_other, twin)
     first_sum = (first_mine + first_swap.astype(f32)).astype(bf16)
-    left_b_part, right_b_part = first_sum[:half], first_sum[half:]
-    left_b = move(left_b_part, down)
-    right_b = move(right_b_part, up)
-    second_sum = second_mine + second_swap.astype(f32)
-    go_up, go_down = after((go_up, go_down), right_b_part, left_b_part)
-    passed = widen(go_up, go_down)
-    left_a_part = (second_sum[:half] + passed[1]).astype(bf16)
-    right_a_part = (second_sum[half:] + passed[0]).astype(bf16)
-    left_a = move(left_a_part, down)
-    right_a = move(right_a_part, up)
-    grad_weight = weight_grad(after(wide, left_a_part, right_a_part), near_rows, far_rows)
-    left_b, right_b = after((left_b, right_b), grad_weight)
-    gathered = gather_own(own_mine, own_swap, left_b, right_b)
-    (right_a, left_a), gathered = lax.optimization_barrier(((right_a, left_a), gathered))
-    parts = fold(vocab_count, (gathered, right_a, left_a))
+    first = move(first_sum, cross)
+    passed = widen(after(passed, first_sum))
+    second_sum = second_mine[:tok_rows] + second_swap[:tok_rows].astype(f32)
+    second_sum = (second_sum + passed).astype(bf16)
+    second = move(second_sum, ring)
+    rows = teacher_logits.shape[0]
+    loss = after(loss, second_sum)
+    cross_entropy, entropy = loss[0, :rows], loss[1, :rows]
+    wide = after(wide, second_sum, cross_entropy, entropy)
+    grad_weight = weight_grad(wide, near_rows, last_rows)
+    first = after(first, grad_weight)
+    gathered = gather_own(second_mine, second_swap, first)
+    second, gathered = lax.optimization_barrier((second, gathered))
+    parts = fold(vocab_count, gathered, second)
     parts = lax.all_to_all(parts, "vocab", split_axis=0, concat_axis=0, tiled=True)
     grad_hidden = sum_parts(parts)
-    rows = teacher_logits.shape[0]
-    return loss[0, :rows], loss[1, :rows], grad_hidden, grad_weight
+    return cross_entropy, entropy, grad_hidden, grad_weight
 
 
 def solution(mesh):

time: 134 us -> 127 us (0.948)
  blocking collectives: 37.9 us -> 52.4 us
  starting transfers between devices: 26 us -> 14.3 us
  waiting for transfers between devices: 29.7 us -> 24 us
  Pallas kernels: 37.1 us -> 33.2 us
    all_to_all x0 -> x1, blocking collectives: none -> 15.4 us  [body(): lax.all_to_all(parts, 'vocab', split_axis=0, concat_axis=0, tiled=True)]
    all_to_all x1 -> x0, waiting for transfers between devices: 12.6 us -> none  [body(): lax.all_to_all(parts, 'vocab', split_axis=0, concat_axis=0, tiled=True)]
    ppermute x19 -> x13, starting transfers between devices: 17.3 us -> 7.65 us  [move(): return lax.ppermute(x, 'seq', perm)]
    ppermute x19 -> x13, waiting for transfers between devices: 7.8 us -> 15.3 us  [move(): return lax.ppermute(x, 'seq', perm)]
    pallas_call x8 -> x7, Pallas kernels: 18.6 us -> 14.7 us  [the longest x1 8.36 us: first_logits(): pl.pallas_call(first_kernel, in_specs=[SCALARS, WHOLE, FAR] + [WHOLE] * 4...]
    all_to_all x1 -> x0, starting transfers between devices: 3.61 us -> none  [body(): lax.all_to_all(parts, 'vocab', split_axis=0, concat_axis=0, tiled=True)]
    all_to_all x1, starting transfers between devices: 5.03 us -> 6.67 us  [body(): got = lax.all_to_all(teach, BOTH, split_axis=0, concat_axis=0, tiled=True)]
  transfers between devices with their start and end apart: 21 -> 14, of which waited for: 6 -> 7; matrix products, arithmetic and copies ran while one was open for 1% -> 1% of each run, Pallas kernels for 21% -> 20%
where the time goes in v4:
time: 127 us
  blocking collectives  52.4 us (41%)
  Pallas kernels  33.2 us (26%)
  waiting for transfers between devices  24 us (19%)
  starting transfers between devices  14.3 us (11%)
  local copies, waits for them, and re-layouts  1.69 us (1%)
    all_to_all x1, blocking collectives, body(): lax.all_to_all(spread, 'vocab', split_axis=0, concat_axis=0, tiled=True)  21.3 us
    all_to_all x1, blocking collectives, body(): stats = lax.all_to_all(send, BOTH, split_axis=0, concat_axis=0, tiled=True)  15.7 us
    all_to_all x1, blocking collectives, body(): lax.all_to_all(parts, 'vocab', split_axis=0, concat_axis=0, tiled=True)  15.4 us
    ppermute x13, waiting for transfers between devices, move(): return lax.ppermute(x, 'seq', perm)  15.3 us
    all_to_all x1, waiting for transfers between devices, body(): got = lax.all_to_all(teach, BOTH, split_axis=0, concat_axis=0, tiled=True)  8.76 us
    pallas_call x1, Pallas kernels, first_logits(): pl.pallas_call(first_kernel, in_specs=[SCALARS, WHOLE, FAR] + [WHOLE] * 4...  8.36 us
    pallas_call x1, Pallas kernels, weight_grad(): pl.pallas_call(weight_kernel, grid=(vocab // rows,), in_specs=[pl.BlockSp...  7.98 us
    ppermute x13, starting transfers between devices, move(): return lax.ppermute(x, 'seq', perm)  7.65 us
  transfers between devices with their start and end apart: 14, of which 7 were waited for; matrix products, arithmetic and copies ran while one was open for 1% of the time, Pallas kernels for 20%

profile of v4, /device:TPU:0, one launch (start us, length us, event | category | flops | bytes accessed | tf_op | source)
XLA Modules:
  0.0 127.0 jit_solution(17885663591006531025)
XLA Ops:
  0.7 0.8 copy-done
  1.6 21.3 %all_to_all.32.parts = bf16[16,64,336]{2,1,0:T(8,128)(2,1)S(1)} all-to-all(bf16[16,64,336]{2,1,0:T(8,128)(2,1)S(1)} %shard_map.75), channel_id=1, replica_groups=mesh['seq'=8,'vocab'=16] {'vocab'}, dimensions={0} | all-to-all | bytes 1376256 | tf_op jit(solution)/shard_map/all_to_all | solution.py:502
  22.9 0.3 shard_map.76.own
  23.3 2.0 %collective-permute-start.1 = (bf16[64,5376]{1,0:T(8,128)(2,1)S(1)}, bf16[64,5376]{1,0:T(8,128)(2,1)S(1)}, u32[]{:S(2)}, u32[]{:S(2)}) collective-permute-start(bf16[64,5376]{1,0:T(8,128)(2,1)S(1)} %shard_map.76.own), channel_id=1, source_target_pairs={{0,32},{16,112},{32,64},{48,16},{64,96},{80,48},{96,0},{112,80},{1... | collective-permute-start | bytes 2064392 | tf_op jit(solution)/shard_map/ppermute | solution.py:492
  25.6 1.9 %collective-permute-start.2 = (bf16[64,5376]{1,0:T(8,128)(2,1)}, bf16[64,5376]{1,0:T(8,128)(2,1)S(1)}, u32[]{:S(2)}, u32[]{:S(2)}) collective-permute-start(bf16[64,5376]{1,0:T(8,128)(2,1)} %collective-permute-done.own2), channel_id=1, source_target_pairs={{0,32},{16,112},{32,64},{48,16},{64,96},{80,48},{96,0},{112,80},{1... | collective-permute-start | bytes 2064392 | tf_op jit(solution)/shard_map/ppermute | solution.py:492
  27.5 1.6 %shard_map.77 = f32[128,64]{1,0:T(8,128)} custom-call(f32[4,256]{1,0:T(4,128)S(1)} %copy-done.1, s32[4,256]{1,0:T(4,128)S(1)} %copy-done.2), custom_call_target="tpu_custom_call" | custom-call | flops 4000000 | bytes 40000 | tf_op jit(solution)/shard_map/pallas_call | solution.py:79
  29.1 6.7 %all-to-all-start.1 = ((f32[128,1,64]{2,1,0:T(1,128)}), f32[128,1,64]{2,1,0:T(1,128)S(1)}, u32[]{:S(2)}, u32[]{:S(2)}) async-start(f32[128,1,64]{2,1,0:T(1,128)} %bitcast.3), calls=%async_computation.1 | async-start | bytes 131072 | tf_op jit(solution)/shard_map/all_to_all | solution.py:509
  35.7 0.6 collective-permute-done.1.next1
  36.3 0.7 collective-permute-start.5
  37.0 8.8 %all-to-all-done.1 = f32[128,1,64]{2,1,0:T(1,128)S(1)} async-done(((f32[128,1,64]{2,1,0:T(1,128)}), f32[128,1,64]{2,1,0:T(1,128)S(1)}, u32[]{:S(2)}, u32[]{:S(2)}) %all-to-all-start.1) | async-done | bytes 32800 | tf_op jit(solution)/shard_map/all_to_all | solution.py:509
  45.8 8.4 %shard_map.78 = (bf16[1024,5376]{1,0:T(8,128)(2,1)S(1)}, f32[2,1024,128]{2,1,0:T(8,128)S(1)}, f32[4,1024,128]{2,1,0:T(8,128)S(1)}, bf16[256,5376]{1,0:T(8,128)(2,1)S(1)}) custom-call(s32[2]{0:T(128)S(1)} %pad_add_fusion.pos, f32[128,64]{1,0:T(8,128)S(1)} %bitcast.16, bf16[1024,5376]{1,0:T(8,128)(2,1)} %source.1, bf16[64,5376]{1,0:T(8,128)(2,1)S(1)} %shard_map.76.own, ...), custom_call_target="tpu_custom_call" | custom-call | flops 99999997952 | bytes 1000000000 | tf_op jit(solution)/shard_map/pallas_call | solution.py:193
  54.3 0.5 collective-permute-start.6
  54.8 1.2 shard_map.79.early
  56.0 0.4 collective-permute-done.4.back2
  56.4 1.0 collective-permute-done.6.far2
  57.4 4.2 %shard_map.80 = (f32[2,1024,128]{2,1,0:T(8,128)S(1)}, f32[128,640]{1,0:T(8,128)S(1)}, bf16[256,5376]{1,0:T(8,128)(2,1)S(1)}) custom-call(s32[2]{0:T(128)S(1)} %pad_add_fusion.pos, bf16[1024,5376]{1,0:T(8,128)(2,1)S(1)} %get-tuple-element.39.w, f32[4,1024,128]{2,1,0:T(8,128)S(1)} %get-tuple-element.40.target, f32[128,640]{1,0:T(8,128)S(1)} %shard_map.79.early, ...), custom_call_target="tpu_custom_call" | custom-call | flops 2818572288 | bytes 11010048 | tf_op jit(solution)/shard_map/pallas_call | solution.py:258
  61.6 0.3 copy.9
  62.0 15.7 %all_to_all.33 = f32[128,1,640]{2,1,0:T(1,128)S(1)} all-to-all(f32[128,1,640]{2,1,0:T(1,128)S(1)} %copy.9), channel_id=1, replica_groups=mesh['seq'=8,'vocab'=16] {'seq','vocab'}, dimensions={0} | all-to-all | bytes 655360 | tf_op jit(solution)/shard_map/all_to_all | solution.py:517
  77.7 2.4 %shard_map.81 = (f32[64,5376]{1,0:T(8,128)S(1)}, bf16[64,5376]{1,0:T(8,128)(2,1)S(1)}, bf16[1024,128]{1,0:T(8,128)(2,1)S(1)}, f32[4,8,128]{2,1,0:T(8,128)S(1)}, f32[8,128]{1,0:T(8,128)S(1)}) custom-call(s32[2]{0:T(128)S(1)} %pad_add_fusion.pos, f32[128,640]{1,0:T(8,128)S(1)} %bitcast.14, f32[2,1024,128]{2,1,0:T(8,128)S(1)} %get-tuple-element.44.logits.last, ...), custom_call_target="tpu_custom_call" | custom-call | flops 1409286144 | bytes 11010048 | tf_op jit(solution)/shard_map/pallas_call | solution.py:313
  80.2 1.0 shard_map.82
  81.2 1.6 %shard_map.83 = (f32[64,5376]{1,0:T(8,128)S(1)}, bf16[64,5376]{1,0:T(8,128)(2,1)S(1)}) custom-call(bf16[128,1024]{1,0:T(8,128)(2,1)S(1)} %get-tuple-element.51.left, bf16[1024,5376]{1,0:T(8,128)(2,1)S(1)} %get-tuple-element.39.w), custom_call_target="tpu_custom_call" | custom-call | flops 1409286144 | bytes 11010048 | tf_op jit(solution)/shard_map/pallas_call | solution.py:374
  82.9 0.6 collective-permute-start.10
  83.6 0.9 collective-permute-start.9
  84.5 3.0 %shard_map.84 = (f32[128,5376]{1,0:T(8,128)S(1)}, bf16[128,5376]{1,0:T(8,128)(2,1)S(1)}) custom-call(bf16[256,1024]{1,0:T(8,128)(2,1)S(1)} %get-tuple-element.53.left, bf16[1024,5376]{1,0:T(8,128)(2,1)S(1)} %get-tuple-element.39.w), custom_call_target="tpu_custom_call" | custom-call | flops 2818572288 | bytes 11010048 | tf_op jit(solution)/shard_map/pallas_call | solution.py:374
  87.8 0.6 collective-permute-start.12
  88.4 7.4 %collective-permute-done.9.block = bf16[64,5376]{1,0:T(8,128)(2,1)S(1)} collective-permute-done((bf16[64,5376]{1,0:T(8,128)(2,1)S(1)}, bf16[64,5376]{1,0:T(8,128)(2,1)S(1)}, u32[]{:S(2)}, u32[]{:S(2)}) %collective-permute-start.9) | collective-permute-done | bytes 688160 | tf_op jit(solution)/shard_map/ppermute | solution.py:492
  96.2 0.5 slice_bitcast_fusion
  96.8 8.0 %shard_map.86 = bf16[1024,5376]{1,0:T(8,128)(2,1)} custom-call(bf16[1024,512]{1,0:T(8,128)(2,1)S(1)} %get-tuple-element.60.grad, bf16[256,5376]{1,0:T(8,128)(2,1)S(1)} %get-tuple-element.61.near, bf16[256,5376]{1,0:T(8,128)(2,1)S(1)} %get-tuple-element.62.far), custom_call_target="tpu_custom_call" | custom-call | flops 5637144576 | bytes 16515072 | tf_op jit(solution)/shard_map/pallas_call | solution.py:398
  105.0 5.6 %collective-permute-done.11.arrived = bf16[64,5376]{1,0:T(8,128)(2,1)S(1)} collective-permute-done((bf16[64,5376]{1,0:T(8,128)(2,1)S(1)}, bf16[64,5376]{1,0:T(8,128)(2,1)S(1)}, u32[]{:S(2)}, u32[]{:S(2)}) %collective-permute-start.11) | collective-permute-done | bytes 688160 | tf_op jit(solution)/shard_map/ppermute | solution.py:492
  110.6 0.3 shard_map.88
  110.9 15.4 %all_to_all.34.parts = bf16[16,64,336]{2,1,0:T(8,128)(2,1)S(1)} all-to-all(bf16[16,64,336]{2,1,0:T(8,128)(2,1)S(1)} %shard_map.88), channel_id=1, replica_groups=mesh['seq'=8,'vocab'=16] {'vocab'}, dimensions={0} | all-to-all | bytes 1376256 | tf_op jit(solution)/shard_map/all_to_all | solution.py:544
  126.3 0.7 shard_map.89
  (27 shorter events, 1.7 us)
Async XLA Ops:
  0.7 0.8 copy-start
  1.6 25.9 %copy-start.1 = (f32[4,256]{1,0:T(4,128)S(1)}, f32[4,256]{1,0:T(4,128)}, u32[]{:S(2)}) copy-start(f32[4,256]{1,0:T(4,128)} %logits_ref) | copy-start | bytes 12292
  1.6 25.9 %copy-start.2 = (s32[4,256]{1,0:T(4,128)S(1)}, s32[4,256]{1,0:T(4,128)}, u32[]{:S(2)}) copy-start(s32[4,256]{1,0:T(4,128)} %ids_ref.1) | copy-start | bytes 12292
  23.2 2.4 %collective-permute-start = (bf16[64,5376]{1,0:T(8,128)(2,1)S(1)}, bf16[64,5376]{1,0:T(8,128)(2,1)}, u32[]{:S(2)}, u32[]{:S(2)}) collective-permute-start(bf16[64,5376]{1,0:T(8,128)(2,1)S(1)} %shard_map.76.own), channel_id=1, source_target_pairs={{0,16},{16,0},{32,48},{48,32},{64,80},{80,64},{96,112},{112,96},{1... | collective-permute-start | bytes 2064392 | tf_op jit(solution)/shard_map/ppermute | solution.py:492
  23.3 13.0 %collective-permute-start.1 = (bf16[64,5376]{1,0:T(8,128)(2,1)S(1)}, bf16[64,5376]{1,0:T(8,128)(2,1)S(1)}, u32[]{:S(2)}, u32[]{:S(2)}) collective-permute-start(bf16[64,5376]{1,0:T(8,128)(2,1)S(1)} %shard_map.76.own), channel_id=1, source_target_pairs={{0,32},{16,112},{32,64},{48,16},{64,96},{80,48},{96,0},{112,80},{1... | collective-permute-start | bytes 2064392 | tf_op jit(solution)/shard_map/ppermute | solution.py:492
  25.6 20.3 %collective-permute-start.2 = (bf16[64,5376]{1,0:T(8,128)(2,1)}, bf16[64,5376]{1,0:T(8,128)(2,1)S(1)}, u32[]{:S(2)}, u32[]{:S(2)}) collective-permute-start(bf16[64,5376]{1,0:T(8,128)(2,1)} %collective-permute-done.own2), channel_id=1, source_target_pairs={{0,32},{16,112},{32,64},{48,16},{64,96},{80,48},{96,0},{112,80},{1... | collective-permute-start | bytes 2064392 | tf_op jit(solution)/shard_map/ppermute | solution.py:492
  29.1 16.8 %all-to-all-start.1 = ((f32[128,1,64]{2,1,0:T(1,128)}), f32[128,1,64]{2,1,0:T(1,128)S(1)}, u32[]{:S(2)}, u32[]{:S(2)}) async-start(f32[128,1,64]{2,1,0:T(1,128)} %bitcast.3), calls=%async_computation.1 | async-start | bytes 131072 | tf_op jit(solution)/shard_map/all_to_all | solution.py:509
  36.3 19.7 %collective-permute-start.3 = (bf16[64,5376]{1,0:T(8,128)(2,1)S(1)}, bf16[64,5376]{1,0:T(8,128)(2,1)S(1)}, u32[]{:S(2)}, u32[]{:S(2)}) collective-permute-start(bf16[64,5376]{1,0:T(8,128)(2,1)S(1)} %collective-permute-done.1.next1), channel_id=1, source_target_pairs={{0,16},{16,0},{32,48},{48,32},{64,80},{80,64},{96,112},{112,96},{1... | collective-permute-start | bytes 2064392 | tf_op jit(solution)/shard_map/ppermute | solution.py:492
  36.3 17.9 %collective-permute-start.5 = (bf16[64,5376]{1,0:T(8,128)(2,1)S(1)}, bf16[64,5376]{1,0:T(8,128)(2,1)S(1)}, u32[]{:S(2)}, u32[]{:S(2)}) collective-permute-start(bf16[64,5376]{1,0:T(8,128)(2,1)S(1)} %collective-permute-done.1.next1), channel_id=1, source_target_pairs={{0,32},{16,112},{32,64},{48,16},{64,96},{80,48},{96,0},{112,80},{1... | collective-permute-start | bytes 2064392 | tf_op jit(solution)/shard_map/ppermute | solution.py:492
  54.2 2.2 %collective-permute-start.4 = (bf16[64,5376]{1,0:T(8,128)(2,1)S(1)}, bf16[64,5376]{1,0:T(8,128)(2,1)S(1)}, u32[]{:S(2)}, u32[]{:S(2)}) collective-permute-start(bf16[64,5376]{1,0:T(8,128)(2,1)S(1)} %collective-permute-done.2.next2), channel_id=1, source_target_pairs={{0,16},{16,0},{32,48},{48,32},{64,80},{80,64},{96,112},{112,96},{1... | collective-permute-start | bytes 2064392 | tf_op jit(solution)/shard_map/ppermute | solution.py:492
  54.3 3.1 %collective-permute-start.6 = (bf16[64,5376]{1,0:T(8,128)(2,1)S(1)}, bf16[64,5376]{1,0:T(8,128)(2,1)S(1)}, u32[]{:S(2)}, u32[]{:S(2)}) collective-permute-start(bf16[64,5376]{1,0:T(8,128)(2,1)S(1)} %collective-permute-done.5.far), channel_id=1, source_target_pairs={{0,16},{16,0},{32,48},{48,32},{64,80},{80,64},{96,112},{112,96},{1... | collective-permute-start | bytes 2064392 | tf_op jit(solution)/shard_map/ppermute | solution.py:492
  80.1 3.3 %collective-permute-start.7 = (bf16[64,5376]{1,0:T(8,128)(2,1)S(1)}, bf16[64,5376]{1,0:T(8,128)(2,1)S(1)}, u32[]{:S(2)}, u32[]{:S(2)}) collective-permute-start(bf16[64,5376]{1,0:T(8,128)(2,1)S(1)} %get-tuple-element.50), channel_id=1, source_target_pairs={{0,16},{16,0},{32,48},{48,32},{64,80},{80,64},{96,112},{112,96},{1... | collective-permute-start | bytes 2064392 | tf_op jit(solution)/shard_map/ppermute | solution.py:492
  82.9 4.8 %collective-permute-start.10 = (bf16[64,5376]{1,0:T(8,128)(2,1)S(1)}, bf16[64,5376]{1,0:T(8,128)(2,1)S(1)}, u32[]{:S(2)}, u32[]{:S(2)}) collective-permute-start(bf16[64,5376]{1,0:T(8,128)(2,1)S(1)} %get-tuple-element.52), channel_id=1, source_target_pairs={{0,16},{16,0},{32,48},{48,32},{64,80},{80,64},{96,112},{112,96},{1... | collective-permute-start | bytes 2064392 | tf_op jit(solution)/shard_map/ppermute | solution.py:492
  83.6 12.2 %collective-permute-start.9 = (bf16[64,5376]{1,0:T(8,128)(2,1)S(1)}, bf16[64,5376]{1,0:T(8,128)(2,1)S(1)}, u32[]{:S(2)}, u32[]{:S(2)}) collective-permute-start(bf16[64,5376]{1,0:T(8,128)(2,1)S(1)} %add_convert_fusion.2), channel_id=1, source_target_pairs={{0,32},{16,112},{32,64},{48,16},{64,96},{80,48},{96,0},{112,80},{1... | collective-permute-start | bytes 2064392 | tf_op jit(solution)/shard_map/ppermute | solution.py:492
  87.5 8.4 %collective-permute-start.8 = (bf16[128,5376]{1,0:T(8,128)(2,1)S(1)}, bf16[128,5376]{1,0:T(8,128)(2,1)S(1)}, u32[]{:S(2)}, u32[]{:S(2)}) collective-permute-start(bf16[128,5376]{1,0:T(8,128)(2,1)S(1)} %get-tuple-element.55), channel_id=1, source_target_pairs={{0,16},{16,0},{32,48},{48,32},{64,80},{80,64},{96,112},{112,96},{1... | collective-permute-start | bytes 4128776 | tf_op jit(solution)/shard_map/ppermute | solution.py:492
  87.8 17.0 %collective-permute-start.12 = (bf16[64,5376]{1,0:T(8,128)(2,1)S(1)}, bf16[64,5376]{1,0:T(8,128)(2,1)S(1)}, u32[]{:S(2)}, u32[]{:S(2)}) collective-permute-start(bf16[64,5376]{1,0:T(8,128)(2,1)S(1)} %add_convert_fusion.1), channel_id=1, source_target_pairs={{0,48},{16,96},{32,80},{48,0},{64,112},{80,32},{96,16},{112,64},{1... | collective-permute-start | bytes 2064392 | tf_op jit(solution)/shard_map/ppermute | solution.py:492
  96.2 14.4 %collective-permute-start.11 = (bf16[64,5376]{1,0:T(8,128)(2,1)S(1)}, bf16[64,5376]{1,0:T(8,128)(2,1)S(1)}, u32[]{:S(2)}, u32[]{:S(2)}) collective-permute-start(bf16[64,5376]{1,0:T(8,128)(2,1)S(1)} %add_convert_fusion), channel_id=1, source_target_pairs={{0,32},{16,112},{32,64},{48,16},{64,96},{80,48},{96,0},{112,80},{1... | collective-permute-start | bytes 2064392 | tf_op jit(solution)/shard_map/ppermute | solution.py:492

commit v5 on v4

--- a/solution.py
+++ b/solution.py
@@ -137,7 +137,8 @@
 
 def first_kernel(pos, got, source, own, own2, next1, next2, w, out, target, held, teach, sems):
     core = pos[1]
-    pieces = (slice(0, 1024),)
+    half = source.shape[0] // 2
+    pieces = (slice(0, half), slice(half, 2 * half))
     copies = [
         pltpu.make_async_copy(
             source.at[pl.ds(at.start, at.stop - at.start)], w.at[pl.ds(at.start, at.stop - at.start)], sems.at[k]
@@ -183,7 +184,7 @@
         copies[k].wait()
         if k + 1 < len(pieces):
             copies[k + 1].start()
-        logits = dot_nt(w[at], held[...])
+        logits = dot_nt(held[...], w[at]).T
         for slot in range(2):
             out[slot, at] = logits[:, slot * LANES : (slot + 1) * LANES]
 
@@ -200,7 +201,7 @@
             jax.ShapeDtypeStruct((4, vocab, LANES), jnp.float32),
             jax.ShapeDtypeStruct((2 * LANES, width), jnp.bfloat16),
         ],
-        scratch_shapes=[pltpu.VMEM((4, 16, LANES), jnp.float32), pltpu.SemaphoreType.DMA((1,))],
+        scratch_shapes=[pltpu.VMEM((4, 16, LANES), jnp.float32), pltpu.SemaphoreType.DMA((2,))],
         compiler_params=params(),
         cost_estimate=cost(1e11, 1e9),
     )(pos, got, pltpu.with_memory_space_constraint(source, pltpu.HBM), *blocks)
@@ -510,9 +511,9 @@
     far = move(next1, ring)
     near_blocks = (own, own2, next1, next2)
     weight, logits, target, near_rows = first_logits(pos, got, head_weight, near_blocks)
-    back = (move(next1, twin), move(next2, twin))
+    back = (move(next1, twin), move(after(next2, got), twin))
     far = after(far, logits)
-    early = near_stats(pos, logits, target)
+    early = near_stats(pos, after(logits, back[1]), target)
     last, send, last_rows = last_logits(pos, weight, target, early, (*back, far, move(far, twin)))
     stats = lax.all_to_all(send, BOTH, split_axis=0, concat_axis=0, tiled=True)
 

time: 127 us -> 126 us (level)
  transfers between devices with their start and end apart: 14 -> 14, of which waited for: 7 -> 6; matrix products, arithmetic and copies ran while one was open for 1% -> 1% of each run, Pallas kernels for 20% -> 20%
where the time goes in v5:
time: 126 us
  blocking collectives  52.4 us (42%)
  Pallas kernels  32.9 us (26%)
  waiting for transfers between devices  23.3 us (18%)
  starting transfers between devices  14.2 us (11%)
  local copies, waits for them, and re-layouts  1.69 us (1%)
    all_to_all x1, blocking collectives, body(): lax.all_to_all(spread, 'vocab', split_axis=0, concat_axis=0, tiled=True)  21.3 us
    all_to_all x1, blocking collectives, body(): stats = lax.all_to_all(send, BOTH, split_axis=0, concat_axis=0, tiled=True)  15.7 us
    all_to_all x1, blocking collectives, body(): lax.all_to_all(parts, 'vocab', split_axis=0, concat_axis=0, tiled=True)  15.4 us
    ppermute x13, waiting for transfers between devices, move(): return lax.ppermute(x, 'seq', perm)  14.4 us
    all_to_all x1, waiting for transfers between devices, body(): got = lax.all_to_all(teach, BOTH, split_axis=0, concat_axis=0, tiled=True)  8.89 us
    pallas_call x1, Pallas kernels, first_logits(): pl.pallas_call(first_kernel, in_specs=[SCALARS, WHOLE, FAR] + [WHOLE] * 4...  8.07 us
    pallas_call x1, Pallas kernels, weight_grad(): pl.pallas_call(weight_kernel, grid=(vocab // rows,), in_specs=[pl.BlockSp...  7.98 us
    ppermute x13, starting transfers between devices, move(): return lax.ppermute(x, 'seq', perm)  7.53 us
  transfers between devices with their start and end apart: 14, of which 6 were waited for; matrix products, arithmetic and copies ran while one was open for 1% of the time, Pallas kernels for 20%

profile of v5, /device:TPU:0, one launch (start us, length us, event | category | flops | bytes accessed | tf_op | source)
XLA Modules:
  0.0 125.9 jit_solution(15474200421453407633)
XLA Ops:
  0.7 0.8 copy-done
  1.6 21.3 %all_to_all.32.parts = bf16[16,64,336]{2,1,0:T(8,128)(2,1)S(1)} all-to-all(bf16[16,64,336]{2,1,0:T(8,128)(2,1)S(1)} %shard_map.75), channel_id=1, replica_groups=mesh['seq'=8,'vocab'=16] {'vocab'}, dimensions={0} | all-to-all | bytes 1376256 | tf_op jit(solution)/shard_map/all_to_all | solution.py:503
  22.9 0.3 shard_map.76.own
  23.3 2.0 %collective-permute-start.1 = (bf16[64,5376]{1,0:T(8,128)(2,1)S(1)}, bf16[64,5376]{1,0:T(8,128)(2,1)S(1)}, u32[]{:S(2)}, u32[]{:S(2)}) collective-permute-start(bf16[64,5376]{1,0:T(8,128)(2,1)S(1)} %shard_map.76.own), channel_id=1, source_target_pairs={{0,32},{16,112},{32,64},{48,16},{64,96},{80,48},{96,0},{112,80},{1... | collective-permute-start | bytes 2064392 | tf_op jit(solution)/shard_map/ppermute | solution.py:493
  25.4 1.9 %collective-permute-start.2 = (bf16[64,5376]{1,0:T(8,128)(2,1)S(1)}, bf16[64,5376]{1,0:T(8,128)(2,1)}, u32[]{:S(2)}, u32[]{:S(2)}) collective-permute-start(bf16[64,5376]{1,0:T(8,128)(2,1)S(1)} %collective-permute-done.own2), channel_id=1, source_target_pairs={{0,32},{16,112},{32,64},{48,16},{64,96},{80,48},{96,0},{112,80},{1... | collective-permute-start | bytes 2064392 | tf_op jit(solution)/shard_map/ppermute | solution.py:493
  27.3 1.6 %shard_map.77 = f32[128,64]{1,0:T(8,128)} custom-call(f32[4,256]{1,0:T(4,128)S(1)} %copy-done.1, s32[4,256]{1,0:T(4,128)S(1)} %copy-done.2), custom_call_target="tpu_custom_call" | custom-call | flops 4000000 | bytes 40000 | tf_op jit(solution)/shard_map/pallas_call | solution.py:79
  28.9 6.7 %all-to-all-start.1 = ((f32[128,1,64]{2,1,0:T(1,128)}), f32[128,1,64]{2,1,0:T(1,128)S(1)}, u32[]{:S(2)}, u32[]{:S(2)}) async-start(f32[128,1,64]{2,1,0:T(1,128)} %bitcast.3), calls=%async_computation.1 | async-start | bytes 131072 | tf_op jit(solution)/shard_map/all_to_all | solution.py:510
  35.6 0.7 collective-permute-done.1.next1
  36.3 0.6 collective-permute-start.5
  36.9 8.9 %all-to-all-done.1 = f32[128,1,64]{2,1,0:T(1,128)S(1)} async-done(((f32[128,1,64]{2,1,0:T(1,128)}), f32[128,1,64]{2,1,0:T(1,128)S(1)}, u32[]{:S(2)}, u32[]{:S(2)}) %all-to-all-start.1) | async-done | bytes 32800 | tf_op jit(solution)/shard_map/all_to_all | solution.py:510
  45.8 8.1 %shard_map.78 = (bf16[1024,5376]{1,0:T(8,128)(2,1)S(1)}, f32[2,1024,128]{2,1,0:T(8,128)S(1)}, f32[4,1024,128]{2,1,0:T(8,128)S(1)}, bf16[256,5376]{1,0:T(8,128)(2,1)S(1)}) custom-call(s32[2]{0:T(128)S(1)} %pad_add_fusion.pos, f32[128,64]{1,0:T(8,128)S(1)} %bitcast.16, bf16[1024,5376]{1,0:T(8,128)(2,1)} %source.1, bf16[64,5376]{1,0:T(8,128)(2,1)S(1)} %shard_map.76.own, ...), custom_call_target="tpu_custom_call" | custom-call | flops 99999997952 | bytes 1000000000 | tf_op jit(solution)/shard_map/pallas_call | solution.py:194
  53.9 0.6 collective-permute-start.6
  54.5 1.2 shard_map.79.early
  55.7 0.6 collective-permute-done.6.far2
  56.3 4.2 %shard_map.80 = (f32[2,1024,128]{2,1,0:T(8,128)S(1)}, f32[128,640]{1,0:T(8,128)S(1)}, bf16[256,5376]{1,0:T(8,128)(2,1)S(1)}) custom-call(s32[2]{0:T(128)S(1)} %pad_add_fusion.pos, bf16[1024,5376]{1,0:T(8,128)(2,1)S(1)} %get-tuple-element.41.w, f32[4,1024,128]{2,1,0:T(8,128)S(1)} %get-tuple-element.42.target, f32[128,640]{1,0:T(8,128)S(1)} %shard_map.79.early, ...), custom_call_target="tpu_custom_call" | custom-call | flops 2818572288 | bytes 11010048 | tf_op jit(solution)/shard_map/pallas_call | solution.py:259
  60.5 0.3 copy.9
  60.8 15.7 %all_to_all.33 = f32[128,1,640]{2,1,0:T(1,128)S(1)} all-to-all(f32[128,1,640]{2,1,0:T(1,128)S(1)} %copy.9), channel_id=1, replica_groups=mesh['seq'=8,'vocab'=16] {'seq','vocab'}, dimensions={0} | all-to-all | bytes 655360 | tf_op jit(solution)/shard_map/all_to_all | solution.py:518
  76.6 2.4 %shard_map.81 = (f32[64,5376]{1,0:T(8,128)S(1)}, bf16[64,5376]{1,0:T(8,128)(2,1)S(1)}, bf16[1024,128]{1,0:T(8,128)(2,1)S(1)}, f32[4,8,128]{2,1,0:T(8,128)S(1)}, f32[8,128]{1,0:T(8,128)S(1)}) custom-call(s32[2]{0:T(128)S(1)} %pad_add_fusion.pos, f32[128,640]{1,0:T(8,128)S(1)} %bitcast.14, f32[2,1024,128]{2,1,0:T(8,128)S(1)} %get-tuple-element.48.logits.last, ...), custom_call_target="tpu_custom_call" | custom-call | flops 1409286144 | bytes 11010048 | tf_op jit(solution)/shard_map/pallas_call | solution.py:314
  79.1 1.0 shard_map.82
  80.1 1.6 %shard_map.83 = (f32[64,5376]{1,0:T(8,128)S(1)}, bf16[64,5376]{1,0:T(8,128)(2,1)S(1)}) custom-call(bf16[128,1024]{1,0:T(8,128)(2,1)S(1)} %get-tuple-element.55.left, bf16[1024,5376]{1,0:T(8,128)(2,1)S(1)} %get-tuple-element.41.w), custom_call_target="tpu_custom_call" | custom-call | flops 1409286144 | bytes 11010048 | tf_op jit(solution)/shard_map/pallas_call | solution.py:375
  81.7 0.6 collective-permute-start.10
  82.5 0.9 collective-permute-start.9
  83.4 3.0 %shard_map.84 = (f32[128,5376]{1,0:T(8,128)S(1)}, bf16[128,5376]{1,0:T(8,128)(2,1)S(1)}) custom-call(bf16[256,1024]{1,0:T(8,128)(2,1)S(1)} %get-tuple-element.57.left, bf16[1024,5376]{1,0:T(8,128)(2,1)S(1)} %get-tuple-element.41.w), custom_call_target="tpu_custom_call" | custom-call | flops 2818572288 | bytes 11010048 | tf_op jit(solution)/shard_map/pallas_call | solution.py:375
  86.7 0.6 collective-permute-start.12
  87.3 7.4 %collective-permute-done.9.block = bf16[64,5376]{1,0:T(8,128)(2,1)S(1)} collective-permute-done((bf16[64,5376]{1,0:T(8,128)(2,1)S(1)}, bf16[64,5376]{1,0:T(8,128)(2,1)S(1)}, u32[]{:S(2)}, u32[]{:S(2)}) %collective-permute-start.9) | collective-permute-done | bytes 688160 | tf_op jit(solution)/shard_map/ppermute | solution.py:493
  94.8 0.2 add_convert_fusion
  95.1 0.5 slice_bitcast_fusion
  95.6 8.0 %shard_map.86 = bf16[1024,5376]{1,0:T(8,128)(2,1)} custom-call(bf16[1024,512]{1,0:T(8,128)(2,1)S(1)} %get-tuple-element.64.grad, bf16[256,5376]{1,0:T(8,128)(2,1)S(1)} %get-tuple-element.65.near, bf16[256,5376]{1,0:T(8,128)(2,1)S(1)} %get-tuple-element.66.far), custom_call_target="tpu_custom_call" | custom-call | flops 5637144576 | bytes 16515072 | tf_op jit(solution)/shard_map/pallas_call | solution.py:399
  103.9 5.6 %collective-permute-done.11.arrived = bf16[64,5376]{1,0:T(8,128)(2,1)S(1)} collective-permute-done((bf16[64,5376]{1,0:T(8,128)(2,1)S(1)}, bf16[64,5376]{1,0:T(8,128)(2,1)S(1)}, u32[]{:S(2)}, u32[]{:S(2)}) %collective-permute-start.11) | collective-permute-done | bytes 688160 | tf_op jit(solution)/shard_map/ppermute | solution.py:493
  109.4 0.3 shard_map.88
  109.8 15.4 %all_to_all.34.parts = bf16[16,64,336]{2,1,0:T(8,128)(2,1)S(1)} all-to-all(bf16[16,64,336]{2,1,0:T(8,128)(2,1)S(1)} %shard_map.88), channel_id=1, replica_groups=mesh['seq'=8,'vocab'=16] {'vocab'}, dimensions={0} | all-to-all | bytes 1376256 | tf_op jit(solution)/shard_map/all_to_all | solution.py:545
  125.2 0.7 shard_map.89
  (27 shorter events, 1.3 us)
Async XLA Ops:
  0.7 0.8 copy-start
  1.6 25.7 %copy-start.1 = (f32[4,256]{1,0:T(4,128)S(1)}, f32[4,256]{1,0:T(4,128)}, u32[]{:S(2)}) copy-start(f32[4,256]{1,0:T(4,128)} %logits_ref) | copy-start | bytes 12292
  1.6 25.7 %copy-start.2 = (s32[4,256]{1,0:T(4,128)S(1)}, s32[4,256]{1,0:T(4,128)}, u32[]{:S(2)}) copy-start(s32[4,256]{1,0:T(4,128)} %ids_ref.1) | copy-start | bytes 12292
  23.2 2.2 %collective-permute-start = (bf16[64,5376]{1,0:T(8,128)(2,1)S(1)}, bf16[64,5376]{1,0:T(8,128)(2,1)S(1)}, u32[]{:S(2)}, u32[]{:S(2)}) collective-permute-start(bf16[64,5376]{1,0:T(8,128)(2,1)S(1)} %shard_map.76.own), channel_id=1, source_target_pairs={{0,16},{16,0},{32,48},{48,32},{64,80},{80,64},{96,112},{112,96},{1... | collective-permute-start | bytes 2064392 | tf_op jit(solution)/shard_map/ppermute | solution.py:493
  23.3 13.0 %collective-permute-start.1 = (bf16[64,5376]{1,0:T(8,128)(2,1)S(1)}, bf16[64,5376]{1,0:T(8,128)(2,1)S(1)}, u32[]{:S(2)}, u32[]{:S(2)}) collective-permute-start(bf16[64,5376]{1,0:T(8,128)(2,1)S(1)} %shard_map.76.own), channel_id=1, source_target_pairs={{0,32},{16,112},{32,64},{48,16},{64,96},{80,48},{96,0},{112,80},{1... | collective-permute-start | bytes 2064392 | tf_op jit(solution)/shard_map/ppermute | solution.py:493
  25.4 20.4 %collective-permute-start.2 = (bf16[64,5376]{1,0:T(8,128)(2,1)S(1)}, bf16[64,5376]{1,0:T(8,128)(2,1)}, u32[]{:S(2)}, u32[]{:S(2)}) collective-permute-start(bf16[64,5376]{1,0:T(8,128)(2,1)S(1)} %collective-permute-done.own2), channel_id=1, source_target_pairs={{0,32},{16,112},{32,64},{48,16},{64,96},{80,48},{96,0},{112,80},{1... | collective-permute-start | bytes 2064392 | tf_op jit(solution)/shard_map/ppermute | solution.py:493
  28.9 16.9 %all-to-all-start.1 = ((f32[128,1,64]{2,1,0:T(1,128)}), f32[128,1,64]{2,1,0:T(1,128)S(1)}, u32[]{:S(2)}, u32[]{:S(2)}) async-start(f32[128,1,64]{2,1,0:T(1,128)} %bitcast.3), calls=%async_computation.1 | async-start | bytes 131072 | tf_op jit(solution)/shard_map/all_to_all | solution.py:510
  36.3 19.4 %collective-permute-start.4 = (bf16[64,5376]{1,0:T(8,128)(2,1)S(1)}, bf16[64,5376]{1,0:T(8,128)(2,1)S(1)}, u32[]{:S(2)}, u32[]{:S(2)}) collective-permute-start(bf16[64,5376]{1,0:T(8,128)(2,1)S(1)} %collective-permute-done.1.next1), channel_id=1, source_target_pairs={{0,16},{16,0},{32,48},{48,32},{64,80},{80,64},{96,112},{112,96},{1... | collective-permute-start | bytes 2064392 | tf_op jit(solution)/shard_map/ppermute | solution.py:493
  36.3 17.6 %collective-permute-start.5 = (bf16[64,5376]{1,0:T(8,128)(2,1)S(1)}, bf16[64,5376]{1,0:T(8,128)(2,1)S(1)}, u32[]{:S(2)}, u32[]{:S(2)}) collective-permute-start(bf16[64,5376]{1,0:T(8,128)(2,1)S(1)} %collective-permute-done.1.next1), channel_id=1, source_target_pairs={{0,32},{16,112},{32,64},{48,16},{64,96},{80,48},{96,0},{112,80},{1... | collective-permute-start | bytes 2064392 | tf_op jit(solution)/shard_map/ppermute | solution.py:493
  45.8 8.7 %collective-permute-start.3 = (bf16[64,5376]{1,0:T(8,128)(2,1)}, bf16[64,5376]{1,0:T(8,128)(2,1)S(1)}, u32[]{:S(2)}, u32[]{:S(2)}) collective-permute-start(bf16[64,5376]{1,0:T(8,128)(2,1)} %collective-permute-done.2.next2), channel_id=1, source_target_pairs={{0,16},{16,0},{32,48},{48,32},{64,80},{80,64},{96,112},{112,96},{1... | collective-permute-start | bytes 2064392 | tf_op jit(solution)/shard_map/ppermute | solution.py:493
  53.9 2.4 %collective-permute-start.6 = (bf16[64,5376]{1,0:T(8,128)(2,1)S(1)}, bf16[64,5376]{1,0:T(8,128)(2,1)S(1)}, u32[]{:S(2)}, u32[]{:S(2)}) collective-permute-start(bf16[64,5376]{1,0:T(8,128)(2,1)S(1)} %collective-permute-done.5.far), channel_id=1, source_target_pairs={{0,16},{16,0},{32,48},{48,32},{64,80},{80,64},{96,112},{112,96},{1... | collective-permute-start | bytes 2064392 | tf_op jit(solution)/shard_map/ppermute | solution.py:493
  79.0 3.3 %collective-permute-start.7 = (bf16[64,5376]{1,0:T(8,128)(2,1)S(1)}, bf16[64,5376]{1,0:T(8,128)(2,1)S(1)}, u32[]{:S(2)}, u32[]{:S(2)}) collective-permute-start(bf16[64,5376]{1,0:T(8,128)(2,1)S(1)} %get-tuple-element.54), channel_id=1, source_target_pairs={{0,16},{16,0},{32,48},{48,32},{64,80},{80,64},{96,112},{112,96},{1... | collective-permute-start | bytes 2064392 | tf_op jit(solution)/shard_map/ppermute | solution.py:493
  81.7 4.8 %collective-permute-start.10 = (bf16[64,5376]{1,0:T(8,128)(2,1)S(1)}, bf16[64,5376]{1,0:T(8,128)(2,1)S(1)}, u32[]{:S(2)}, u32[]{:S(2)}) collective-permute-start(bf16[64,5376]{1,0:T(8,128)(2,1)S(1)} %get-tuple-element.56), channel_id=1, source_target_pairs={{0,16},{16,0},{32,48},{48,32},{64,80},{80,64},{96,112},{112,96},{1... | collective-permute-start | bytes 2064392 | tf_op jit(solution)/shard_map/ppermute | solution.py:493
  82.5 12.2 %collective-permute-start.9 = (bf16[64,5376]{1,0:T(8,128)(2,1)S(1)}, bf16[64,5376]{1,0:T(8,128)(2,1)S(1)}, u32[]{:S(2)}, u32[]{:S(2)}) collective-permute-start(bf16[64,5376]{1,0:T(8,128)(2,1)S(1)} %add_convert_fusion.2), channel_id=1, source_target_pairs={{0,32},{16,112},{32,64},{48,16},{64,96},{80,48},{96,0},{112,80},{1... | collective-permute-start | bytes 2064392 | tf_op jit(solution)/shard_map/ppermute | solution.py:493
  86.4 8.3 %collective-permute-start.8 = (bf16[128,5376]{1,0:T(8,128)(2,1)S(1)}, bf16[128,5376]{1,0:T(8,128)(2,1)S(1)}, u32[]{:S(2)}, u32[]{:S(2)}) collective-permute-start(bf16[128,5376]{1,0:T(8,128)(2,1)S(1)} %get-tuple-element.59), channel_id=1, source_target_pairs={{0,16},{16,0},{32,48},{48,32},{64,80},{80,64},{96,112},{112,96},{1... | collective-permute-start | bytes 4128776 | tf_op jit(solution)/shard_map/ppermute | solution.py:493
  86.7 16.9 %collective-permute-start.12 = (bf16[64,5376]{1,0:T(8,128)(2,1)S(1)}, bf16[64,5376]{1,0:T(8,128)(2,1)S(1)}, u32[]{:S(2)}, u32[]{:S(2)}) collective-permute-start(bf16[64,5376]{1,0:T(8,128)(2,1)S(1)} %add_convert_fusion.1), channel_id=1, source_target_pairs={{0,48},{16,96},{32,80},{48,0},{64,112},{80,32},{96,16},{112,64},{1... | collective-permute-start | bytes 2064392 | tf_op jit(solution)/shard_map/ppermute | solution.py:493
  95.0 14.4 %collective-permute-start.11 = (bf16[64,5376]{1,0:T(8,128)(2,1)S(1)}, bf16[64,5376]{1,0:T(8,128)(2,1)S(1)}, u32[]{:S(2)}, u32[]{:S(2)}) collective-permute-start(bf16[64,5376]{1,0:T(8,128)(2,1)S(1)} %add_convert_fusion), channel_id=1, source_target_pairs={{0,32},{16,112},{32,64},{48,16},{64,96},{80,48},{96,0},{112,80},{1... | collective-permute-start | bytes 2064392 | tf_op jit(solution)/shard_map/ppermute | solution.py:493

commit v6 on v5

--- a/solution.py
+++ b/solution.py
@@ -524,10 +524,10 @@
     first_swap = move(first_other, twin)
     far_sum = (far_mine + far_swap.astype(f32)).astype(bf16)
     passed = move(far_sum, ring)
-    second_left = after(second_left, far_sum, first_other)
+    first_sum = (first_mine + first_swap.astype(f32)).astype(bf16)
+    second_left = after(second_left, far_sum, first_sum)
     second_mine, second_other = near_grad(second_left, weight)
     second_swap = move(second_other, twin)
-    first_sum = (first_mine + first_swap.astype(f32)).astype(bf16)
     first = move(first_sum, cross)
     passed = widen(after(passed, first_sum))
     second_sum = second_mine[:tok_rows] + second_swap[:tok_rows].astype(f32)

time: 126 us -> 126 us (level)
  transfers between devices with their start and end apart: 14 -> 14, of which waited for: 6 -> 7; matrix products, arithmetic and copies ran while one was open for 1% -> 1% of each run, Pallas kernels for 20% -> 20%
where the time goes in v6:
time: 126 us
  blocking collectives  52.4 us (42%)
  Pallas kernels  32.9 us (26%)
  waiting for transfers between devices  22.1 us (18%)
  starting transfers between devices  15.4 us (12%)
  local copies, waits for them, and re-layouts  1.69 us (1%)
    all_to_all x1, blocking collectives, body(): lax.all_to_all(spread, 'vocab', split_axis=0, concat_axis=0, tiled=True)  21.3 us
    all_to_all x1, blocking collectives, body(): stats = lax.all_to_all(send, BOTH, split_axis=0, concat_axis=0, tiled=True)  15.7 us
    all_to_all x1, blocking collectives, body(): lax.all_to_all(parts, 'vocab', split_axis=0, concat_axis=0, tiled=True)  15.4 us
    ppermute x13, waiting for transfers between devices, move(): return lax.ppermute(x, 'seq', perm)  13.2 us
    all_to_all x1, waiting for transfers between devices, body(): got = lax.all_to_all(teach, BOTH, split_axis=0, concat_axis=0, tiled=True)  8.89 us
    ppermute x13, starting transfers between devices, move(): return lax.ppermute(x, 'seq', perm)  8.77 us
    pallas_call x1, Pallas kernels, first_logits(): pl.pallas_call(first_kernel, in_specs=[SCALARS, WHOLE, FAR] + [WHOLE] * 4...  8.07 us
    pallas_call x1, Pallas kernels, weight_grad(): pl.pallas_call(weight_kernel, grid=(vocab // rows,), in_specs=[pl.BlockSp...  7.96 us
  transfers between devices with their start and end apart: 14, of which 7 were waited for; matrix products, arithmetic and copies ran while one was open for 1% of the time, Pallas kernels for 20%

profile of v6, /device:TPU:0, one launch (start us, length us, event | category | flops | bytes accessed | tf_op | source)
XLA Modules:
  0.0 125.9 jit_solution(2382429656926505223)
XLA Ops:
  0.7 0.8 copy-done
  1.6 21.3 %all_to_all.32.parts = bf16[16,64,336]{2,1,0:T(8,128)(2,1)S(1)} all-to-all(bf16[16,64,336]{2,1,0:T(8,128)(2,1)S(1)} %shard_map.75), channel_id=1, replica_groups=mesh['seq'=8,'vocab'=16] {'vocab'}, dimensions={0} | all-to-all | bytes 1376256 | tf_op jit(solution)/shard_map/all_to_all | solution.py:503
  23.3 2.0 %collective-permute-start.1 = (bf16[64,5376]{1,0:T(8,128)(2,1)S(1)}, bf16[64,5376]{1,0:T(8,128)(2,1)S(1)}, u32[]{:S(2)}, u32[]{:S(2)}) collective-permute-start(bf16[64,5376]{1,0:T(8,128)(2,1)S(1)} %shard_map.76.own), channel_id=1, source_target_pairs={{0,32},{16,112},{32,64},{48,16},{64,96},{80,48},{96,0},{112,80},{1... | collective-permute-start | bytes 2064392 | tf_op jit(solution)/shard_map/ppermute | solution.py:493
  25.4 1.9 %collective-permute-start.2 = (bf16[64,5376]{1,0:T(8,128)(2,1)S(1)}, bf16[64,5376]{1,0:T(8,128)(2,1)}, u32[]{:S(2)}, u32[]{:S(2)}) collective-permute-start(bf16[64,5376]{1,0:T(8,128)(2,1)S(1)} %collective-permute-done.own2), channel_id=1, source_target_pairs={{0,32},{16,112},{32,64},{48,16},{64,96},{80,48},{96,0},{112,80},{1... | collective-permute-start | bytes 2064392 | tf_op jit(solution)/shard_map/ppermute | solution.py:493
  27.3 1.6 %shard_map.77 = f32[128,64]{1,0:T(8,128)} custom-call(f32[4,256]{1,0:T(4,128)S(1)} %copy-done.1, s32[4,256]{1,0:T(4,128)S(1)} %copy-done.2), custom_call_target="tpu_custom_call" | custom-call | flops 4000000 | bytes 40000 | tf_op jit(solution)/shard_map/pallas_call | solution.py:79
  28.9 6.7 %all-to-all-start.1 = ((f32[128,1,64]{2,1,0:T(1,128)}), f32[128,1,64]{2,1,0:T(1,128)S(1)}, u32[]{:S(2)}, u32[]{:S(2)}) async-start(f32[128,1,64]{2,1,0:T(1,128)} %bitcast.3), calls=%async_computation.1 | async-start | bytes 131072 | tf_op jit(solution)/shard_map/all_to_all | solution.py:510
  35.6 0.7 collective-permute-done.1.next1
  36.3 0.6 collective-permute-start.5
  36.9 8.9 %all-to-all-done.1 = f32[128,1,64]{2,1,0:T(1,128)S(1)} async-done(((f32[128,1,64]{2,1,0:T(1,128)}), f32[128,1,64]{2,1,0:T(1,128)S(1)}, u32[]{:S(2)}, u32[]{:S(2)}) %all-to-all-start.1) | async-done | bytes 32800 | tf_op jit(solution)/shard_map/all_to_all | solution.py:510
  45.8 8.1 %shard_map.78 = (bf16[1024,5376]{1,0:T(8,128)(2,1)S(1)}, f32[2,1024,128]{2,1,0:T(8,128)S(1)}, f32[4,1024,128]{2,1,0:T(8,128)S(1)}, bf16[256,5376]{1,0:T(8,128)(2,1)S(1)}) custom-call(s32[2]{0:T(128)S(1)} %pad_add_fusion.pos, f32[128,64]{1,0:T(8,128)S(1)} %bitcast.16, bf16[1024,5376]{1,0:T(8,128)(2,1)} %source.1, bf16[64,5376]{1,0:T(8,128)(2,1)S(1)} %shard_map.76.own, ...), custom_call_target="tpu_custom_call" | custom-call | flops 99999997952 | bytes 1000000000 | tf_op jit(solution)/shard_map/pallas_call | solution.py:194
  53.9 0.6 collective-permute-start.6
  54.5 1.2 shard_map.79.early
  55.7 0.6 collective-permute-done.6.far2
  56.3 4.2 %shard_map.80 = (f32[2,1024,128]{2,1,0:T(8,128)S(1)}, f32[128,640]{1,0:T(8,128)S(1)}, bf16[256,5376]{1,0:T(8,128)(2,1)S(1)}) custom-call(s32[2]{0:T(128)S(1)} %pad_add_fusion.pos, bf16[1024,5376]{1,0:T(8,128)(2,1)S(1)} %get-tuple-element.41.w, f32[4,1024,128]{2,1,0:T(8,128)S(1)} %get-tuple-element.42.target, f32[128,640]{1,0:T(8,128)S(1)} %shard_map.79.early, ...), custom_call_target="tpu_custom_call" | custom-call | flops 2818572288 | bytes 11010048 | tf_op jit(solution)/shard_map/pallas_call | solution.py:259
  60.5 0.3 copy.9
  60.8 15.7 %all_to_all.33 = f32[128,1,640]{2,1,0:T(1,128)S(1)} all-to-all(f32[128,1,640]{2,1,0:T(1,128)S(1)} %copy.9), channel_id=1, replica_groups=mesh['seq'=8,'vocab'=16] {'seq','vocab'}, dimensions={0} | all-to-all | bytes 655360 | tf_op jit(solution)/shard_map/all_to_all | solution.py:518
  76.6 2.4 %shard_map.81 = (f32[64,5376]{1,0:T(8,128)S(1)}, bf16[64,5376]{1,0:T(8,128)(2,1)S(1)}, bf16[1024,128]{1,0:T(8,128)(2,1)S(1)}, f32[4,8,128]{2,1,0:T(8,128)S(1)}, f32[8,128]{1,0:T(8,128)S(1)}) custom-call(s32[2]{0:T(128)S(1)} %pad_add_fusion.pos, f32[128,640]{1,0:T(8,128)S(1)} %bitcast.14, f32[2,1024,128]{2,1,0:T(8,128)S(1)} %get-tuple-element.48.logits.last, ...), custom_call_target="tpu_custom_call" | custom-call | flops 1409286144 | bytes 11010048 | tf_op jit(solution)/shard_map/pallas_call | solution.py:314
  79.1 1.0 shard_map.82
  80.1 1.6 %shard_map.83 = (f32[64,5376]{1,0:T(8,128)S(1)}, bf16[64,5376]{1,0:T(8,128)(2,1)S(1)}) custom-call(bf16[128,1024]{1,0:T(8,128)(2,1)S(1)} %get-tuple-element.55.left, bf16[1024,5376]{1,0:T(8,128)(2,1)S(1)} %get-tuple-element.41.w), custom_call_target="tpu_custom_call" | custom-call | flops 1409286144 | bytes 11010048 | tf_op jit(solution)/shard_map/pallas_call | solution.py:375
  81.7 0.6 collective-permute-start.8
  82.4 0.9 collective-permute-start.10
  83.4 0.7 collective-permute-done.8
  84.2 0.9 collective-permute-start.12
  85.1 3.0 %shard_map.84 = (f32[128,5376]{1,0:T(8,128)S(1)}, bf16[128,5376]{1,0:T(8,128)(2,1)S(1)}) custom-call(bf16[256,1024]{1,0:T(8,128)(2,1)S(1)} %get-tuple-element.58.left, bf16[1024,5376]{1,0:T(8,128)(2,1)S(1)} %get-tuple-element.41.w), custom_call_target="tpu_custom_call" | custom-call | flops 2818572288 | bytes 11010048 | tf_op jit(solution)/shard_map/pallas_call | solution.py:375
  88.2 1.0 collective-permute-start.9
  89.2 5.4 %collective-permute-done.10.block = bf16[64,5376]{1,0:T(8,128)(2,1)S(1)} collective-permute-done((bf16[64,5376]{1,0:T(8,128)(2,1)S(1)}, bf16[64,5376]{1,0:T(8,128)(2,1)S(1)}, u32[]{:S(2)}, u32[]{:S(2)}) %collective-permute-start.10) | collective-permute-done | bytes 688160 | tf_op jit(solution)/shard_map/ppermute | solution.py:493
  95.1 0.5 slice_bitcast_fusion
  95.6 8.0 %shard_map.86 = bf16[1024,5376]{1,0:T(8,128)(2,1)} custom-call(bf16[1024,512]{1,0:T(8,128)(2,1)S(1)} %get-tuple-element.64.grad, bf16[256,5376]{1,0:T(8,128)(2,1)S(1)} %get-tuple-element.65.near, bf16[256,5376]{1,0:T(8,128)(2,1)S(1)} %get-tuple-element.66.far), custom_call_target="tpu_custom_call" | custom-call | flops 5637144576 | bytes 16515072 | tf_op jit(solution)/shard_map/pallas_call | solution.py:399
  103.8 5.6 %collective-permute-done.11.arrived = bf16[64,5376]{1,0:T(8,128)(2,1)S(1)} collective-permute-done((bf16[64,5376]{1,0:T(8,128)(2,1)S(1)}, bf16[64,5376]{1,0:T(8,128)(2,1)S(1)}, u32[]{:S(2)}, u32[]{:S(2)}) %collective-permute-start.11) | collective-permute-done | bytes 688160 | tf_op jit(solution)/shard_map/ppermute | solution.py:493
  109.4 0.3 shard_map.88
  109.7 15.4 %all_to_all.34.parts = bf16[16,64,336]{2,1,0:T(8,128)(2,1)S(1)} all-to-all(bf16[16,64,336]{2,1,0:T(8,128)(2,1)S(1)} %shard_map.88), channel_id=1, replica_groups=mesh['seq'=8,'vocab'=16] {'vocab'}, dimensions={0} | all-to-all | bytes 1376256 | tf_op jit(solution)/shard_map/all_to_all | solution.py:545
  125.2 0.7 shard_map.89
  (27 shorter events, 1.7 us)
Async XLA Ops:
  0.7 0.8 copy-start
  1.6 25.7 %copy-start.1 = (f32[4,256]{1,0:T(4,128)S(1)}, f32[4,256]{1,0:T(4,128)}, u32[]{:S(2)}) copy-start(f32[4,256]{1,0:T(4,128)} %logits_ref) | copy-start | bytes 12292
  1.6 25.7 %copy-start.2 = (s32[4,256]{1,0:T(4,128)S(1)}, s32[4,256]{1,0:T(4,128)}, u32[]{:S(2)}) copy-start(s32[4,256]{1,0:T(4,128)} %ids_ref.1) | copy-start | bytes 12292
  23.2 2.2 %collective-permute-start = (bf16[64,5376]{1,0:T(8,128)(2,1)S(1)}, bf16[64,5376]{1,0:T(8,128)(2,1)S(1)}, u32[]{:S(2)}, u32[]{:S(2)}) collective-permute-start(bf16[64,5376]{1,0:T(8,128)(2,1)S(1)} %shard_map.76.own), channel_id=1, source_target_pairs={{0,16},{16,0},{32,48},{48,32},{64,80},{80,64},{96,112},{112,96},{1... | collective-permute-start | bytes 2064392 | tf_op jit(solution)/shard_map/ppermute | solution.py:493
  23.3 13.0 %collective-permute-start.1 = (bf16[64,5376]{1,0:T(8,128)(2,1)S(1)}, bf16[64,5376]{1,0:T(8,128)(2,1)S(1)}, u32[]{:S(2)}, u32[]{:S(2)}) collective-permute-start(bf16[64,5376]{1,0:T(8,128)(2,1)S(1)} %shard_map.76.own), channel_id=1, source_target_pairs={{0,32},{16,112},{32,64},{48,16},{64,96},{80,48},{96,0},{112,80},{1... | collective-permute-start | bytes 2064392 | tf_op jit(solution)/shard_map/ppermute | solution.py:493
  25.4 20.4 %collective-permute-start.2 = (bf16[64,5376]{1,0:T(8,128)(2,1)S(1)}, bf16[64,5376]{1,0:T(8,128)(2,1)}, u32[]{:S(2)}, u32[]{:S(2)}) collective-permute-start(bf16[64,5376]{1,0:T(8,128)(2,1)S(1)} %collective-permute-done.own2), channel_id=1, source_target_pairs={{0,32},{16,112},{32,64},{48,16},{64,96},{80,48},{96,0},{112,80},{1... | collective-permute-start | bytes 2064392 | tf_op jit(solution)/shard_map/ppermute | solution.py:493
  28.9 16.9 %all-to-all-start.1 = ((f32[128,1,64]{2,1,0:T(1,128)}), f32[128,1,64]{2,1,0:T(1,128)S(1)}, u32[]{:S(2)}, u32[]{:S(2)}) async-start(f32[128,1,64]{2,1,0:T(1,128)} %bitcast.3), calls=%async_computation.1 | async-start | bytes 131072 | tf_op jit(solution)/shard_map/all_to_all | solution.py:510
  36.3 19.4 %collective-permute-start.4 = (bf16[64,5376]{1,0:T(8,128)(2,1)S(1)}, bf16[64,5376]{1,0:T(8,128)(2,1)S(1)}, u32[]{:S(2)}, u32[]{:S(2)}) collective-permute-start(bf16[64,5376]{1,0:T(8,128)(2,1)S(1)} %collective-permute-done.1.next1), channel_id=1, source_target_pairs={{0,16},{16,0},{32,48},{48,32},{64,80},{80,64},{96,112},{112,96},{1... | collective-permute-start | bytes 2064392 | tf_op jit(solution)/shard_map/ppermute | solution.py:493
  36.3 17.6 %collective-permute-start.5 = (bf16[64,5376]{1,0:T(8,128)(2,1)S(1)}, bf16[64,5376]{1,0:T(8,128)(2,1)S(1)}, u32[]{:S(2)}, u32[]{:S(2)}) collective-permute-start(bf16[64,5376]{1,0:T(8,128)(2,1)S(1)} %collective-permute-done.1.next1), channel_id=1, source_target_pairs={{0,32},{16,112},{32,64},{48,16},{64,96},{80,48},{96,0},{112,80},{1... | collective-permute-start | bytes 2064392 | tf_op jit(solution)/shard_map/ppermute | solution.py:493
  45.8 8.7 %collective-permute-start.3 = (bf16[64,5376]{1,0:T(8,128)(2,1)}, bf16[64,5376]{1,0:T(8,128)(2,1)S(1)}, u32[]{:S(2)}, u32[]{:S(2)}) collective-permute-start(bf16[64,5376]{1,0:T(8,128)(2,1)} %collective-permute-done.2.next2), channel_id=1, source_target_pairs={{0,16},{16,0},{32,48},{48,32},{64,80},{80,64},{96,112},{112,96},{1... | collective-permute-start | bytes 2064392 | tf_op jit(solution)/shard_map/ppermute | solution.py:493
  53.9 2.4 %collective-permute-start.6 = (bf16[64,5376]{1,0:T(8,128)(2,1)S(1)}, bf16[64,5376]{1,0:T(8,128)(2,1)S(1)}, u32[]{:S(2)}, u32[]{:S(2)}) collective-permute-start(bf16[64,5376]{1,0:T(8,128)(2,1)S(1)} %collective-permute-done.5.far), channel_id=1, source_target_pairs={{0,16},{16,0},{32,48},{48,32},{64,80},{80,64},{96,112},{112,96},{1... | collective-permute-start | bytes 2064392 | tf_op jit(solution)/shard_map/ppermute | solution.py:493
  79.0 3.3 %collective-permute-start.7 = (bf16[64,5376]{1,0:T(8,128)(2,1)S(1)}, bf16[64,5376]{1,0:T(8,128)(2,1)S(1)}, u32[]{:S(2)}, u32[]{:S(2)}) collective-permute-start(bf16[64,5376]{1,0:T(8,128)(2,1)S(1)} %get-tuple-element.54), channel_id=1, source_target_pairs={{0,16},{16,0},{32,48},{48,32},{64,80},{80,64},{96,112},{112,96},{1... | collective-permute-start | bytes 2064392 | tf_op jit(solution)/shard_map/ppermute | solution.py:493
  81.7 2.3 %collective-permute-start.8 = (bf16[64,5376]{1,0:T(8,128)(2,1)S(1)}, bf16[64,5376]{1,0:T(8,128)(2,1)S(1)}, u32[]{:S(2)}, u32[]{:S(2)}) collective-permute-start(bf16[64,5376]{1,0:T(8,128)(2,1)S(1)} %get-tuple-element.57), channel_id=1, source_target_pairs={{0,16},{16,0},{32,48},{48,32},{64,80},{80,64},{96,112},{112,96},{1... | collective-permute-start | bytes 2064392 | tf_op jit(solution)/shard_map/ppermute | solution.py:493
  82.4 12.2 %collective-permute-start.10 = (bf16[64,5376]{1,0:T(8,128)(2,1)S(1)}, bf16[64,5376]{1,0:T(8,128)(2,1)S(1)}, u32[]{:S(2)}, u32[]{:S(2)}) collective-permute-start(bf16[64,5376]{1,0:T(8,128)(2,1)S(1)} %add_convert_fusion.2), channel_id=1, source_target_pairs={{0,32},{16,112},{32,64},{48,16},{64,96},{80,48},{96,0},{112,80},{1... | collective-permute-start | bytes 2064392 | tf_op jit(solution)/shard_map/ppermute | solution.py:493
  84.2 19.3 %collective-permute-start.12 = (bf16[64,5376]{1,0:T(8,128)(2,1)S(1)}, bf16[64,5376]{1,0:T(8,128)(2,1)S(1)}, u32[]{:S(2)}, u32[]{:S(2)}) collective-permute-start(bf16[64,5376]{1,0:T(8,128)(2,1)S(1)} %add_convert_fusion.1), channel_id=1, source_target_pairs={{0,48},{16,96},{32,80},{48,0},{64,112},{80,32},{96,16},{112,64},{1... | collective-permute-start | bytes 2064392 | tf_op jit(solution)/shard_map/ppermute | solution.py:493
  88.2 6.6 %collective-permute-start.9 = (bf16[128,5376]{1,0:T(8,128)(2,1)S(1)}, bf16[128,5376]{1,0:T(8,128)(2,1)S(1)}, u32[]{:S(2)}, u32[]{:S(2)}) collective-permute-start(bf16[128,5376]{1,0:T(8,128)(2,1)S(1)} %get-tuple-element.60), channel_id=1, source_target_pairs={{0,16},{16,0},{32,48},{48,32},{64,80},{80,64},{96,112},{112,96},{1... | collective-permute-start | bytes 4128776 | tf_op jit(solution)/shard_map/ppermute | solution.py:493
  95.0 14.4 %collective-permute-start.11 = (bf16[64,5376]{1,0:T(8,128)(2,1)S(1)}, bf16[64,5376]{1,0:T(8,128)(2,1)S(1)}, u32[]{:S(2)}, u32[]{:S(2)}) collective-permute-start(bf16[64,5376]{1,0:T(8,128)(2,1)S(1)} %add_convert_fusion), channel_id=1, source_target_pairs={{0,32},{16,112},{32,64},{48,16},{64,96},{80,48},{96,0},{112,80},{1... | collective-permute-start | bytes 2064392 | tf_op jit(solution)/shard_map/ppermute | solution.py:493
